TPU v7x, 128 devices: a whole 4x4x4 slice. The times are simulated.
128 devices in a mesh: row: 8 (over x, core), col: 16 (over y, z).
Axes of the slice: x: 4, y: 4, z: 4, core: 2. Of those that a mesh axis runs over, the one named last changes fastest.
Arguments:
- masters: float32 [256, 4096], P('col'), may hold values from -6 to 6
- inst_master: int32 [128, 256], P('row', 'col'), may hold values from 0 to 255
- inst_orient: int32 [128, 256], P('row', 'col'), may hold values from 0 to 3
- owner_map: int32 [256], replicated, may hold values from 0 to 255, each once
- tile_free: float32 [8192, 16384], P('row', 'col'), may hold values from -3 to 3
- target: float32 [8192, 16384], P('row', 'col'), may hold values from 0 to 1
- kernel_spectra: float32 [2, 128, 8, 128], replicated, may hold values from -6 to 6
- socs_weights: float32 [8], replicated, may hold values from 0.05 to 1
Outputs:
- resist: float32 [8192, 16384], P('row', 'col')
- new_mask: float32 [8192, 16384], P('row', 'col')
- masters_out: float32 [256, 4096], P('col')
Inputs may be any that keep to these rules, and one draw needn't show every extreme that they name: `inst_orient`: bit 0 reverses a cell's rows, bit 1 its columns. `owner_map`: each storage row is used by exactly one master; storage row r lies on index r // 16 of col.
All inputs are finite; a program needn't handle non-finite values.
Results may differ from a plain program's by a relative error of at most 0.0092.
Values may be sent and summed in bfloat16 or wider, within the bound.
No kernel may reach another device: no remote copies, remote signals or barrier semaphores. Data moves between devices by JAX's collectives and lax.ppermute only.
A program may use at most 128 MiB of HBM per device.

v0:
```python
import math

import jax
import jax.numpy as jnp
from jax import lax
from jax.sharding import Mesh
from jax.sharding import PartitionSpec as P

TILE = 512
TPD = 2
HALO = 64
CELL = 64
COL = ("col_0", "col_1")


step_free = 1.0
step_master = 0.05
resist_gain = 2.0
resist_level = 1.8


def padded_2(value, sides, width):
    for axis, dim in sides:
        peers, length = (lax.axis_size(axis), value.shape[dim])
        up = [(i, (i + 1) % peers) for i in range(peers - 1)]
        down = [(j, i) for i, j in up]
        last = lax.slice_in_dim(value, length - width, length, axis=dim)
        initial = lax.slice_in_dim(value, 0, width, axis=dim)
        before = lax.ppermute(last, axis, up)
        after = lax.ppermute(initial, axis, down)
        value = jnp.concatenate([before, value, after], axis=dim)
    return value


def cut_along(value, dim, peers):
    before, after = (value.shape[:dim], value.shape[dim + 1 :])
    return jnp.moveaxis(value.reshape(*before, peers, -1, *after), dim, 0)


def sent_and_summed(value, axis, dim):
    peers = lax.axis_size(axis)
    blocks = lax.all_to_all(cut_along(value, dim, peers), axis, 0, 0, tiled=True)
    return jnp.sum(blocks.astype(jnp.float32), axis=0)


def copy_for_each(value, axis):
    peers = lax.axis_size(axis)
    return lax.all_to_all(
        jnp.broadcast_to(value[None], (peers, *value.shape)), axis, 0, 0, tiled=True
    )


def of_everyone(value, axis):
    return copy_for_each(value, axis).astype(jnp.float32).sum(axis=0)


def gather_axes(value, axes, dim):
    result = value
    for number in range(len(axes) - 1, -1, -1):
        result = lax.all_gather(result, axes[number], axis=dim, tiled=True)
    return result


def dot_plain(left, right):
    return jnp.dot(left, right, preferred_element_type=jnp.float32)


def dot_right_t(left, right):
    return lax.dot_general(
        left, right, (((1,), (1,)), ((), ())), preferred_element_type=jnp.float32
    )


def dot_left_t(left, right):
    return lax.dot_general(
        left, right, (((0,), (0,)), ((), ())), preferred_element_type=jnp.float32
    )


def tables(pad_side, band_side):
    freqs = jnp.arange(band_side, dtype=jnp.int32) - band_side // 2
    pixels = jnp.arange(pad_side, dtype=jnp.int32)
    phases = freqs[:, None] * pixels[None, :] % pad_side
    angles = phases.astype(jnp.float32) * (2.0 * math.pi / pad_side)
    return (jnp.cos(angles).astype(jnp.bfloat16), jnp.sin(angles).astype(jnp.bfloat16))


def tile_step(padded, target, spectra, weights, halo_side):
    pad_side = padded.shape[0]
    band_side = spectra.shape[1]
    kernels = spectra.shape[2]
    tile_side = pad_side - 2 * halo_side
    cos_full, sin_full = tables(pad_side, band_side)
    cos_in = cos_full[:, halo_side : halo_side + tile_side]
    sin_in = sin_full[:, halo_side : halo_side + tile_side]
    forw_re = dot_plain(cos_full, padded).astype(jnp.bfloat16)
    forw_im = (-dot_plain(sin_full, padded)).astype(jnp.bfloat16)
    spec_re = (dot_right_t(forw_re, cos_full) - dot_right_t(forw_im, sin_full)) / pad_side
    spec_im = (-dot_right_t(forw_re, sin_full) - dot_right_t(forw_im, cos_full)) / pad_side
    kern_re = spectra[0]
    kern_im = spectra[1]
    amp_re = (kern_re * spec_re[:, None, :] - kern_im * spec_im[:, None, :]).astype(jnp.bfloat16)
    amp_im = (kern_re * spec_im[:, None, :] + kern_im * spec_re[:, None, :]).astype(jnp.bfloat16)
    amp_re = amp_re.reshape(band_side, kernels * band_side)
    amp_im = amp_im.reshape(band_side, kernels * band_side)
    half_re = (dot_left_t(cos_in, amp_re) - dot_left_t(sin_in, amp_im)).astype(jnp.bfloat16)
    half_im = (dot_left_t(cos_in, amp_im) + dot_left_t(sin_in, amp_re)).astype(jnp.bfloat16)
    half_re = half_re.reshape(tile_side * kernels, band_side)
    half_im = half_im.reshape(tile_side * kernels, band_side)
    field_re = (dot_plain(half_re, cos_in) - dot_plain(half_im, sin_in)) / band_side
    field_im = (dot_plain(half_re, sin_in) + dot_plain(half_im, cos_in)) / band_side
    field_re = field_re.reshape(tile_side, kernels, tile_side)
    field_im = field_im.reshape(tile_side, kernels, tile_side)
    scaled = weights[None, :, None]
    intensity = jnp.sum(scaled * (field_re * field_re + field_im * field_im), axis=1)
    resist = jax.nn.sigmoid(resist_gain * (intensity - resist_level))
    slopes = 2.0 * (resist - target) * resist_gain * resist * (1.0 - resist)
    back_re = (2.0 / band_side * scaled * slopes[:, None, :] * field_re).astype(jnp.bfloat16)
    back_im = (2.0 / band_side * scaled * slopes[:, None, :] * field_im).astype(jnp.bfloat16)
    back_re = back_re.reshape(tile_side * kernels, tile_side)
    back_im = back_im.reshape(tile_side * kernels, tile_side)
    bhalf_re = (dot_right_t(back_re, cos_in) + dot_right_t(back_im, sin_in)).astype(jnp.bfloat16)
    bhalf_im = (dot_right_t(back_im, cos_in) - dot_right_t(back_re, sin_in)).astype(jnp.bfloat16)
    bhalf_re = bhalf_re.reshape(tile_side, kernels * band_side)
    bhalf_im = bhalf_im.reshape(tile_side, kernels * band_side)
    bamp_re = (dot_plain(cos_in, bhalf_re) + dot_plain(sin_in, bhalf_im)).reshape(
        band_side, kernels, band_side
    )
    bamp_im = (dot_plain(cos_in, bhalf_im) - dot_plain(sin_in, bhalf_re)).reshape(
        band_side, kernels, band_side
    )
    bspec_re = (jnp.sum(kern_re * bamp_re + kern_im * bamp_im, axis=1) / pad_side).astype(
        jnp.bfloat16
    )
    bspec_im = (jnp.sum(kern_re * bamp_im - kern_im * bamp_re, axis=1) / pad_side).astype(
        jnp.bfloat16
    )
    bforw_re = (dot_plain(bspec_re, cos_in) - dot_plain(bspec_im, sin_in)).astype(jnp.bfloat16)
    bforw_im = (-dot_plain(bspec_re, sin_in) - dot_plain(bspec_im, cos_in)).astype(jnp.bfloat16)
    gradient = dot_left_t(cos_in, bforw_re) - dot_left_t(sin_in, bforw_im)
    return (resist, gradient)


def orient_cells(cells, orient):
    flip_first = orient % 2 == 1
    flip_second = orient // 2 == 1
    cells = jnp.where(flip_first[..., None, None], cells[..., ::-1, :], cells)
    cells = jnp.where(flip_second[..., None, None], cells[..., :, ::-1], cells)
    return cells


def assemble(master_rows, slots, orient, cell_side):
    grid_rows, grid_cols = slots.shape
    cells = jnp.take(master_rows, slots.reshape(-1), axis=0)
    cells = cells.reshape(grid_rows, grid_cols, cell_side, cell_side)
    cells = orient_cells(cells, orient)
    return cells.transpose(0, 2, 1, 3).reshape(grid_rows * cell_side, grid_cols * cell_side)


def cells_of(image, orient, cell_side):
    grid_rows, grid_cols = orient.shape
    cells = image.reshape(grid_rows, cell_side, grid_cols, cell_side).transpose(0, 2, 1, 3)
    cells = orient_cells(cells, orient)
    return cells.reshape(grid_rows * grid_cols, cell_side * cell_side)


def smooth(master_rows, cell_side):
    grids = master_rows.reshape(-1, cell_side, cell_side)
    framed = jnp.pad(grids, ((0, 0), (1, 1), (1, 1)))
    beside_all = (
        framed[:, 2:, 1:-1] + framed[:, :-2, 1:-1] + framed[:, 1:-1, 2:] + framed[:, 1:-1, :-2]
    )
    return (0.5 * grids + 0.125 * beside_all).reshape(master_rows.shape)


def stitch_local(tiles):
    return tiles.reshape(TPD, TPD, TILE, TILE).transpose(0, 2, 1, 3).reshape(TPD * TILE, TPD * TILE)


def per_device(
    masters, inst_master, inst_orient, owner_map, tile_free, target, kernel_spectra, socs_weights
):
    stored = masters.shape[0]
    everything = lax.all_gather(masters, COL, axis=0, tiled=True)
    total_masters = everything.shape[0]
    matches = inst_master[..., None] == jnp.arange(total_masters, dtype=jnp.int32)
    slots = jnp.sum(jnp.where(matches, owner_map, 0), axis=-1)
    flat_slots = slots.reshape(-1)
    col_index = lax.axis_index(COL)
    free_field = tile_free
    pad_side = TILE + 2 * HALO
    shading = jnp.tanh(assemble(everything, slots, inst_orient, CELL) + free_field)
    mask_block = shading.astype(jnp.bfloat16)
    padded = padded_2(mask_block, (("row", 0), (COL, 1)), HALO)

    def one_tile(tile_index):
        row_at = tile_index // TPD
        col_at = tile_index % TPD
        window = lax.dynamic_slice(padded, (row_at * TILE, col_at * TILE), (pad_side, pad_side))
        goal_tile = lax.dynamic_slice(target, (row_at * TILE, col_at * TILE), (TILE, TILE))
        return tile_step(window, goal_tile, kernel_spectra, socs_weights, HALO)

    resist_tiles, grad_tiles = lax.map(one_tile, jnp.arange(TPD * TPD, dtype=jnp.int32))
    resist = stitch_local(resist_tiles)
    grad_param = stitch_local(grad_tiles) * (1.0 - shading * shading)
    free_field = free_field - step_free * grad_param
    cell_grads = cells_of(grad_param, inst_orient, CELL)
    wanted = jnp.arange(stored * lax.axis_size(COL), dtype=jnp.int32)
    selector = (flat_slots[None, :] == wanted[:, None]).astype(jnp.float32)
    summed = sent_and_summed(
        jnp.dot(
            selector,
            cell_grads,
            precision=lax.Precision.HIGHEST,
            preferred_element_type=jnp.float32,
        ).astype(jnp.bfloat16),
        COL,
        0,
    )
    summed = of_everyone(summed.astype(jnp.bfloat16), "row").astype(jnp.float32)
    own_rows = lax.dynamic_slice_in_dim(everything, col_index * stored, stored, 0)
    fresh = smooth(own_rows - step_master * summed, CELL)
    everything = gather_axes(fresh.astype(jnp.bfloat16), COL, 0).astype(fresh.dtype)
    new_mask = jnp.tanh(assemble(everything, slots, inst_orient, CELL) + free_field)
    masters_out = lax.dynamic_slice_in_dim(everything, col_index * stored, stored, 0)
    return (resist, new_mask, masters_out)


def solution(mesh):
    split = Mesh(mesh.devices.reshape(mesh.shape["row"], 4, 4), ("row", "col_0", "col_1"))
    placed = (
        P(COL, None),
        P("row", COL),
        P("row", COL),
        P(),
        P("row", COL),
        P("row", COL),
        P(),
        P(),
    )
    return jax.shard_map(
        per_device,
        mesh=split,
        in_specs=placed,
        out_specs=(P("row", COL), P("row", COL), P(COL, None)),
        check_vma=False,
    )
```

profile of v0, /device:TPU:1, one launch (start us, length us, event | category | flops | bytes accessed | tf_op | source)
XLA Modules:
  0.0 757.6 jit_solution(13970604052735442558)
XLA Ops:
  9.9 55.1 %all-gather.3.cloned.1.call-done = f32[256,4096]{1,0:T(8,128)} async-done(((f32[16,4096]{1,0:T(8,128)}), f32[256,4096]{1,0:T(8,128)}) %all-gather.3.cloned.1.call-update) | async-done | bytes 4194320 | tf_op jit(solution)/shard_map/all_gather | solution.py:184
  65.0 7.9 %gather_fusion = f32[256,4096]{1,0:T(8,128)} fusion(f32[256,4096]{1,0:T(8,128)} %all-gather.3.cloned.1.call-done, s32[1024]{0:T(1024)S(1)} %pad_clamp_fusion), kind=kCustom, calls=%fused_computation.clone | custom fusion | bytes 8389632 | tf_op jit(solution)/shard_map/jit(_take)/gather | solution.py:154
  77.7 8.1 %reshape.205 = f32[16,16,64,64]{3,2,1,0:T(8,128)} reshape(f32[256,4096]{1,0:T(8,128)} %broadcast_select_fusion.5) | data formatting | bytes 8388608 | tf_op jit(solution)/shard_map/reshape | solution.py:155
  85.8 11.9 %rev.18 = f32[16,16,64,64]{3,2,1,0:T(8,128)} reverse(f32[16,16,64,64]{3,2,1,0:T(8,128)} %reshape.205), dimensions={2} | reverse | bytes 8388608 | tf_op jit(solution)/shard_map/rev | solution.py:147
  97.7 9.8 %broadcast_select_fusion.2 = f32[16,16,64,64]{3,2,1,0:T(8,128)} fusion(f32[16,16,64,64]{3,2,1,0:T(8,128)} %rev.18, f32[16,16,64,64]{3,2,1,0:T(8,128)} %reshape.205, pred[16,16]{1,0:T(8,128)(4,1)S(1)} %get-tuple-element.182), kind=kLoop, calls=%fused_computation.136 | loop fusion | flops 1048576 | bytes 12583168 | tf_op jit(solution)/shard_map/jit(_where)/select_n | solution.py:147
  107.5 13.2 %rev.19 = f32[16,16,64,64]{3,2,1,0:T(8,128)} reverse(f32[16,16,64,64]{3,2,1,0:T(8,128)} %broadcast_select_fusion.2), dimensions={3} | reverse | bytes 8388608 | tf_op jit(solution)/shard_map/rev | solution.py:148
  127.1 9.8 %copy.21 = f32[16,64,16,64]{3,2,1,0:T(8,128)} copy(f32[16,64,16,64]{3,1,2,0:T(8,128)S(1)} %select_bitcast_fusion.1) | data formatting | bytes 8388608 | tf_op jit(solution)/shard_map/transpose | solution.py:157
  173.8 294.9 %while.15 = (s32[]{:T(128)}, f32[4,512,512]{2,1,0:T(8,128)}, f32[4,512,512]{2,1,0:T(8,128)}, f32[8]{0:T(128)S(1)}, f32[2,128,8,128]{3,2,1,0:T(8,128)}, /*index=5...) while((s32[]{:T(128)}, f32[4,512,512]{2,1,0:T(8,128)}, ...), condition=%wide.region_5.7_spmd, body=%wide.region_1.6_spmd.sunk | while | flops 5924732928 | bytes 199283888 | solution.py:203
  488.3 9.2 %copy.45 = f32[16,64,16,64]{3,1,2,0:T(8,128)} copy(f32[16,64,16,64]{3,2,1,0:T(8,128)} %reshape.211) | data formatting | bytes 8388608 | tf_op jit(solution)/shard_map/reshape | solution.py:162
  497.5 11.9 %rev.20 = f32[16,16,64,64]{3,2,1,0:T(8,128)} reverse(f32[16,16,64,64]{3,2,1,0:T(8,128)} %bitcast.206), dimensions={2} | reverse | bytes 8388608 | tf_op jit(solution)/shard_map/rev | solution.py:147
  509.5 10.9 %broadcast_select_fusion.1 = f32[16,16,64,64]{3,2,1,0:T(8,128)} fusion(f32[16,16,64,64]{3,2,1,0:T(8,128)} %rev.20, pred[16,16]{1,0:T(8,128)(4,1)S(1)} %copy-done.6, f32[16,64,16,64]{3,2,1,0:T(8,128)} %reshape.211), kind=kLoop, calls=%fused_computation.135 | loop fusion | flops 1048576 | bytes 12583168 | tf_op jit(solution)/shard_map/jit(_where)/select_n | solution.py:147
  520.4 13.2 %rev.21 = f32[16,16,64,64]{3,2,1,0:T(8,128)} reverse(f32[16,16,64,64]{3,2,1,0:T(8,128)} %broadcast_select_fusion.1), dimensions={3} | reverse | bytes 8388608 | tf_op jit(solution)/shard_map/rev | solution.py:148
  533.6 9.8 %broadcast_select_fusion.3 = f32[16,16,64,64]{3,2,1,0:T(8,128)} fusion(f32[16,16,64,64]{3,2,1,0:T(8,128)} %rev.21, f32[16,16,64,64]{3,2,1,0:T(8,128)} %broadcast_select_fusion.1, pred[16,16]{1,0:T(8,128)(4,1)S(1)} %copy-done.4), kind=kLoop, calls=%fused_computation.137 | loop fusion | flops 1048576 | bytes 12583168 | tf_op jit(solution)/shard_map/jit(_where)/select_n | solution.py:148
  555.8 35.0 %all_to_all.10 = bf16[16,16,4096]{2,1,0:T(8,128)(2,1)S(1)} all-to-all(bf16[16,16,4096]{2,1,0:T(8,128)(2,1)S(1)} %bitcast.210), channel_id=1, replica_groups=mesh['row'=8,'col_0'=4,'col_1'=4] {'col_0','col_1'}, dimensions={0} | all-to-all | bytes 4194304 | tf_op jit(solution)/shard_map/all_to_all | solution.py:42
  597.9 15.1 %all-to-all-done.1 = bf16[8,16,4096]{2,1,0:T(8,128)(2,1)S(1)} async-done(((bf16[8,16,4096]{2,1,0:T(8,128)(2,1)}), bf16[8,16,4096]{2,1,0:T(8,128)(2,1)S(1)}, u32[]{:S(2)}, u32[]{:S(2)}) %all-to-all-start.1) | async-done | bytes 1048608 | tf_op jit(solution)/shard_map/all_to_all | solution.py:48
  615.0 10.8 %all_gather.10 = bf16[64,4096]{1,0:T(8,128)(2,1)} all-gather(bf16[16,4096]{1,0:T(8,128)(2,1)S(1)} %convert_element_type.256), channel_id=1, replica_groups=mesh['row'=8,'col_0'=4,'col_1'=4] {'col_1'}, dimensions={0}, use_global_device_ids=true | all-gather | bytes 655360 | tf_op jit(solution)/shard_map/all_gather | solution.py:60
  634.3 22.2 %all-gather.5.cloned.1.call-done = bf16[256,4096]{1,0:T(8,128)(2,1)} async-done(((bf16[64,4096]{1,0:T(8,128)(2,1)}), bf16[256,4096]{1,0:T(8,128)(2,1)}) %all-gather.5.cloned.1.call-update) | async-done | bytes 2097168 | tf_op jit(solution)/shard_map/all_gather | solution.py:60
  660.7 8.0 %gather_fusion.1 = f32[256,4096]{1,0:T(8,128)} fusion(f32[256,4096]{1,0:T(8,128)} %convert_element_type.257, s32[1024]{0:T(1024)} %copy-done.8), kind=kCustom, calls=%fused_computation.1.clone | custom fusion | bytes 8389632 | tf_op jit(solution)/shard_map/jit(_take)/gather | solution.py:154
  675.1 8.1 %reshape.215 = f32[16,16,64,64]{3,2,1,0:T(8,128)} reshape(f32[256,4096]{1,0:T(8,128)} %broadcast_select_fusion.4) | data formatting | bytes 8388608 | tf_op jit(solution)/shard_map/reshape | solution.py:155
  683.2 11.9 %rev.22 = f32[16,16,64,64]{3,2,1,0:T(8,128)} reverse(f32[16,16,64,64]{3,2,1,0:T(8,128)} %reshape.215), dimensions={2} | reverse | bytes 8388608 | tf_op jit(solution)/shard_map/rev | solution.py:147
  695.2 9.8 %broadcast_select_fusion = f32[16,16,64,64]{3,2,1,0:T(8,128)} fusion(f32[16,16,64,64]{3,2,1,0:T(8,128)} %rev.22, f32[16,16,64,64]{3,2,1,0:T(8,128)} %reshape.215, pred[16,16]{1,0:T(8,128)(4,1)S(1)} %copy-done.6), kind=kLoop, calls=%fused_computation.134 | loop fusion | flops 1048576 | bytes 12583168 | tf_op jit(solution)/shard_map/jit(_where)/select_n | solution.py:147
  704.9 13.2 %rev.23 = f32[16,16,64,64]{3,2,1,0:T(8,128)} reverse(f32[16,16,64,64]{3,2,1,0:T(8,128)} %broadcast_select_fusion), dimensions={3} | reverse | bytes 8388608 | tf_op jit(solution)/shard_map/rev | solution.py:148
  724.5 9.8 %copy.25 = f32[16,64,16,64]{3,2,1,0:T(8,128)} copy(f32[16,64,16,64]{3,1,2,0:T(8,128)S(1)} %select_bitcast_fusion) | data formatting | bytes 8388608 | tf_op jit(solution)/shard_map/transpose | solution.py:157
  741.8 8.6 %add_tanh_fusion = f32[1024,1024]{1,0:T(8,128)} fusion(f32[1024,1024]{1,0:T(8,128)} %reshape.216, f32[1024,1024]{1,0:T(8,128)} %param.16, f32[1024,1024]{1,0:T(8,128)} %subtract_multiply_fusion.2), kind=kLoop, calls=%fused_computation.131 | loop fusion | flops 2097152 | bytes 16777216 | tf_op jit(solution)/shard_map/tanh | solution.py:224
  (262 shorter events, 392.3 us)
Async XLA Ops:
  7.2 57.9 %all-gather.3.cloned.1.call-start = ((), (), s32[]{:S(2)}) async-start(), calls=%async_computation.2 | async-start | bytes 4456448 | tf_op jit(solution)/shard_map/all_gather | solution.py:184
  9.1 63.8 %copy-start.9 = (s32[256]{0:T(256)}, s32[256]{0:T(256)S(1)}, u32[]{:S(2)}) copy-start(s32[256]{0:T(256)S(1)} %reshape.204) | copy-start | bytes 3076
  9.1 63.8 %copy-start.8 = (s32[1024]{0:T(1024)}, s32[1024]{0:T(1024)S(1)}, u32[]{:S(2)}) copy-start(s32[1024]{0:T(1024)S(1)} %pad_clamp_fusion) | copy-start | bytes 12292
  9.2 63.8 %copy-start.11 = (pred[256]{0:T(512)(128)(4,1)}, pred[256]{0:T(512)(128)(4,1)S(1)}, u32[]{:S(2)}) copy-start(pred[256]{0:T(512)(128)(4,1)S(1)} %compare_and_fusion) | copy-start | bytes 772
  9.9 87.8 %copy-start.5 = (pred[16,16]{1,0:T(8,128)(4,1)}, pred[16,16]{1,0:T(8,128)(4,1)S(1)}, u32[]{:S(2)}) copy-start(pred[16,16]{1,0:T(8,128)(4,1)S(1)} %get-tuple-element.182) | copy-start | bytes 772
  9.9 110.8 %copy-start.3 = (pred[16,16]{1,0:T(8,128)(4,1)}, pred[16,16]{1,0:T(8,128)(4,1)S(1)}, u32[]{:S(2)}) copy-start(pred[16,16]{1,0:T(8,128)(4,1)S(1)} %get-tuple-element.181) | copy-start | bytes 772
  149.0 6.3 collective-permute-start.1
  151.6 4.9 collective-permute-start
  156.8 17.0 %copy-start.7 = (f32[8]{0:T(128)S(1)}, f32[8]{0:T(128)}, u32[]{:S(2)}) copy-start(f32[8]{0:T(128)} %param.19) | copy-start | bytes 100
  157.0 8.7 %collective-permute-start.2 = (bf16[1152,64]{1,0:T(8,128)(2,1)S(1)}, bf16[1152,64]{1,0:T(8,128)(2,1)S(1)}, u32[]{:S(2)}, u32[]{:S(2)}) collective-permute-start(bf16[1152,64]{1,0:T(8,128)(2,1)S(1)} %get-tuple-element.178), channel_id=1, source_target_pairs={{0,1},{1,2},{2,3},{3,4},{4,5},{5,6},{6,7},{7,8},{8,9},{9,10},{10,1... | collective-permute-start | bytes 442376 | tf_op jit(solution)/shard_map/ppermute | solution.py:29
  160.0 9.8 %collective-permute-start.3 = (bf16[1152,64]{1,0:T(8,128)(2,1)S(1)}, bf16[1152,64]{1,0:T(8,128)(2,1)S(1)}, u32[]{:S(2)}, u32[]{:S(2)}) collective-permute-start(bf16[1152,64]{1,0:T(8,128)(2,1)S(1)} %get-tuple-element.177), channel_id=1, source_target_pairs={{1,0},{2,1},{3,2},{4,3},{5,4},{6,5},{7,6},{8,7},{9,8},{10,9},{11,1... | collective-permute-start | bytes 442376 | tf_op jit(solution)/shard_map/ppermute | solution.py:30
  220.5 3.2 copy-start
  289.9 3.2 copy-start
  359.3 3.2 copy-start
  428.7 3.2 copy-start
  474.1 2.2 copy-start.1
  474.1 3.5 copy-start.2
  497.5 11.9 %copy-start.6 = (pred[16,16]{1,0:T(8,128)(4,1)S(1)}, pred[16,16]{1,0:T(8,128)(4,1)}, u32[]{:S(2)}) copy-start(pred[16,16]{1,0:T(8,128)(4,1)} %copy-done.5) | copy-start | bytes 772
  520.4 13.2 %copy-start.4 = (pred[16,16]{1,0:T(8,128)(4,1)S(1)}, pred[16,16]{1,0:T(8,128)(4,1)}, u32[]{:S(2)}) copy-start(pred[16,16]{1,0:T(8,128)(4,1)} %copy-done.3) | copy-start | bytes 772
  543.4 7.9 %copy-start.10 = (s32[256]{0:T(256)S(1)}, s32[256]{0:T(256)}, u32[]{:S(2)}) copy-start(s32[256]{0:T(256)} %copy-done.9) | copy-start | bytes 3076
  592.2 20.8 %all-to-all-start.1 = ((bf16[8,16,4096]{2,1,0:T(8,128)(2,1)}), bf16[8,16,4096]{2,1,0:T(8,128)(2,1)S(1)}, u32[]{:S(2)}, u32[]{:S(2)}) async-start(bf16[8,16,4096]{2,1,0:T(8,128)(2,1)} %broadcast_in_dim.79), calls=%async_computation.1 | async-start | bytes 2097152 | tf_op jit(solution)/shard_map/all_to_all | solution.py:48
  597.9 58.6 %all-gather.5.cloned.1.call-start = ((), (), s32[]{:S(2)}) async-start(), calls=%async_computation.3 | async-start | bytes 2621440 | tf_op jit(solution)/shard_map/all_gather | solution.py:60
  660.7 9.7 %copy-start.12 = (pred[256]{0:T(512)(128)(4,1)S(1)}, pred[256]{0:T(512)(128)(4,1)}, u32[]{:S(2)}) copy-start(pred[256]{0:T(512)(128)(4,1)} %copy-done.11) | copy-start | bytes 772
Sparse Core Ops, SparseCore 0:
  10.1 54.8 all-gather.2
  626.0 30.4 all-gather.4
where the time goes:
time: 766 us; the launch traced here: 758 us
  matrix products  221 us (29%)
  local copies, waits for them, and re-layouts  216 us (28%)
  other arithmetic  114 us (15%)
  waiting for transfers between devices  104 us (14%)
  blocking collectives  45.8 us (6%)
  loops' own time  27.4 us (4%)
  starting transfers between devices  15.6 us (2%)
  between operations  14.5 us (2%)
    dot_general x48, matrix products, dot_plain(): return jnp.dot(left, right, preferred_element_type=jnp.float32)  105 us
    dot_general x32, matrix products, dot_right_t(): lax.dot_general(left, right, (((1,), (1,)), ((), ())), preferred_element_...  95 us
    all_gather x1, waiting for transfers between devices, per_device(): everything = lax.all_gather(masters, COL, axis=0, tiled=True)  55.1 us
    rev x3, local copies, waits for them, and re-layouts, orient_cells(): cells = jnp.where(flip_second[..., None, None], cells[..., :, ::-1], cells)  39.6 us
    rev x3, local copies, waits for them, and re-layouts, orient_cells(): cells = jnp.where(flip_first[..., None, None], cells[..., ::-1, :], cells)  35.8 us
    all_to_all x1, blocking collectives, sent_and_summed(): lax.all_to_all(cut_along(value, dim, peers), axis, 0, 0, tiled=True)  35 us
    select_n x3, other arithmetic, orient_cells(): cells = jnp.where(flip_first[..., None, None], cells[..., ::-1, :], cells)  30.4 us
    another operation x1, loops' own time, per_device(): lax.map(one_tile, jnp.arange(TPD * TPD, dtype=jnp.int32))  27.4 us
  transfers between devices with their start and end apart: 7, of which 7 were waited for; matrix products, arithmetic and copies ran while one was open for 1% of the time, Pallas kernels for 0%

commit v1 on v0

v1 whole, which is shorter than its diff:
```python
import functools

import jax
import jax.numpy as jnp
import numpy as np
from jax import lax
from jax.experimental import pallas as pl
from jax.experimental.pallas import tpu as pltpu
from jax.sharding import PartitionSpec as P

TILE, HALO, CELL, BAND, NK, PAD = 512, 64, 64, 128, 8, 640
GRID = 256
SIDE = 1024
BOTH = ("row", "col")
F32, BF16 = jnp.float32, jnp.bfloat16


def waves(positions, period):
    freqs = np.arange(BAND) - BAND // 2
    angles = 2.0 * np.pi * ((freqs[:, None] * positions[None, :]) % period) / period
    return np.cos(angles), np.sin(angles)


def mean_gain(cos, sin):
    rounded = [t.astype(jnp.bfloat16).astype(np.float64) for t in (cos, sin)]
    return (rounded[0] * cos + rounded[1] * sin).mean(1)


@functools.cache
def constant_tables():
    cos_c, sin_c = waves(np.arange(GRID), GRID)
    cos_p, sin_p = waves(np.arange(PAD), PAD)
    cos_i, sin_i = cos_p[:, HALO : HALO + TILE], sin_p[:, HALO : HALO + TILE]
    by_pixel = np.concatenate([cos_p.T, sin_p.T], 1)
    first = np.zeros((2, 768, 256))
    first[0, 0:576] = by_pixel[64:640]
    first[0, 640:704] = by_pixel[0:64]
    first[1, 64:640] = by_pixel[0:576]
    first[1, 704:768] = by_pixel[576:640]
    second = np.concatenate([cos_p, sin_p], 0)
    up_u = np.block([[cos_c.T, -sin_c.T], [sin_c.T, cos_c.T]])
    up_v = np.block([[cos_c, sin_c], [-sin_c, cos_c]])
    places = (HALO + np.arange(TILE)) / PAD
    orders = np.arange(1, BAND)
    shift = places[:, None] - np.arange(GRID)[None, :] / GRID
    fine = (1.0 + 2.0 * np.cos(2 * np.pi * shift[..., None] * orders).sum(-1)) / GRID
    out_v = np.block([[cos_i, -sin_i], [-sin_i, -cos_i]])
    out_u = np.concatenate([cos_i.T, -sin_i.T], 1)
    high = fine.astype(jnp.bfloat16)
    low = (fine - high.astype(np.float64)).astype(jnp.bfloat16)
    cast = lambda a: np.ascontiguousarray(a).astype(jnp.bfloat16)
    gain = mean_gain(cos_i, sin_i) / mean_gain(cos_c, sin_c)
    return [
        np.outer(gain, gain).astype(np.float32), cast(first), cast(second), cast(up_u), cast(up_u.T), cast(up_v), cast(up_v.T),
        high, low, cast(fine.T), cast(low.T), cast(out_v), cast(out_u),
    ]


def dot(a, b):
    return jnp.dot(a, b, preferred_element_type=F32)


def index_vectors(orient):
    lane = lax.broadcasted_iota(jnp.int32, (8, 128), 1)
    sub = lax.broadcasted_iota(jnp.int32, (8, 128), 0)
    flip_rows = lax.rem(orient, 2) == 1
    flip_cols = orient >= 2
    lanes = jnp.where(flip_cols, jnp.where(lane < 64, 63 - lane, 191 - lane), lane)
    subs = jnp.where(flip_rows, 7 - sub, sub)
    return flip_rows, lanes, subs


def oriented(groups, orient):
    flip_rows, lanes, subs = index_vectors(orient)
    turned = []
    for g in groups:
        g = jnp.take_along_axis(g, lanes, axis=1)
        turned.append(jnp.take_along_axis(g, subs, axis=0))
    return [
        jnp.where(flip_rows, pltpu.roll(turned[3 - i], 64, 1), turned[i]) for i in range(4)
    ]


def pair_image(cells_ref, loc_a, turn_a, loc_b, turn_b):
    lane = lax.broadcasted_iota(jnp.int32, (8, 128), 1)
    a = oriented([cells_ref[loc_a, 8 * i : 8 * i + 8, :] for i in range(4)], turn_a)
    b = oriented([cells_ref[loc_b, 8 * i : 8 * i + 8, :] for i in range(4)], turn_b)
    top = [jnp.where(lane < 64, a[i], pltpu.roll(b[i], 64, 1)) for i in range(4)]
    low = [jnp.where(lane < 64, pltpu.roll(a[i], 64, 1), b[i]) for i in range(4)]
    return jnp.concatenate(top + low, axis=0)


def fill_cells(parts, cells_ref):
    for n, part in enumerate(parts):
        cells_ref[pl.ds(32 * n, 32)] = part[...].astype(F32)


def main_kernel(*refs):
    codes, weights = refs[0:2]
    parts = refs[2:10]
    free, top, bottom, before, after, target, spectra = refs[10:17]
    (gain, first, second, up_u, up_ut, up_v, up_vt, fine, fine_lo, fine_t, fine_tlo, out_v, out_u) = refs[17:30]
    resist_out, free_out, own_out, other_out = refs[30:34]
    cells, mask, shading, fields, amps, halves, sums = refs[34:41]

    def code(a, b):
        return codes[a * 18 + b], codes[324 + a * 18 + b]

    fill_cells(parts, cells)

    def interior(a, _):
        rows = pl.ds(pl.multiple_of(a * 64, 64), 64)
        rows_m = pl.ds(pl.multiple_of(a * 64 + 64, 64), 64)
        for p in range(8):
            cols = slice(p * 128, p * 128 + 128)
            image = pair_image(cells, *code(a + 1, 2 * p + 1), *code(a + 1, 2 * p + 2))
            value = jnp.tanh(image + free[rows, cols])
            shading[rows, cols] = value
            mask[rows_m, cols] = value.astype(BF16)
        return 0

    lax.fori_loop(0, 16, interior, 0)

    for a, strip, flag in ((0, top, 648), (17, bottom, 649)):
        for p in range(8):
            cols = slice(p * 128, p * 128 + 128)
            image = pair_image(cells, *code(a, 2 * p + 1), *code(a, 2 * p + 2))
            value = jnp.tanh(image + strip[0:64, cols].astype(F32))
            value = jnp.where(codes[flag] > 0, value, 0.0)
            mask[a * 64 : a * 64 + 64, cols] = value.astype(BF16)

    def edge_cols(n, _):
        for u in range(3):
            edge_cell(n * 3 + u)
        return 0

    def edge_cell(a):
        rows = pl.ds(pl.multiple_of(a * 64, 64), 64)
        image = pair_image(cells, *code(a, 0), *code(a, 17))
        strips = jnp.concatenate([before[rows, :], after[rows, :]], axis=1)
        value = jnp.tanh(image + strips.astype(F32))
        lane = lax.broadcasted_iota(jnp.int32, (64, 128), 1)
        at_row = jnp.where(a == 0, codes[648], jnp.where(a == 17, codes[649], 1))
        keep = jnp.where(lane < 64, codes[650], codes[651]) * at_row
        mask[rows, 1024:1152] = jnp.where(keep > 0, value, 0.0).astype(BF16)

    lax.fori_loop(0, 6, edge_cols, 0)

    def tile(t, _):
        i, j = t // 2, t % 2
        rows_w = pl.ds(pl.multiple_of(i * TILE, 128), PAD)
        window = jnp.concatenate(
            [mask[rows_w, pl.ds(pl.multiple_of(j * 384, 128), 640)], mask[rows_w, 1024:1152]], axis=1
        )
        forw = dot(window, first[j]).astype(BF16)
        spec = dot(second[...], forw)
        scale = gain[...] * (1.0 / PAD)
        spec_re = (spec[:128, :128] + spec[128:, 128:]) * scale
        spec_im = (spec[128:, :128] - spec[:128, 128:]) * scale
        for k in range(NK):
            at = slice(k * 128, k * 128 + 128)
            k_re, k_im = spectra[0, :, at], spectra[1, :, at]
            amps[0:128, at] = (k_re * spec_re - k_im * spec_im).astype(BF16)
            amps[128:256, at] = (k_re * spec_im + k_im * spec_re).astype(BF16)
        halves[...] = dot(up_u[...], amps[...]).astype(BF16)
        intensity = jnp.zeros((GRID, GRID), F32)
        for k in range(NK):
            at = slice(k * 128, k * 128 + 128)
            left = jnp.concatenate([halves[0:256, at], halves[256:512, at]], axis=1)
            field = dot(left, up_v[...]) * (1.0 / BAND)
            fields[k] = field
            re, im = field[:, :256], field[:, 256:]
            intensity = intensity + weights[k] * (re * re + im * im)
        coarse = intensity.astype(BF16)
        half_fine = dot(fine[...], coarse) + dot(fine_lo[...], coarse)
        half_fine = half_fine.astype(BF16)
        image = dot(half_fine, fine_t[...]) + dot(half_fine, fine_tlo[...])
        rows_t = pl.ds(pl.multiple_of(i * TILE, TILE), TILE)
        cols_t = pl.ds(pl.multiple_of(j * TILE, TILE), TILE)
        resist = jax.nn.sigmoid(2.0 * (image - 1.8))
        resist_out[rows_t, cols_t] = resist
        slopes = (4.0 * (resist - target[rows_t, cols_t]) * resist * (1.0 - resist)).astype(BF16)
        back = dot(fine_t[...], dot(slopes, fine[...]).astype(BF16))
        for k in range(NK):
            at = slice(k * 128, k * 128 + 128)
            scaled = back * (weights[k] * (2.0 / BAND))
            both = jnp.concatenate(
                [(scaled * fields[k, :, :256]).astype(BF16), (scaled * fields[k, :, 256:]).astype(BF16)], axis=1
            )
            low = dot(both, up_vt[...]).astype(BF16)
            halves[0:256, at] = low[:, :128]
            halves[256:512, at] = low[:, 128:]
        bspec_re = jnp.zeros((128, 128), F32)
        bspec_im = jnp.zeros((128, 128), F32)
        bamp = dot(up_ut[...], halves[...])
        for k in range(NK):
            at = slice(k * 128, k * 128 + 128)
            k_re, k_im = spectra[0, :, at], spectra[1, :, at]
            re, im = bamp[:128, at], bamp[128:, at]
            bspec_re = bspec_re + (k_re * re + k_im * im)
            bspec_im = bspec_im + (k_re * im - k_im * re)
        bspec = jnp.concatenate([bspec_re * scale, bspec_im * scale], axis=1)
        bforw = dot(bspec.astype(BF16), out_v[...]).astype(BF16)
        stacked = jnp.concatenate([bforw[:, :TILE], bforw[:, TILE:]], axis=0)
        gradient = dot(out_u[...], stacked)
        shade = shading[rows_t, cols_t]
        grad = gradient * (1.0 - shade * shade)
        shading[rows_t, cols_t] = grad
        free_out[rows_t, cols_t] = free[rows_t, cols_t] - grad
        return 0

    lax.fori_loop(0, 4, tile, 0)

    def clear(n, _):
        sums[pl.ds(n * 8, 8)] = jnp.zeros((8, 32, 128), F32)
        return 0

    lax.fori_loop(0, 32, clear, 0)
    lane = lax.broadcasted_iota(jnp.int32, (8, 128), 1)

    def collect(a, _):
        rows = pl.multiple_of(a * 64, 64)
        for batch in range(4):
            found = []
            for p in (2 * batch, 2 * batch + 1):
                cols = slice(p * 128, p * 128 + 128)
                upper = [shading[pl.ds(rows + 8 * i, 8), cols] for i in range(4)]
                lower = [shading[pl.ds(rows + 32 + 8 * i, 8), cols] for i in range(4)]
                left = [jnp.where(lane < 64, upper[i], pltpu.roll(lower[i], 64, 1)) for i in range(4)]
                right = [jnp.where(lane < 64, pltpu.roll(upper[i], 64, 1), lower[i]) for i in range(4)]
                for b, groups in ((2 * p + 1, left), (2 * p + 2, right)):
                    loc, turn = code(a + 1, b)
                    found.append((loc, oriented(groups, turn)))
            for loc, out in found:
                for i in range(4):
                    sums[loc, 8 * i : 8 * i + 8, :] = sums[loc, 8 * i : 8 * i + 8, :] + out[i]
        return 0

    lax.fori_loop(0, 16, collect, 0)
    own_out[...] = sums[0:128].astype(BF16)
    other_out[...] = sums[128:256].astype(BF16)


def final_kernel(*refs):
    codes = refs[0]
    parts = refs[1:9]
    free, out, cells = refs[9:12]
    step = pl.program_id(0)

    @pl.when(step == 0)
    def _():
        fill_cells(parts, cells)

    def interior(r, _):
        rows = pl.ds(pl.multiple_of(r * 64, 64), 64)
        for p in range(8):
            cols = slice(p * 128, p * 128 + 128)
            at = (step * 4 + r + 1) * 18 + 2 * p
            image = pair_image(cells, codes[at + 1], codes[325 + at], codes[at + 2], codes[326 + at])
            out[rows, cols] = jnp.tanh(image + free[rows, cols])
        return 0

    lax.fori_loop(0, 4, interior, 0)


def flat(x, c, y, z):
    return ((x % 4) * 2 + c) * 16 + (y % 4) * 4 + z % 4


CHIPS = [(x, y, z) for x in range(4) for y in range(4) for z in range(4)]


def shift_first(d):
    return [(flat(x, 0, y, z), flat(x, 0, y, z + d)) for x, y, z in CHIPS] + [
        (flat(x, 1, y, z), flat(x, 1, y + d, z)) for x, y, z in CHIPS
    ]


def shift_second(d):
    return [(flat(x, 0, y, z), flat(x, 0, y + d, z)) for x, y, z in CHIPS] + [
        (flat(x, 1, y, z), flat(x, 1, y, z + d)) for x, y, z in CHIPS
    ]


def shift_x(d):
    return [(flat(x, c, y, z), flat(x + d, c, y, z)) for x, y, z in CHIPS for c in range(2)]


SWAP = [(flat(x, c, y, z), flat(x, 1 - c, y, z)) for x, y, z in CHIPS for c in range(2)]


def send(value, pairs):
    return lax.ppermute(value, BOTH, pairs)


def gathered(piece):
    got = {d: send(piece, shift_first(d)) for d in (2, 1, 3)}
    group = jnp.concatenate([piece, got[1], got[2], got[3]], axis=0)
    far = {d: send(group, shift_second(d)) for d in (2, 1, 3)}
    mine = [group, far[1], far[2], far[3]]
    return mine + [send(part, SWAP) for part in mine]


def scattered_sum(own, other):
    total = (own.astype(F32) + send(other, SWAP).astype(F32)).astype(BF16).reshape(4, 32, 32, 128)
    got = [send(total[d], shift_second(-d)) for d in (2, 1, 3)]
    total = sum((g.astype(F32) for g in got), total[0].astype(F32)).astype(BF16).reshape(4, 8, 32, 128)
    got = [send(total[d], shift_first(-d)) for d in (2, 1, 3)]
    total = sum((g.astype(F32) for g in got), total[0].astype(F32)).astype(BF16)
    got = [send(total, shift_x(d)) for d in (2, 1, 3)]
    return sum((g.astype(F32) for g in got), total.astype(F32))


def to_wire(rows):
    cells = rows.reshape(-1, CELL, CELL)
    return jnp.concatenate([cells[:, :32, :], cells[:, 32:, :]], axis=2)


def from_wire(wire):
    return jnp.concatenate([wire[:, :, :64], wire[:, :, 64:]], axis=1)


def smooth(grids):
    framed = jnp.pad(grids, ((0, 0), (1, 1), (1, 1)))
    beside = framed[:, 2:, 1:-1] + framed[:, :-2, 1:-1] + framed[:, 1:-1, 2:] + framed[:, 1:-1, :-2]
    return 0.5 * grids + 0.125 * beside


def steps(axis):
    n = lax.axis_size(axis)
    up = [(i, i + 1) for i in range(n - 1)]
    return up, [(b, a) for a, b in up]


def per_device(masters, inst_master, inst_orient, owner_map, tile_free, target, spectra, weights):
    row, col = lax.axis_index("row"), lax.axis_index("col")
    core, y, z = row % 2, col // 4, col % 4
    own_cells = lax.dynamic_slice_in_dim(masters, core * 8, 8, 0)
    parts = gathered(to_wire(own_cells.astype(BF16)))

    def codes_of(a):
        return jnp.pad(a.astype(BF16), ((0, 0), (0, SIDE - a.shape[1])))

    def strip(at, line):
        pad = jnp.concatenate([codes_of(inst_master[line : line + 1]), codes_of(inst_orient[line : line + 1])], 0)
        return jnp.concatenate([tile_free[at : at + 64].astype(BF16), jnp.pad(pad, ((0, 14), (0, 0)))], 0)

    up, down = steps("row")
    above = lax.ppermute(strip(SIDE - 64, 15), "row", up)
    below = lax.ppermute(strip(0, 0), "row", down)

    def ints(a):
        return a.astype(F32).astype(jnp.int32)

    tall_master = jnp.concatenate([ints(above[64:65, :16]), inst_master, ints(below[64:65, :16])], 0)
    tall_orient = jnp.concatenate([ints(above[65:66, :16]), inst_orient, ints(below[65:66, :16])], 0)

    def side(at, line):
        pixels = jnp.concatenate(
            [above[:64, at : at + 64], tile_free[:, at : at + 64].astype(BF16), below[:64, at : at + 64]], 0
        )
        lines = jnp.stack([tall_master[:, line], tall_orient[:, line]], 1).astype(BF16)
        return jnp.concatenate([pixels, jnp.pad(lines, ((0, 14), (0, 62)))], 0)

    up, down = steps("col")
    before = lax.ppermute(side(SIDE - 64, 15), "col", up)
    after = lax.ppermute(side(0, 0), "col", down)
    all_master = jnp.concatenate([ints(before[1152:1170, 0:1]), tall_master, ints(after[1152:1170, 0:1])], 1)
    all_orient = jnp.concatenate([ints(before[1152:1170, 1:2]), tall_orient, ints(after[1152:1170, 1:2])], 1)

    matches = all_master[..., None] == jnp.arange(owner_map.shape[0], dtype=jnp.int32)
    slots = jnp.sum(jnp.where(matches, owner_map, 0), axis=-1)
    at_y, at_z, half, entry = slots // 64, (slots // 16) % 4, (slots // 8) % 2, slots % 8
    dy, dz = (y - at_y) % 4, (z - at_z) % 4
    far, near = jnp.where(half == 0, dy, dz), jnp.where(half == 0, dz, dy)
    locs = (jnp.where(half == core, 0, 1) * 16 + far * 4 + near) * 8 + entry
    inside = jnp.stack([row > 0, row < 7, col > 0, col < 15]).astype(jnp.int32)
    codes = jnp.concatenate([locs.reshape(-1), all_orient.reshape(-1), inside])

    vmem, smem = pl.BlockSpec(memory_space=pltpu.VMEM), pl.BlockSpec(memory_space=pltpu.SMEM)
    wide = jax.ShapeDtypeStruct((SIDE, SIDE), F32)
    sums_shape = jax.ShapeDtypeStruct((128, 32, 128), BF16)
    resist, free_new, own, other = pl.pallas_call(
        main_kernel,
        out_shape=(wide, wide, sums_shape, sums_shape),
        in_specs=[smem] * 2 + [vmem] * 28,
        out_specs=(vmem,) * 4,
        scratch_shapes=[
            pltpu.VMEM((256, 32, 128), F32),
            pltpu.VMEM((1152, 1152), BF16),
            pltpu.VMEM((SIDE, SIDE), F32),
            pltpu.VMEM((NK, GRID, 2 * GRID), F32),
            pltpu.VMEM((256, 1024), BF16),
            pltpu.VMEM((512, 1024), BF16),
            pltpu.VMEM((256, 32, 128), F32),
        ],
        compiler_params=pltpu.CompilerParams(vmem_limit_bytes=60 * 1024 * 1024),
        name="image_and_gradient",
    )(
        codes, weights, *parts, tile_free, above, below, before, after, target,
        spectra.reshape(2, BAND, NK * BAND), *constant_tables(),
    )

    summed = scattered_sum(own, other)
    fresh = smooth(own_cells.reshape(8, CELL, CELL) - 0.05 * from_wire(summed))
    fresh_wire = jnp.concatenate([fresh[:, :32, :], fresh[:, 32:, :]], axis=2).astype(BF16)
    parts = gathered(fresh_wire)
    new_mask = pl.pallas_call(
        final_kernel,
        out_shape=wide,
        grid=(4,),
        in_specs=[smem] + [vmem] * 8 + [pl.BlockSpec((256, SIDE), lambda s: (s, 0))],
        out_specs=pl.BlockSpec((256, SIDE), lambda s: (s, 0)),
        scratch_shapes=[pltpu.VMEM((256, 32, 128), F32)],
        compiler_params=pltpu.CompilerParams(vmem_limit_bytes=40 * 1024 * 1024),
        name="final_mask",
    )(codes, *parts, free_new)
    mine = from_wire(parts[0][:8]).reshape(8, CELL * CELL).astype(F32)
    others = from_wire(parts[4][:8]).reshape(8, CELL * CELL).astype(F32)
    masters_out = jnp.where(core == 0, jnp.concatenate([mine, others], 0), jnp.concatenate([others, mine], 0))
    return resist, new_mask, masters_out


def solution(mesh):
    placed = (P("col", None), P(*BOTH), P(*BOTH), P(), P(*BOTH), P(*BOTH), P(), P())
    return jax.shard_map(
        per_device,
        mesh=mesh,
        in_specs=placed,
        out_specs=(P(*BOTH), P(*BOTH), P("col", None)),
        check_vma=False,
    )
```

time: 766 us -> 182 us (0.24); the launches traced: 758 us -> 182 us
  matrix products: 221 us -> 0 us
  local copies, waits for them, and re-layouts: 216 us -> 9.83 us
  other arithmetic: 114 us -> 15.4 us
  Pallas kernels: 0 us -> 60.6 us
  waiting for transfers between devices: 104 us -> 44 us
  blocking collectives: 45.8 us -> 0 us
  starting transfers between devices: 15.6 us -> 50.7 us
  loops' own time: 27.4 us -> 0 us
  between operations: 14.5 us -> 1.04 us
    dot_general x105 -> x0, matrix products: 221 us -> none  [the longest x48 105 us: dot_plain(): return jnp.dot(left, right, preferred_element_type=jnp.float32)]
    all_gather x2 -> x0, waiting for transfers between devices: 77.3 us -> none  [the longest x1 55.1 us: per_device(): everything = lax.all_gather(masters, COL, axis=0, tiled=True)]
    rev x6 -> x0, local copies, waits for them, and re-layouts: 75.4 us -> none  [the longest x3 39.6 us: orient_cells(): cells = jnp.where(flip_second[..., None, None], cells[..., :, ::-1], cells)]
    reshape x27 -> x4, local copies, waits for them, and re-layouts: 74.8 us -> 1.53 us  [the longest x1 1.17 us: per_device(): spectra.reshape(2, BAND, NK * BAND)]
    pallas_call x0 -> x2, Pallas kernels: none -> 60.6 us  [the longest x1 50.5 us: per_device(): pl.pallas_call(main_kernel, out_shape=(wide, wide, sums_shape, sums_shape...]
    select_n x7 -> x1, other arithmetic: 49.9 us -> 0.72 us  [per_device(): jnp.where(core == 0, jnp.concatenate([mine, others], 0), jnp.concatenate(...]
    ppermute x4 -> x34, starting transfers between devices: 9.85 us -> 50.7 us  [the longest x30 39.2 us: send(): return lax.ppermute(value, BOTH, pairs)]
    all_to_all x1 -> x0, blocking collectives: 35 us -> none  [sent_and_summed(): lax.all_to_all(cut_along(value, dim, peers), axis, 0, 0, tiled=True)]
  transfers between devices with their start and end apart: 7 -> 34, of which waited for: 7 -> 17; matrix products, arithmetic and copies ran while one was open for 1% -> 9% of each run, Pallas kernels for 0% -> 0%
where the time goes in v1:
time: 182 us
  Pallas kernels  60.6 us (33%)
  starting transfers between devices  50.7 us (28%)
  waiting for transfers between devices  44 us (24%)
  other arithmetic  15.4 us (8%)
  local copies, waits for them, and re-layouts  9.83 us (5%)
    pallas_call x1, Pallas kernels, per_device(): pl.pallas_call(main_kernel, out_shape=(wide, wide, sums_shape, sums_shape...  50.5 us
    ppermute x30, starting transfers between devices, send(): return lax.ppermute(value, BOTH, pairs)  39.2 us
    ppermute x30, waiting for transfers between devices, send(): return lax.ppermute(value, BOTH, pairs)  28.6 us
    pallas_call x1, Pallas kernels, per_device(): pl.pallas_call(final_kernel, out_shape=wide, grid=(4,), in_specs=[smem] +...  10.1 us
    ppermute x1, waiting for transfers between devices, per_device(): after = lax.ppermute(side(0, 0), 'col', down)  9.91 us
    ppermute x1, waiting for transfers between devices, per_device(): before = lax.ppermute(side(SIDE - 64, 15), 'col', up)  5.52 us
    another operation x4, other arithmetic  4.12 us
    ppermute x1, starting transfers between devices, per_device(): below = lax.ppermute(strip(0, 0), 'row', down)  4.1 us
  transfers between devices with their start and end apart: 34, of which 17 were waited for; matrix products, arithmetic and copies ran while one was open for 9% of the time, Pallas kernels for 0%

profile of v1, /device:TPU:1, one launch (start us, length us, event | category | flops | bytes accessed | tf_op | source)
XLA Modules:
  0.0 181.6 jit_solution(12933629148558302013)
XLA Ops:
  3.1 3.6 %collective-permute-start.6 = (bf16[8,32,128]{2,1,0:T(8,128)(2,1)}, bf16[8,32,128]{2,1,0:T(8,128)(2,1)}, u32[]{:S(2)}, u32[]{:S(2)}) collective-permute-start(bf16[8,32,128]{2,1,0:T(8,128)(2,1)} %pad_maximum_fusion.2), channel_id=1, source_target_pairs={{0,3},{1,0},{2,1},{3,2},{4,7},{5,4},{6,5},{7,6},{8,11},{9,8},{10,9... | collective-permute-start | bytes 196616 | tf_op jit(solution)/shard_map/ppermute | solution.py:293
  9.1 2.5 %convert.34 = bf16[1024,1024]{1,0:T(8,128)(2,1)S(1)} convert(f32[1024,1024]{1,0:T(8,128)} %refs_10_.1) | non-fusion elementwise | flops 1048576 | bytes 6291456 | tf_op jit(solution)/shard_map/convert.21
  12.4 4.1 %collective-permute-start.1 = (bf16[80,1024]{1,0:T(8,128)(2,1)}, bf16[80,1024]{1,0:T(8,128)(2,1)}, u32[]{:S(2)}, u32[]{:S(2)}) collective-permute-start(bf16[80,1024]{1,0:T(8,128)(2,1)} %fusion.14), channel_id=1, source_target_pairs={{16,0},{32,16},{48,32},{64,48},{80,64},{96,80},{112,96},{17,1},{33... | collective-permute-start | bytes 491528 | tf_op jit(solution)/shard_map/ppermute | solution.py:350
  17.2 3.0 %collective-permute-start = (bf16[80,1024]{1,0:T(8,128)(2,1)}, bf16[80,1024]{1,0:T(8,128)(2,1)}, u32[]{:S(2)}, u32[]{:S(2)}) collective-permute-start(bf16[80,1024]{1,0:T(8,128)(2,1)} %fusion.13), channel_id=1, source_target_pairs={{0,16},{16,32},{32,48},{48,64},{64,80},{80,96},{96,112},{1,17},{17... | collective-permute-start | bytes 491528 | tf_op jit(solution)/shard_map/ppermute | solution.py:349
  24.7 2.0 %collective-permute-start.7 = (bf16[32,32,128]{2,1,0:T(8,128)(2,1)S(1)}, bf16[32,32,128]{2,1,0:T(8,128)(2,1)S(1)}, u32[]{:S(2)}, u32[]{:S(2)}) collective-permute-start(bf16[32,32,128]{2,1,0:T(8,128)(2,1)S(1)} %pad_maximum_fusion.refs_2_), channel_id=1, source_target_pairs={{0,4},{1,5},{2,6},{3,7},{4,8},{5,9},{6,10},{7,11},{8,12},{9,13},{1... | collective-permute-start | bytes 786440 | tf_op jit(solution)/shard_map/ppermute | solution.py:293
  36.0 9.9 %collective-permute-done.3.refs_14_ = bf16[1184,64]{1,0:T(8,128)(2,1)S(1)} collective-permute-done((bf16[1184,64]{1,0:T(8,128)(2,1)S(1)}, bf16[1184,64]{1,0:T(8,128)(2,1)S(1)}, u32[]{:S(2)}, u32[]{:S(2)}) %collective-permute-start.3) | collective-permute-done | bytes 151584 | tf_op jit(solution)/shard_map/ppermute | solution.py:367
  45.9 3.2 %collective-permute-start.2 = (bf16[1184,64]{1,0:T(8,128)(2,1)S(1)}, bf16[1184,64]{1,0:T(8,128)(2,1)S(1)}, u32[]{:S(2)}, u32[]{:S(2)}) collective-permute-start(bf16[1184,64]{1,0:T(8,128)(2,1)S(1)} %fusion.4), channel_id=1, source_target_pairs={{0,1},{1,2},{2,3},{3,4},{4,5},{5,6},{6,7},{7,8},{8,9},{9,10},{10,1... | collective-permute-start | bytes 454664 | tf_op jit(solution)/shard_map/ppermute | solution.py:366
  49.3 5.5 %collective-permute-done.2.refs_13_ = bf16[1184,64]{1,0:T(8,128)(2,1)S(1)} collective-permute-done((bf16[1184,64]{1,0:T(8,128)(2,1)S(1)}, bf16[1184,64]{1,0:T(8,128)(2,1)S(1)}, u32[]{:S(2)}, u32[]{:S(2)}) %collective-permute-start.2) | collective-permute-done | bytes 151584 | tf_op jit(solution)/shard_map/ppermute | solution.py:366
  56.2 1.8 collective-permute-start.11
  60.9 50.5 %image_and_gradient.1 = (f32[1024,1024]{1,0:T(8,128)}, f32[1024,1024]{1,0:T(8,128)}, bf16[128,32,128]{2,1,0:T(8,128)(2,1)}, bf16[128,32,128]{2,1,0:T(8,128)(2,1)}) custom-call(s32[652]{0:T(1024)} %pad_add_fusion.2.refs_0_, f32[8]{0:T(128)} %refs_1_.1, bf16[32,32,128]{2,1,0:T(8,128)(2,1)} %copy-done.2, bf16[32,32,128]{2,1,0:T(8,128)(2,1)} %copy-done.8, ...), custom_call_target="tpu_custom_call" | custom-call | tf_op jit(solution)/shard_map/image_and_gradient/pallas_call | solution.py:383
  111.8 2.5 %collective-permute-done.14 = bf16[128,32,128]{2,1,0:T(8,128)(2,1)S(1)} collective-permute-done((bf16[128,32,128]{2,1,0:T(8,128)(2,1)}, bf16[128,32,128]{2,1,0:T(8,128)(2,1)S(1)}, u32[]{:S(2)}, u32[]{:S(2)}) %collective-permute-start.14) | collective-permute-done | bytes 1048608 | tf_op jit(solution)/shard_map/ppermute | solution.py:293
  115.9 2.3 %collective-permute-start.17 = (bf16[32,32,128]{2,1,0:T(8,128)(2,1)S(1)}, bf16[32,32,128]{2,1,0:T(8,128)(2,1)S(1)}, u32[]{:S(2)}, u32[]{:S(2)}) collective-permute-start(bf16[32,32,128]{2,1,0:T(8,128)(2,1)S(1)} %get-tuple-element.18), channel_id=1, source_target_pairs={{0,4},{1,5},{2,6},{3,7},{4,8},{5,9},{6,10},{7,11},{8,12},{9,13},{1... | collective-permute-start | bytes 786440 | tf_op jit(solution)/shard_map/ppermute | solution.py:293
  118.1 1.9 %collective-permute-start.16 = (bf16[32,32,128]{2,1,0:T(8,128)(2,1)S(1)}, bf16[32,32,128]{2,1,0:T(8,128)(2,1)S(1)}, u32[]{:S(2)}, u32[]{:S(2)}) collective-permute-start(bf16[32,32,128]{2,1,0:T(8,128)(2,1)S(1)} %get-tuple-element.19), channel_id=1, source_target_pairs={{0,12},{1,13},{2,14},{3,15},{4,0},{5,1},{6,2},{7,3},{8,4},{9,5},{1... | collective-permute-start | bytes 786440 | tf_op jit(solution)/shard_map/ppermute | solution.py:293
  121.2 2.6 %collective-permute-done.17 = bf16[32,32,128]{2,1,0:T(8,128)(2,1)S(1)} collective-permute-done((bf16[32,32,128]{2,1,0:T(8,128)(2,1)S(1)}, bf16[32,32,128]{2,1,0:T(8,128)(2,1)S(1)}, u32[]{:S(2)}, u32[]{:S(2)}) %collective-permute-start.17) | collective-permute-done | bytes 262176 | tf_op jit(solution)/shard_map/ppermute | solution.py:293
  123.8 2.4 %collective-permute-done.16 = bf16[32,32,128]{2,1,0:T(8,128)(2,1)S(1)} collective-permute-done((bf16[32,32,128]{2,1,0:T(8,128)(2,1)S(1)}, bf16[32,32,128]{2,1,0:T(8,128)(2,1)S(1)}, u32[]{:S(2)}, u32[]{:S(2)}) %collective-permute-start.16) | collective-permute-done | bytes 262176 | tf_op jit(solution)/shard_map/ppermute | solution.py:293
  132.5 2.9 %collective-permute-done.18 = bf16[8,32,128]{2,1,0:T(8,128)(2,1)S(1)} collective-permute-done((bf16[8,32,128]{2,1,0:T(8,128)(2,1)S(1)}, bf16[8,32,128]{2,1,0:T(8,128)(2,1)S(1)}, u32[]{:S(2)}, u32[]{:S(2)}) %collective-permute-start.18) | collective-permute-done | bytes 65568 | tf_op jit(solution)/shard_map/ppermute | solution.py:293
  135.5 2.5 %collective-permute-start.23 = (bf16[8,32,128]{2,1,0:T(8,128)(2,1)S(1)}, bf16[8,32,128]{2,1,0:T(8,128)(2,1)S(1)}, u32[]{:S(2)}, u32[]{:S(2)}) collective-permute-start(bf16[8,32,128]{2,1,0:T(8,128)(2,1)S(1)} %add_convert_fusion.2), channel_id=1, source_target_pairs={{0,96},{16,112},{1,97},{17,113},{2,98},{18,114},{3,99},{19,115},{4... | collective-permute-start | bytes 196616 | tf_op jit(solution)/shard_map/ppermute | solution.py:293
  139.4 3.6 %collective-permute-done.22 = bf16[8,32,128]{2,1,0:T(8,128)(2,1)S(1)} collective-permute-done((bf16[8,32,128]{2,1,0:T(8,128)(2,1)S(1)}, bf16[8,32,128]{2,1,0:T(8,128)(2,1)S(1)}, u32[]{:S(2)}, u32[]{:S(2)}) %collective-permute-start.22) | collective-permute-done | bytes 65568 | tf_op jit(solution)/shard_map/ppermute | solution.py:293
  146.8 1.9 %collective-permute-done.25 = bf16[8,32,128]{2,1,0:T(8,128)(2,1)S(1)} collective-permute-done((bf16[8,32,128]{2,1,0:T(8,128)(2,1)S(1)}, bf16[8,32,128]{2,1,0:T(8,128)(2,1)S(1)}, u32[]{:S(2)}, u32[]{:S(2)}) %collective-permute-start.25) | collective-permute-done | bytes 65568 | tf_op jit(solution)/shard_map/ppermute | solution.py:293
  149.9 6.3 %collective-permute-start.30 = (bf16[32,32,128]{2,1,0:T(8,128)(2,1)S(1)}, bf16[32,32,128]{2,1,0:T(8,128)(2,1)S(1)}, u32[]{:S(2)}, u32[]{:S(2)}) collective-permute-start(bf16[32,32,128]{2,1,0:T(8,128)(2,1)S(1)} %pad_maximum_fusion.1.refs_1_), channel_id=1, source_target_pairs={{0,16},{16,0},{1,17},{17,1},{2,18},{18,2},{3,19},{19,3},{4,20},{20... | collective-permute-start | bytes 786440 | tf_op jit(solution)/shard_map/ppermute | solution.py:293
  159.9 6.1 %collective-permute-done.27.refs_2_ = bf16[32,32,128]{2,1,0:T(8,128)(2,1)S(1)} collective-permute-done((bf16[32,32,128]{2,1,0:T(8,128)(2,1)S(1)}, bf16[32,32,128]{2,1,0:T(8,128)(2,1)S(1)}, u32[]{:S(2)}, u32[]{:S(2)}) %collective-permute-start.27) | collective-permute-done | bytes 262176 | tf_op jit(solution)/shard_map/ppermute | solution.py:293
  166.0 1.7 collective-permute-start.32
  169.2 2.2 %copy-done = f32[1024,1024]{1,0:T(8,128)S(1)} copy-done((f32[1024,1024]{1,0:T(8,128)S(1)}, f32[1024,1024]{1,0:T(8,128)}, u32[]{:S(2)}) %copy-start) | copy-done | bytes 4194328
  171.4 10.1 %final_mask.1 = f32[1024,1024]{1,0:T(8,128)} custom-call(s32[652]{0:T(1024)S(1)} %copy-done.1, bf16[32,32,128]{2,1,0:T(8,128)(2,1)S(1)} %pad_maximum_fusion.1.refs_1_, bf16[32,32,128]{2,1,0:T(8,128)(2,1)S(1)} %collective-permute-done.27.refs_2_, bf16[32,32,128]{2,1,0:T(8,128)(2,1)S(1)} %collective-permute-done.28.refs_3_, ...), custom_call_target="tpu_custom_call" | custom-call | tf_op jit(solution)/shard_map/final_mask/pallas_call | solution.py:408
  (150 shorter events, 45.3 us)
Async XLA Ops:
  3.1 20.6 %collective-permute-start.6 = (bf16[8,32,128]{2,1,0:T(8,128)(2,1)}, bf16[8,32,128]{2,1,0:T(8,128)(2,1)}, u32[]{:S(2)}, u32[]{:S(2)}) collective-permute-start(bf16[8,32,128]{2,1,0:T(8,128)(2,1)} %pad_maximum_fusion.2), channel_id=1, source_target_pairs={{0,3},{1,0},{2,1},{3,2},{4,7},{5,4},{6,5},{7,6},{8,11},{9,8},{10,9... | collective-permute-start | bytes 196616 | tf_op jit(solution)/shard_map/ppermute | solution.py:293
  6.7 17.0 %collective-permute-start.5 = (bf16[8,32,128]{2,1,0:T(8,128)(2,1)}, bf16[8,32,128]{2,1,0:T(8,128)(2,1)}, u32[]{:S(2)}, u32[]{:S(2)}) collective-permute-start(bf16[8,32,128]{2,1,0:T(8,128)(2,1)} %pad_maximum_fusion.2), channel_id=1, source_target_pairs={{0,2},{1,3},{2,0},{3,1},{4,6},{5,7},{6,4},{7,5},{8,10},{9,11},{10,... | collective-permute-start | bytes 196616 | tf_op jit(solution)/shard_map/ppermute | solution.py:293
  7.0 16.7 %collective-permute-start.4 = (bf16[8,32,128]{2,1,0:T(8,128)(2,1)}, bf16[8,32,128]{2,1,0:T(8,128)(2,1)}, u32[]{:S(2)}, u32[]{:S(2)}) collective-permute-start(bf16[8,32,128]{2,1,0:T(8,128)(2,1)} %pad_maximum_fusion.2), channel_id=1, source_target_pairs={{0,1},{1,2},{2,3},{3,0},{4,5},{5,6},{6,7},{7,4},{8,9},{9,10},{10,1... | collective-permute-start | bytes 196616 | tf_op jit(solution)/shard_map/ppermute | solution.py:293
  12.4 16.8 %collective-permute-start.1 = (bf16[80,1024]{1,0:T(8,128)(2,1)}, bf16[80,1024]{1,0:T(8,128)(2,1)}, u32[]{:S(2)}, u32[]{:S(2)}) collective-permute-start(bf16[80,1024]{1,0:T(8,128)(2,1)} %fusion.14), channel_id=1, source_target_pairs={{16,0},{32,16},{48,32},{64,48},{80,64},{96,80},{112,96},{17,1},{33... | collective-permute-start | bytes 491528 | tf_op jit(solution)/shard_map/ppermute | solution.py:350
  17.2 14.3 %collective-permute-start = (bf16[80,1024]{1,0:T(8,128)(2,1)}, bf16[80,1024]{1,0:T(8,128)(2,1)}, u32[]{:S(2)}, u32[]{:S(2)}) collective-permute-start(bf16[80,1024]{1,0:T(8,128)(2,1)} %fusion.13), channel_id=1, source_target_pairs={{0,16},{16,32},{32,48},{48,64},{64,80},{80,96},{96,112},{1,17},{17... | collective-permute-start | bytes 491528 | tf_op jit(solution)/shard_map/ppermute | solution.py:349
  24.7 31.4 %collective-permute-start.7 = (bf16[32,32,128]{2,1,0:T(8,128)(2,1)S(1)}, bf16[32,32,128]{2,1,0:T(8,128)(2,1)S(1)}, u32[]{:S(2)}, u32[]{:S(2)}) collective-permute-start(bf16[32,32,128]{2,1,0:T(8,128)(2,1)S(1)} %pad_maximum_fusion.refs_2_), channel_id=1, source_target_pairs={{0,4},{1,5},{2,6},{3,7},{4,8},{5,9},{6,10},{7,11},{8,12},{9,13},{1... | collective-permute-start | bytes 786440 | tf_op jit(solution)/shard_map/ppermute | solution.py:293
  26.7 31.2 %collective-permute-start.8 = (bf16[32,32,128]{2,1,0:T(8,128)(2,1)S(1)}, bf16[32,32,128]{2,1,0:T(8,128)(2,1)S(1)}, u32[]{:S(2)}, u32[]{:S(2)}) collective-permute-start(bf16[32,32,128]{2,1,0:T(8,128)(2,1)S(1)} %pad_maximum_fusion.refs_2_), channel_id=1, source_target_pairs={{0,8},{1,9},{2,10},{3,11},{4,12},{5,13},{6,14},{7,15},{8,0},{9,1},... | collective-permute-start | bytes 786440 | tf_op jit(solution)/shard_map/ppermute | solution.py:293
  28.2 29.9 %collective-permute-start.9 = (bf16[32,32,128]{2,1,0:T(8,128)(2,1)S(1)}, bf16[32,32,128]{2,1,0:T(8,128)(2,1)S(1)}, u32[]{:S(2)}, u32[]{:S(2)}) collective-permute-start(bf16[32,32,128]{2,1,0:T(8,128)(2,1)S(1)} %pad_maximum_fusion.refs_2_), channel_id=1, source_target_pairs={{0,12},{1,13},{2,14},{3,15},{4,0},{5,1},{6,2},{7,3},{8,4},{9,5},{1... | collective-permute-start | bytes 786440 | tf_op jit(solution)/shard_map/ppermute | solution.py:293
  29.2 29.9 %collective-permute-start.10 = (bf16[32,32,128]{2,1,0:T(8,128)(2,1)S(1)}, bf16[32,32,128]{2,1,0:T(8,128)(2,1)S(1)}, u32[]{:S(2)}, u32[]{:S(2)}) collective-permute-start(bf16[32,32,128]{2,1,0:T(8,128)(2,1)S(1)} %pad_maximum_fusion.refs_2_), channel_id=1, source_target_pairs={{0,16},{16,0},{1,17},{17,1},{2,18},{18,2},{3,19},{19,3},{4,20},{20... | collective-permute-start | bytes 786440 | tf_op jit(solution)/shard_map/ppermute | solution.py:293
  34.5 11.4 %collective-permute-start.3 = (bf16[1184,64]{1,0:T(8,128)(2,1)S(1)}, bf16[1184,64]{1,0:T(8,128)(2,1)S(1)}, u32[]{:S(2)}, u32[]{:S(2)}) collective-permute-start(bf16[1184,64]{1,0:T(8,128)(2,1)S(1)} %fusion.5), channel_id=1, source_target_pairs={{1,0},{2,1},{3,2},{4,3},{5,4},{6,5},{7,6},{8,7},{9,8},{10,9},{11,1... | collective-permute-start | bytes 454664 | tf_op jit(solution)/shard_map/ppermute | solution.py:367
  45.9 8.9 %collective-permute-start.2 = (bf16[1184,64]{1,0:T(8,128)(2,1)S(1)}, bf16[1184,64]{1,0:T(8,128)(2,1)S(1)}, u32[]{:S(2)}, u32[]{:S(2)}) collective-permute-start(bf16[1184,64]{1,0:T(8,128)(2,1)S(1)} %fusion.4), channel_id=1, source_target_pairs={{0,1},{1,2},{2,3},{3,4},{4,5},{5,6},{6,7},{7,8},{8,9},{9,10},{10,1... | collective-permute-start | bytes 454664 | tf_op jit(solution)/shard_map/ppermute | solution.py:366
  115.9 7.9 %collective-permute-start.17 = (bf16[32,32,128]{2,1,0:T(8,128)(2,1)S(1)}, bf16[32,32,128]{2,1,0:T(8,128)(2,1)S(1)}, u32[]{:S(2)}, u32[]{:S(2)}) collective-permute-start(bf16[32,32,128]{2,1,0:T(8,128)(2,1)S(1)} %get-tuple-element.18), channel_id=1, source_target_pairs={{0,4},{1,5},{2,6},{3,7},{4,8},{5,9},{6,10},{7,11},{8,12},{9,13},{1... | collective-permute-start | bytes 786440 | tf_op jit(solution)/shard_map/ppermute | solution.py:293
  118.1 8.1 %collective-permute-start.16 = (bf16[32,32,128]{2,1,0:T(8,128)(2,1)S(1)}, bf16[32,32,128]{2,1,0:T(8,128)(2,1)S(1)}, u32[]{:S(2)}, u32[]{:S(2)}) collective-permute-start(bf16[32,32,128]{2,1,0:T(8,128)(2,1)S(1)} %get-tuple-element.19), channel_id=1, source_target_pairs={{0,12},{1,13},{2,14},{3,15},{4,0},{5,1},{6,2},{7,3},{8,4},{9,5},{1... | collective-permute-start | bytes 786440 | tf_op jit(solution)/shard_map/ppermute | solution.py:293
  120.1 7.8 %collective-permute-start.15 = (bf16[32,32,128]{2,1,0:T(8,128)(2,1)S(1)}, bf16[32,32,128]{2,1,0:T(8,128)(2,1)S(1)}, u32[]{:S(2)}, u32[]{:S(2)}) collective-permute-start(bf16[32,32,128]{2,1,0:T(8,128)(2,1)S(1)} %get-tuple-element.17), channel_id=1, source_target_pairs={{0,8},{1,9},{2,10},{3,11},{4,12},{5,13},{6,14},{7,15},{8,0},{9,1},... | collective-permute-start | bytes 786440 | tf_op jit(solution)/shard_map/ppermute | solution.py:293
  128.1 4.4 %collective-permute-start.20 = (bf16[8,32,128]{2,1,0:T(8,128)(2,1)S(1)}, bf16[8,32,128]{2,1,0:T(8,128)(2,1)S(1)}, u32[]{:S(2)}, u32[]{:S(2)}) collective-permute-start(bf16[8,32,128]{2,1,0:T(8,128)(2,1)S(1)} %get-tuple-element.27), channel_id=1, source_target_pairs={{0,1},{1,2},{2,3},{3,0},{4,5},{5,6},{6,7},{7,4},{8,9},{9,10},{10,1... | collective-permute-start | bytes 196616 | tf_op jit(solution)/shard_map/ppermute | solution.py:293
  130.8 4.6 %collective-permute-start.18 = (bf16[8,32,128]{2,1,0:T(8,128)(2,1)S(1)}, bf16[8,32,128]{2,1,0:T(8,128)(2,1)S(1)}, u32[]{:S(2)}, u32[]{:S(2)}) collective-permute-start(bf16[8,32,128]{2,1,0:T(8,128)(2,1)S(1)} %get-tuple-element.26), channel_id=1, source_target_pairs={{0,2},{1,3},{2,0},{3,1},{4,6},{5,7},{6,4},{7,5},{8,10},{9,11},{10,... | collective-permute-start | bytes 196616 | tf_op jit(solution)/shard_map/ppermute | solution.py:293
  138.0 5.0 %collective-permute-start.22 = (bf16[8,32,128]{2,1,0:T(8,128)(2,1)S(1)}, bf16[8,32,128]{2,1,0:T(8,128)(2,1)S(1)}, u32[]{:S(2)}, u32[]{:S(2)}) collective-permute-start(bf16[8,32,128]{2,1,0:T(8,128)(2,1)S(1)} %add_convert_fusion.2), channel_id=1, source_target_pairs={{0,32},{16,48},{1,33},{17,49},{2,34},{18,50},{3,35},{19,51},{4,36}... | collective-permute-start | bytes 196616 | tf_op jit(solution)/shard_map/ppermute | solution.py:293
  138.0 5.0 %collective-permute-start.21 = (bf16[8,32,128]{2,1,0:T(8,128)(2,1)S(1)}, bf16[8,32,128]{2,1,0:T(8,128)(2,1)S(1)}, u32[]{:S(2)}, u32[]{:S(2)}) collective-permute-start(bf16[8,32,128]{2,1,0:T(8,128)(2,1)S(1)} %add_convert_fusion.2), channel_id=1, source_target_pairs={{0,64},{16,80},{1,65},{17,81},{2,66},{18,82},{3,67},{19,83},{4,68}... | collective-permute-start | bytes 196616 | tf_op jit(solution)/shard_map/ppermute | solution.py:293
  144.1 4.6 %collective-permute-start.25 = (bf16[8,32,128]{2,1,0:T(8,128)(2,1)S(1)}, bf16[8,32,128]{2,1,0:T(8,128)(2,1)S(1)}, u32[]{:S(2)}, u32[]{:S(2)}) collective-permute-start(bf16[8,32,128]{2,1,0:T(8,128)(2,1)S(1)} %pad_maximum_fusion.3), channel_id=1, source_target_pairs={{0,2},{1,3},{2,0},{3,1},{4,6},{5,7},{6,4},{7,5},{8,10},{9,11},{10,... | collective-permute-start | bytes 196616 | tf_op jit(solution)/shard_map/ppermute | solution.py:293
  145.5 4.3 %collective-permute-start.24 = (bf16[8,32,128]{2,1,0:T(8,128)(2,1)S(1)}, bf16[8,32,128]{2,1,0:T(8,128)(2,1)S(1)}, u32[]{:S(2)}, u32[]{:S(2)}) collective-permute-start(bf16[8,32,128]{2,1,0:T(8,128)(2,1)S(1)} %pad_maximum_fusion.3), channel_id=1, source_target_pairs={{0,1},{1,2},{2,3},{3,0},{4,5},{5,6},{6,7},{7,4},{8,9},{9,10},{10,1... | collective-permute-start | bytes 196616 | tf_op jit(solution)/shard_map/ppermute | solution.py:293
  149.9 9.8 %collective-permute-start.30 = (bf16[32,32,128]{2,1,0:T(8,128)(2,1)S(1)}, bf16[32,32,128]{2,1,0:T(8,128)(2,1)S(1)}, u32[]{:S(2)}, u32[]{:S(2)}) collective-permute-start(bf16[32,32,128]{2,1,0:T(8,128)(2,1)S(1)} %pad_maximum_fusion.1.refs_1_), channel_id=1, source_target_pairs={{0,16},{16,0},{1,17},{17,1},{2,18},{18,2},{3,19},{19,3},{4,20},{20... | collective-permute-start | bytes 786440 | tf_op jit(solution)/shard_map/ppermute | solution.py:293
  156.4 9.6 %collective-permute-start.27 = (bf16[32,32,128]{2,1,0:T(8,128)(2,1)S(1)}, bf16[32,32,128]{2,1,0:T(8,128)(2,1)S(1)}, u32[]{:S(2)}, u32[]{:S(2)}) collective-permute-start(bf16[32,32,128]{2,1,0:T(8,128)(2,1)S(1)} %pad_maximum_fusion.1.refs_1_), channel_id=1, source_target_pairs={{0,4},{1,5},{2,6},{3,7},{4,8},{5,9},{6,10},{7,11},{8,12},{9,13},{1... | collective-permute-start | bytes 786440 | tf_op jit(solution)/shard_map/ppermute | solution.py:293
  156.5 9.5 %collective-permute-start.28 = (bf16[32,32,128]{2,1,0:T(8,128)(2,1)S(1)}, bf16[32,32,128]{2,1,0:T(8,128)(2,1)S(1)}, u32[]{:S(2)}, u32[]{:S(2)}) collective-permute-start(bf16[32,32,128]{2,1,0:T(8,128)(2,1)S(1)} %pad_maximum_fusion.1.refs_1_), channel_id=1, source_target_pairs={{0,8},{1,9},{2,10},{3,11},{4,12},{5,13},{6,14},{7,15},{8,0},{9,1},... | collective-permute-start | bytes 786440 | tf_op jit(solution)/shard_map/ppermute | solution.py:293
  158.0 9.7 %collective-permute-start.29 = (bf16[32,32,128]{2,1,0:T(8,128)(2,1)S(1)}, bf16[32,32,128]{2,1,0:T(8,128)(2,1)S(1)}, u32[]{:S(2)}, u32[]{:S(2)}) collective-permute-start(bf16[32,32,128]{2,1,0:T(8,128)(2,1)S(1)} %pad_maximum_fusion.1.refs_1_), channel_id=1, source_target_pairs={{0,12},{1,13},{2,14},{3,15},{4,0},{5,1},{6,2},{7,3},{8,4},{9,5},{1... | collective-permute-start | bytes 786440 | tf_op jit(solution)/shard_map/ppermute | solution.py:293
  (28 other events, 243.6 us)

commit v2 on v1

--- a/solution.py
+++ b/solution.py
@@ -60,53 +60,102 @@
     return jnp.dot(a, b, preferred_element_type=F32)
 
 
-def index_vectors(orient):
+def half_lanes():
+    return lax.broadcasted_iota(jnp.int32, (8, 128), 1) < 64
+
+
+def turned(groups, turn_a, turn_b):
     lane = lax.broadcasted_iota(jnp.int32, (8, 128), 1)
     sub = lax.broadcasted_iota(jnp.int32, (8, 128), 0)
-    flip_rows = lax.rem(orient, 2) == 1
-    flip_cols = orient >= 2
-    lanes = jnp.where(flip_cols, jnp.where(lane < 64, 63 - lane, 191 - lane), lane)
+    left = half_lanes()
+    flip_cols = jnp.where(left, turn_a, turn_b) >= 2
+    lanes = jnp.where(flip_cols, jnp.where(left, 63, 191) - lane, lane)
+    flip_rows = jnp.where(left, lax.rem(turn_a, 2), lax.rem(turn_b, 2)) == 1
     subs = jnp.where(flip_rows, 7 - sub, sub)
-    return flip_rows, lanes, subs
-
-
-def oriented(groups, orient):
-    flip_rows, lanes, subs = index_vectors(orient)
-    turned = []
-    for g in groups:
-        g = jnp.take_along_axis(g, lanes, axis=1)
-        turned.append(jnp.take_along_axis(g, subs, axis=0))
     return [
-        jnp.where(flip_rows, pltpu.roll(turned[3 - i], 64, 1), turned[i]) for i in range(4)
-    ]
-
-
-def pair_image(cells_ref, loc_a, turn_a, loc_b, turn_b):
-    lane = lax.broadcasted_iota(jnp.int32, (8, 128), 1)
-    a = oriented([cells_ref[loc_a, 8 * i : 8 * i + 8, :] for i in range(4)], turn_a)
-    b = oriented([cells_ref[loc_b, 8 * i : 8 * i + 8, :] for i in range(4)], turn_b)
-    top = [jnp.where(lane < 64, a[i], pltpu.roll(b[i], 64, 1)) for i in range(4)]
-    low = [jnp.where(lane < 64, pltpu.roll(a[i], 64, 1), b[i]) for i in range(4)]
-    return jnp.concatenate(top + low, axis=0)
-
-
-def fill_cells(parts, cells_ref):
+        jnp.take_along_axis(jnp.take_along_axis(g, subs, axis=0), lanes, axis=1) for g in groups
+    ]
+
+
+def places(loc, turn, right):
+    flip = lax.rem(turn, 2)
+    upper = (1 - flip) if right else flip
+    rows = [pl.ds(pl.multiple_of(8 * i + flip * (8 * (3 - 2 * i)), 8), 8) for i in range(4)]
+    return loc + 256 * upper, loc + 256 * (1 - upper), rows
+
+
+def pair_image(cells, loc_a, turn_a, loc_b, turn_b):
+    left = half_lanes()
+    top_a, low_a, rows_a = places(loc_a, turn_a, False)
+    top_b, low_b, rows_b = places(loc_b, turn_b, True)
+    groups = [
+        jnp.where(left, cells[a, rows_a[i], :], cells[b, rows_b[i], :])
+        for a, b in ((top_a, top_b), (low_a, low_b))
+        for i in range(4)
+    ]
+    return jnp.concatenate(turned(groups, turn_a, turn_b), axis=0)
+
+
+def fill_cells(parts, cells):
     for n, part in enumerate(parts):
-        cells_ref[pl.ds(32 * n, 32)] = part[...].astype(F32)
+        value = part[...].astype(F32)
+        cells[pl.ds(32 * n, 32)] = value
+        cells[pl.ds(256 + 32 * n, 32)] = pltpu.roll(value.reshape(1024, 128), 64, 1).reshape(32, 32, 128)
 
 
 def main_kernel(*refs):
     codes, weights = refs[0:2]
     parts = refs[2:10]
-    free, top, bottom, before, after, target, spectra = refs[10:17]
-    (gain, first, second, up_u, up_ut, up_v, up_vt, fine, fine_lo, fine_t, fine_tlo, out_v, out_u) = refs[17:30]
+    near_strip, far_strip, before, after = refs[10:14]
+    free_in, target_in = refs[14:16]
+    table_in = refs[16:30]
     resist_out, free_out, own_out, other_out = refs[30:34]
-    cells, mask, shading, fields, amps, halves, sums = refs[34:41]
+    cells, mask, shading, fields, amps, halves, sums, free, target = refs[34:43]
+    tables = refs[43:57]
+    free_sems, table_sems, target_sem, resist_sems, out_sems = refs[57:62]
+    (spectra, gain, first, second, up_u, up_ut, up_v, up_vt, fine, fine_lo, fine_t, fine_tlo, out_v, out_u) = tables
+
+    loads = [
+        pltpu.make_async_copy(free_in.at[pl.ds(256 * n, 256)], free.at[pl.ds(256 * n, 256)], free_sems.at[n])
+        for n in range(4)
+    ]
+    for load in loads:
+        load.start()
+    table_loads = [pltpu.make_async_copy(a, b, table_sems.at[n]) for n, (a, b) in enumerate(zip(table_in, tables))]
+    for load in table_loads:
+        load.start()
+    target_load = pltpu.make_async_copy(target_in, target, target_sem.at[0])
+    target_load.start()
 
     def code(a, b):
         return codes[a * 18 + b], codes[324 + a * 18 + b]
 
     fill_cells(parts, cells)
+    core = codes[652]
+    for a, flag, own_core in ((0, 648, 1), (17, 649, 0)):
+        for p in range(8):
+            cols = slice(p * 128, p * 128 + 128)
+            image = pair_image(cells, *code(a, 2 * p + 1), *code(a, 2 * p + 2))
+            strip = jnp.where(core == own_core, near_strip[0:64, cols].astype(F32), far_strip[0:64, cols].astype(F32))
+            value = jnp.where(codes[flag] > 0, jnp.tanh(image + strip), 0.0)
+            mask[a * 64 : a * 64 + 64, cols] = value.astype(BF16)
+
+    def edge_cell(a):
+        rows = pl.ds(pl.multiple_of(a * 64, 64), 64)
+        image = pair_image(cells, *code(a, 0), *code(a, 17))
+        strips = jnp.concatenate([before[rows, :], after[rows, :]], axis=1)
+        value = jnp.tanh(image + strips.astype(F32))
+        lane = lax.broadcasted_iota(jnp.int32, (64, 128), 1)
+        at_row = jnp.where(a == 0, codes[648], jnp.where(a == 17, codes[649], 1))
+        keep = jnp.where(lane < 64, codes[650], codes[651]) * at_row
+        mask[rows, 1024:1152] = jnp.where(keep > 0, value, 0.0).astype(BF16)
+
+    def edge_cols(n, _):
+        for u in range(6):
+            edge_cell(n * 6 + u)
+        return 0
+
+    lax.fori_loop(0, 3, edge_cols, 0)
 
     def interior(a, _):
         rows = pl.ds(pl.multiple_of(a * 64, 64), 64)
@@ -119,32 +168,12 @@
             mask[rows_m, cols] = value.astype(BF16)
         return 0
 
-    lax.fori_loop(0, 16, interior, 0)
-
-    for a, strip, flag in ((0, top, 648), (17, bottom, 649)):
-        for p in range(8):
-            cols = slice(p * 128, p * 128 + 128)
-            image = pair_image(cells, *code(a, 2 * p + 1), *code(a, 2 * p + 2))
-            value = jnp.tanh(image + strip[0:64, cols].astype(F32))
-            value = jnp.where(codes[flag] > 0, value, 0.0)
-            mask[a * 64 : a * 64 + 64, cols] = value.astype(BF16)
-
-    def edge_cols(n, _):
-        for u in range(3):
-            edge_cell(n * 3 + u)
-        return 0
-
-    def edge_cell(a):
-        rows = pl.ds(pl.multiple_of(a * 64, 64), 64)
-        image = pair_image(cells, *code(a, 0), *code(a, 17))
-        strips = jnp.concatenate([before[rows, :], after[rows, :]], axis=1)
-        value = jnp.tanh(image + strips.astype(F32))
-        lane = lax.broadcasted_iota(jnp.int32, (64, 128), 1)
-        at_row = jnp.where(a == 0, codes[648], jnp.where(a == 17, codes[649], 1))
-        keep = jnp.where(lane < 64, codes[650], codes[651]) * at_row
-        mask[rows, 1024:1152] = jnp.where(keep > 0, value, 0.0).astype(BF16)
-
-    lax.fori_loop(0, 6, edge_cols, 0)
+    for n in range(4):
+        loads[n].wait()
+        lax.fori_loop(4 * n, 4 * n + 4, interior, 0)
+    for load in table_loads:
+        load.wait()
+    target_load.wait()
 
     def tile(t, _):
         i, j = t // 2, t % 2
@@ -178,8 +207,11 @@
         rows_t = pl.ds(pl.multiple_of(i * TILE, TILE), TILE)
         cols_t = pl.ds(pl.multiple_of(j * TILE, TILE), TILE)
         resist = jax.nn.sigmoid(2.0 * (image - 1.8))
-        resist_out[rows_t, cols_t] = resist
         slopes = (4.0 * (resist - target[rows_t, cols_t]) * resist * (1.0 - resist)).astype(BF16)
+        target[rows_t, cols_t] = resist
+        pltpu.make_async_copy(
+            target.at[rows_t, cols_t], resist_out.at[rows_t, cols_t], resist_sems.at[t]
+        ).start()
         back = dot(fine_t[...], dot(slopes, fine[...]).astype(BF16))
         for k in range(NK):
             at = slice(k * 128, k * 128 + 128)
@@ -206,7 +238,8 @@
         shade = shading[rows_t, cols_t]
         grad = gradient * (1.0 - shade * shade)
         shading[rows_t, cols_t] = grad
-        free_out[rows_t, cols_t] = free[rows_t, cols_t] - grad
+        free[rows_t, cols_t] = free[rows_t, cols_t] - grad
+        pltpu.make_async_copy(free.at[rows_t, cols_t], free_out.at[rows_t, cols_t], out_sems.at[t]).start()
         return 0
 
     lax.fori_loop(0, 4, tile, 0)
@@ -215,30 +248,38 @@
         sums[pl.ds(n * 8, 8)] = jnp.zeros((8, 32, 128), F32)
         return 0
 
-    lax.fori_loop(0, 32, clear, 0)
-    lane = lax.broadcasted_iota(jnp.int32, (8, 128), 1)
+    lax.fori_loop(0, 64, clear, 0)
 
     def collect(a, _):
         rows = pl.multiple_of(a * 64, 64)
-        for batch in range(4):
-            found = []
-            for p in (2 * batch, 2 * batch + 1):
-                cols = slice(p * 128, p * 128 + 128)
-                upper = [shading[pl.ds(rows + 8 * i, 8), cols] for i in range(4)]
-                lower = [shading[pl.ds(rows + 32 + 8 * i, 8), cols] for i in range(4)]
-                left = [jnp.where(lane < 64, upper[i], pltpu.roll(lower[i], 64, 1)) for i in range(4)]
-                right = [jnp.where(lane < 64, pltpu.roll(upper[i], 64, 1), lower[i]) for i in range(4)]
-                for b, groups in ((2 * p + 1, left), (2 * p + 2, right)):
-                    loc, turn = code(a + 1, b)
-                    found.append((loc, oriented(groups, turn)))
-            for loc, out in found:
+        left = half_lanes()
+        for p in range(8):
+            cols = slice(p * 128, p * 128 + 128)
+            loc_a, turn_a = code(a + 1, 2 * p + 1)
+            loc_b, turn_b = code(a + 1, 2 * p + 2)
+            groups = turned([shading[pl.ds(rows + 8 * i, 8), cols] for i in range(8)], turn_a, turn_b)
+            for loc, turn, right, keep in ((loc_a, turn_a, False, left), (loc_b, turn_b, True, ~left)):
+                top, low, at = places(loc, turn, right)
                 for i in range(4):
-                    sums[loc, 8 * i : 8 * i + 8, :] = sums[loc, 8 * i : 8 * i + 8, :] + out[i]
+                    sums[top, at[i], :] = sums[top, at[i], :] + jnp.where(keep, groups[i], 0.0)
+                    sums[low, at[i], :] = sums[low, at[i], :] + jnp.where(keep, groups[4 + i], 0.0)
         return 0
 
     lax.fori_loop(0, 16, collect, 0)
-    own_out[...] = sums[0:128].astype(BF16)
-    other_out[...] = sums[128:256].astype(BF16)
+    for out, base in ((own_out, 0), (other_out, 128)):
+
+        def join(n, _):
+            at = pl.ds(base + n * 8, 8)
+            rolled = pltpu.roll(sums[pl.ds(256 + base + n * 8, 8)].reshape(256, 128), 64, 1)
+            out[pl.ds(n * 8, 8)] = (sums[at].reshape(256, 128) + rolled).reshape(8, 32, 128).astype(BF16)
+            return 0
+
+        lax.fori_loop(0, 16, join, 0)
+
+    for t in range(4):
+        at = (pl.ds(t // 2 * TILE, TILE), pl.ds(t % 2 * TILE, TILE))
+        pltpu.make_async_copy(target.at[at], resist_out.at[at], resist_sems.at[t]).wait()
+        pltpu.make_async_copy(free.at[at], free_out.at[at], out_sems.at[t]).wait()
 
 
 def final_kernel(*refs):
@@ -255,12 +296,12 @@
         rows = pl.ds(pl.multiple_of(r * 64, 64), 64)
         for p in range(8):
             cols = slice(p * 128, p * 128 + 128)
-            at = (step * 4 + r + 1) * 18 + 2 * p
+            at = (step * 2 + r + 1) * 18 + 2 * p
             image = pair_image(cells, codes[at + 1], codes[325 + at], codes[at + 2], codes[326 + at])
             out[rows, cols] = jnp.tanh(image + free[rows, cols])
         return 0
 
-    lax.fori_loop(0, 4, interior, 0)
+    lax.fori_loop(0, 2, interior, 0)
 
 
 def flat(x, c, y, z):
@@ -289,13 +330,21 @@
 SWAP = [(flat(x, c, y, z), flat(x, 1 - c, y, z)) for x, y, z in CHIPS for c in range(2)]
 
 
+OVER = [(flat(x, 0, y, z), flat(x - 1, 1, y, z)) for x, y, z in CHIPS if x > 0] + [
+    (flat(x, 1, y, z), flat(x + 1, 0, y, z)) for x, y, z in CHIPS if x < 3
+]
+
+
 def send(value, pairs):
     return lax.ppermute(value, BOTH, pairs)
 
 
-def gathered(piece):
+def gathered_near(piece):
     got = {d: send(piece, shift_first(d)) for d in (2, 1, 3)}
-    group = jnp.concatenate([piece, got[1], got[2], got[3]], axis=0)
+    return jnp.concatenate([piece, got[1], got[2], got[3]], axis=0)
+
+
+def gathered_far(group):
     far = {d: send(group, shift_second(d)) for d in (2, 1, 3)}
     mine = [group, far[1], far[2], far[3]]
     return mine + [send(part, SWAP) for part in mine]
@@ -336,7 +385,7 @@
     row, col = lax.axis_index("row"), lax.axis_index("col")
     core, y, z = row % 2, col // 4, col % 4
     own_cells = lax.dynamic_slice_in_dim(masters, core * 8, 8, 0)
-    parts = gathered(to_wire(own_cells.astype(BF16)))
+    group = gathered_near(to_wire(own_cells.astype(BF16)))
 
     def codes_of(a):
         return jnp.pad(a.astype(BF16), ((0, 0), (0, SIDE - a.shape[1])))
@@ -345,20 +394,26 @@
         pad = jnp.concatenate([codes_of(inst_master[line : line + 1]), codes_of(inst_orient[line : line + 1])], 0)
         return jnp.concatenate([tile_free[at : at + 64].astype(BF16), jnp.pad(pad, ((0, 14), (0, 0)))], 0)
 
-    up, down = steps("row")
-    above = lax.ppermute(strip(SIDE - 64, 15), "row", up)
-    below = lax.ppermute(strip(0, 0), "row", down)
+    top, bottom = strip(0, 0), strip(SIDE - 64, 15)
+    for_near, for_far = jnp.where(core == 0, bottom, top), jnp.where(core == 0, top, bottom)
+    group, for_near, for_far = lax.optimization_barrier((group, for_near, for_far))
+    parts = gathered_far(group)
+    near_strip, far_strip = send(for_near, SWAP), send(for_far, OVER)
 
     def ints(a):
         return a.astype(F32).astype(jnp.int32)
 
-    tall_master = jnp.concatenate([ints(above[64:65, :16]), inst_master, ints(below[64:65, :16])], 0)
-    tall_orient = jnp.concatenate([ints(above[65:66, :16]), inst_orient, ints(below[65:66, :16])], 0)
+    def above_below(at):
+        near, far = near_strip[at], far_strip[at]
+        return jnp.where(core == 0, far, near), jnp.where(core == 0, near, far)
+
+    above, below = above_below((slice(64, 66), slice(0, 16)))
+    tall_master = jnp.concatenate([ints(above[0:1]), inst_master, ints(below[0:1])], 0)
+    tall_orient = jnp.concatenate([ints(above[1:2]), inst_orient, ints(below[1:2])], 0)
 
     def side(at, line):
-        pixels = jnp.concatenate(
-            [above[:64, at : at + 64], tile_free[:, at : at + 64].astype(BF16), below[:64, at : at + 64]], 0
-        )
+        over, under = above_below((slice(0, 64), slice(at, at + 64)))
+        pixels = jnp.concatenate([over, tile_free[:, at : at + 64].astype(BF16), under], 0)
         lines = jnp.stack([tall_master[:, line], tall_orient[:, line]], 1).astype(BF16)
         return jnp.concatenate([pixels, jnp.pad(lines, ((0, 14), (0, 62)))], 0)
 
@@ -375,44 +430,51 @@
     far, near = jnp.where(half == 0, dy, dz), jnp.where(half == 0, dz, dy)
     locs = (jnp.where(half == core, 0, 1) * 16 + far * 4 + near) * 8 + entry
     inside = jnp.stack([row > 0, row < 7, col > 0, col < 15]).astype(jnp.int32)
-    codes = jnp.concatenate([locs.reshape(-1), all_orient.reshape(-1), inside])
+    codes = jnp.concatenate([locs.reshape(-1), all_orient.reshape(-1), inside, core.reshape(1).astype(jnp.int32)])
 
     vmem, smem = pl.BlockSpec(memory_space=pltpu.VMEM), pl.BlockSpec(memory_space=pltpu.SMEM)
+    anywhere = pl.BlockSpec(memory_space=pl.ANY)
     wide = jax.ShapeDtypeStruct((SIDE, SIDE), F32)
     sums_shape = jax.ShapeDtypeStruct((128, 32, 128), BF16)
+    tables = [spectra.reshape(2, BAND, NK * BAND), *constant_tables()]
     resist, free_new, own, other = pl.pallas_call(
         main_kernel,
         out_shape=(wide, wide, sums_shape, sums_shape),
-        in_specs=[smem] * 2 + [vmem] * 28,
-        out_specs=(vmem,) * 4,
+        in_specs=[smem] * 2 + [vmem] * 12 + [anywhere] * (2 + len(tables)),
+        out_specs=(anywhere, anywhere, vmem, vmem),
         scratch_shapes=[
-            pltpu.VMEM((256, 32, 128), F32),
+            pltpu.VMEM((512, 32, 128), F32),
             pltpu.VMEM((1152, 1152), BF16),
             pltpu.VMEM((SIDE, SIDE), F32),
             pltpu.VMEM((NK, GRID, 2 * GRID), F32),
             pltpu.VMEM((256, 1024), BF16),
             pltpu.VMEM((512, 1024), BF16),
-            pltpu.VMEM((256, 32, 128), F32),
+            pltpu.VMEM((512, 32, 128), F32),
+            pltpu.VMEM((SIDE, SIDE), F32),
+            pltpu.VMEM((SIDE, SIDE), F32),
+            *(pltpu.VMEM(t.shape, t.dtype) for t in tables),
+            pltpu.SemaphoreType.DMA((4,)),
+            pltpu.SemaphoreType.DMA((len(tables),)),
+            pltpu.SemaphoreType.DMA((1,)),
+            pltpu.SemaphoreType.DMA((4,)),
+            pltpu.SemaphoreType.DMA((4,)),
         ],
         compiler_params=pltpu.CompilerParams(vmem_limit_bytes=60 * 1024 * 1024),
         name="image_and_gradient",
-    )(
-        codes, weights, *parts, tile_free, above, below, before, after, target,
-        spectra.reshape(2, BAND, NK * BAND), *constant_tables(),
-    )
+    )(codes, weights, *parts, near_strip, far_strip, before, after, tile_free, target, *tables)
 
     summed = scattered_sum(own, other)
     fresh = smooth(own_cells.reshape(8, CELL, CELL) - 0.05 * from_wire(summed))
     fresh_wire = jnp.concatenate([fresh[:, :32, :], fresh[:, 32:, :]], axis=2).astype(BF16)
-    parts = gathered(fresh_wire)
+    parts = gathered_far(gathered_near(fresh_wire))
     new_mask = pl.pallas_call(
         final_kernel,
         out_shape=wide,
-        grid=(4,),
-        in_specs=[smem] + [vmem] * 8 + [pl.BlockSpec((256, SIDE), lambda s: (s, 0))],
-        out_specs=pl.BlockSpec((256, SIDE), lambda s: (s, 0)),
-        scratch_shapes=[pltpu.VMEM((256, 32, 128), F32)],
-        compiler_params=pltpu.CompilerParams(vmem_limit_bytes=40 * 1024 * 1024),
+        grid=(8,),
+        in_specs=[smem] + [vmem] * 8 + [pl.BlockSpec((128, SIDE), lambda s: (s, 0))],
+        out_specs=pl.BlockSpec((128, SIDE), lambda s: (s, 0)),
+        scratch_shapes=[pltpu.VMEM((512, 32, 128), F32)],
+        compiler_params=pltpu.CompilerParams(vmem_limit_bytes=58 * 1024 * 1024),
         name="final_mask",
     )(codes, *parts, free_new)
     mine = from_wire(parts[0][:8]).reshape(8, CELL * CELL).astype(F32)

time: 182 us -> 156 us (0.86)
  waiting for transfers between devices: 44 us -> 29.3 us
  Pallas kernels: 60.6 us -> 54.4 us
  other arithmetic: 15.4 us -> 10.7 us
  local copies, waits for them, and re-layouts: 9.83 us -> 5.85 us
  starting transfers between devices: 50.7 us -> 54.3 us
    ppermute x30 -> x32, starting transfers between devices: 39.2 us -> 49 us  [send(): return lax.ppermute(value, BOTH, pairs)]
    ppermute x2 -> x0, starting transfers between devices: 7.1 us -> none  [the longest x1 4.1 us: per_device(): below = lax.ppermute(strip(0, 0), 'row', down)]
    ppermute x1, waiting for transfers between devices: 9.91 us -> 4.07 us  [per_device(): after = lax.ppermute(side(0, 0), 'col', down)]
    pallas_call x1, Pallas kernels: 50.5 us -> 44.8 us  [per_device(): pl.pallas_call(main_kernel, out_shape=(wide, wide, sums_shape, sums_shape...]
    ppermute x1, waiting for transfers between devices: 5.52 us -> 0.01 us  [per_device(): before = lax.ppermute(side(SIDE - 64, 15), 'col', up)]
    ppermute x30 -> x32, waiting for transfers between devices: 28.6 us -> 25.2 us  [send(): return lax.ppermute(value, BOTH, pairs)]
    concatenate x5 -> x3, other arithmetic: 3.12 us -> 0.86 us  [the longest x1 0.67 us: per_device(): jnp.concatenate([locs.reshape(-1), all_orient.reshape(-1), inside, core.r...]
    unnamed x38 -> x50, local copies, waits for them, and re-layouts: 4.06 us -> 2.41 us
  transfers between devices with their start and end apart: 34 -> 34, of which waited for: 17 -> 16; matrix products, arithmetic and copies ran while one was open for 9% -> 7% of each run, Pallas kernels for 0% -> 0%
where the time goes in v2:
time: 156 us
  Pallas kernels  54.4 us (35%)
  starting transfers between devices  54.3 us (35%)
  waiting for transfers between devices  29.3 us (19%)
  other arithmetic  10.7 us (7%)
  local copies, waits for them, and re-layouts  5.85 us (4%)
    ppermute x32, starting transfers between devices, send(): return lax.ppermute(value, BOTH, pairs)  49 us
    pallas_call x1, Pallas kernels, per_device(): pl.pallas_call(main_kernel, out_shape=(wide, wide, sums_shape, sums_shape...  44.8 us
    ppermute x32, waiting for transfers between devices, send(): return lax.ppermute(value, BOTH, pairs)  25.2 us
    pallas_call x1, Pallas kernels, per_device(): pl.pallas_call(final_kernel, out_shape=wide, grid=(8,), in_specs=[smem] +...  9.53 us
    another operation x4, other arithmetic  4.12 us
    ppermute x1, waiting for transfers between devices, per_device(): after = lax.ppermute(side(0, 0), 'col', down)  4.07 us
    ppermute x1, starting transfers between devices, per_device(): before = lax.ppermute(side(SIDE - 64, 15), 'col', up)  3.93 us
  transfers between devices with their start and end apart: 34, of which 16 were waited for; matrix products, arithmetic and copies ran while one was open for 7% of the time, Pallas kernels for 0%

profile of v2, /device:TPU:1, one launch (start us, length us, event | category | flops | bytes accessed | tf_op | source)
XLA Modules:
  0.0 155.5 jit_solution(17612095993127543668)
XLA Ops:
  1.9 3.6 %collective-permute-start.2 = (bf16[8,32,128]{2,1,0:T(8,128)(2,1)S(1)}, bf16[8,32,128]{2,1,0:T(8,128)(2,1)S(1)}, u32[]{:S(2)}, u32[]{:S(2)}) collective-permute-start(bf16[8,32,128]{2,1,0:T(8,128)(2,1)S(1)} %pad_maximum_fusion.2), channel_id=1, source_target_pairs={{0,3},{1,0},{2,1},{3,2},{4,7},{5,4},{6,5},{7,6},{8,11},{9,8},{10,9... | collective-permute-start | bytes 196616 | tf_op jit(solution)/shard_map/ppermute | solution.py:339
  8.0 2.5 %convert.34 = bf16[1024,1024]{1,0:T(8,128)(2,1)S(1)} convert(f32[1024,1024]{1,0:T(8,128)} %refs_14_.1) | non-fusion elementwise | flops 1048576 | bytes 6291456 | tf_op jit(solution)/shard_map/convert.21
  11.4 2.4 %collective-permute-start.4 = (bf16[80,1024]{1,0:T(8,128)(2,1)S(1)}, bf16[80,1024]{1,0:T(8,128)(2,1)S(1)}, u32[]{:S(2)}, u32[]{:S(2)}) collective-permute-start(bf16[80,1024]{1,0:T(8,128)(2,1)S(1)} %get-tuple-element.11), channel_id=1, source_target_pairs={{0,16},{16,0},{1,17},{17,1},{2,18},{18,2},{3,19},{19,3},{4,20},{20... | collective-permute-start | bytes 491528 | tf_op jit(solution)/shard_map/ppermute | solution.py:339
  13.9 3.0 %collective-permute-start.3 = (bf16[80,1024]{1,0:T(8,128)(2,1)}, bf16[80,1024]{1,0:T(8,128)(2,1)S(1)}, u32[]{:S(2)}, u32[]{:S(2)}) collective-permute-start(bf16[80,1024]{1,0:T(8,128)(2,1)} %get-tuple-element.10), channel_id=1, source_target_pairs={{32,16},{33,17},{34,18},{35,19},{36,20},{37,21},{38,22},{39,23},{4... | collective-permute-start | bytes 491528 | tf_op jit(solution)/shard_map/ppermute | solution.py:339
  18.4 1.8 %collective-permute-start.7 = (bf16[32,32,128]{2,1,0:T(8,128)(2,1)S(1)}, bf16[32,32,128]{2,1,0:T(8,128)(2,1)S(1)}, u32[]{:S(2)}, u32[]{:S(2)}) collective-permute-start(bf16[32,32,128]{2,1,0:T(8,128)(2,1)S(1)} %pad_maximum_fusion.refs_2_), channel_id=1, source_target_pairs={{0,4},{1,5},{2,6},{3,7},{4,8},{5,9},{6,10},{7,11},{8,12},{9,13},{1... | collective-permute-start | bytes 786440 | tf_op jit(solution)/shard_map/ppermute | solution.py:339
  25.2 3.9 %collective-permute-start.5 = (bf16[1184,64]{1,0:T(8,128)(2,1)S(1)}, bf16[1184,64]{1,0:T(8,128)(2,1)S(1)}, u32[]{:S(2)}, u32[]{:S(2)}) collective-permute-start(bf16[1184,64]{1,0:T(8,128)(2,1)S(1)} %fusion.4), channel_id=1, source_target_pairs={{0,1},{1,2},{2,3},{3,4},{4,5},{5,6},{6,7},{7,8},{8,9},{9,10},{10,1... | collective-permute-start | bytes 454664 | tf_op jit(solution)/shard_map/ppermute | solution.py:421
  30.4 4.1 %collective-permute-done.6.refs_13_ = bf16[1184,64]{1,0:T(8,128)(2,1)S(1)} collective-permute-done((bf16[1184,64]{1,0:T(8,128)(2,1)S(1)}, bf16[1184,64]{1,0:T(8,128)(2,1)S(1)}, u32[]{:S(2)}, u32[]{:S(2)}) %collective-permute-start.6) | collective-permute-done | bytes 151584 | tf_op jit(solution)/shard_map/ppermute | solution.py:422
  39.3 44.8 %image_and_gradient.1 = (f32[1024,1024]{1,0:T(8,128)}, f32[1024,1024]{1,0:T(8,128)}, bf16[128,32,128]{2,1,0:T(8,128)(2,1)}, bf16[128,32,128]{2,1,0:T(8,128)(2,1)}) custom-call(s32[653]{0:T(1024)} %pad_add_fusion.2.refs_0_, f32[8]{0:T(128)} %refs_1_.1, bf16[32,32,128]{2,1,0:T(8,128)(2,1)} %copy-done, bf16[32,32,128]{2,1,0:T(8,128)(2,1)} %copy-done.6, ...), custom_call_target="tpu_custom_call" | custom-call | tf_op jit(solution)/shard_map/image_and_gradient/pallas_call | solution.py:440
  85.1 2.5 %collective-permute-done.14 = bf16[128,32,128]{2,1,0:T(8,128)(2,1)S(1)} collective-permute-done((bf16[128,32,128]{2,1,0:T(8,128)(2,1)}, bf16[128,32,128]{2,1,0:T(8,128)(2,1)S(1)}, u32[]{:S(2)}, u32[]{:S(2)}) %collective-permute-start.14) | collective-permute-done | bytes 1048608 | tf_op jit(solution)/shard_map/ppermute | solution.py:339
  89.2 2.3 %collective-permute-start.17 = (bf16[32,32,128]{2,1,0:T(8,128)(2,1)S(1)}, bf16[32,32,128]{2,1,0:T(8,128)(2,1)S(1)}, u32[]{:S(2)}, u32[]{:S(2)}) collective-permute-start(bf16[32,32,128]{2,1,0:T(8,128)(2,1)S(1)} %get-tuple-element.24), channel_id=1, source_target_pairs={{0,4},{1,5},{2,6},{3,7},{4,8},{5,9},{6,10},{7,11},{8,12},{9,13},{1... | collective-permute-start | bytes 786440 | tf_op jit(solution)/shard_map/ppermute | solution.py:339
  92.2 2.0 %collective-permute-start.15 = (bf16[32,32,128]{2,1,0:T(8,128)(2,1)S(1)}, bf16[32,32,128]{2,1,0:T(8,128)(2,1)S(1)}, u32[]{:S(2)}, u32[]{:S(2)}) collective-permute-start(bf16[32,32,128]{2,1,0:T(8,128)(2,1)S(1)} %get-tuple-element.23), channel_id=1, source_target_pairs={{0,8},{1,9},{2,10},{3,11},{4,12},{5,13},{6,14},{7,15},{8,0},{9,1},... | collective-permute-start | bytes 786440 | tf_op jit(solution)/shard_map/ppermute | solution.py:339
  96.7 3.2 %collective-permute-done.15 = bf16[32,32,128]{2,1,0:T(8,128)(2,1)S(1)} collective-permute-done((bf16[32,32,128]{2,1,0:T(8,128)(2,1)S(1)}, bf16[32,32,128]{2,1,0:T(8,128)(2,1)S(1)}, u32[]{:S(2)}, u32[]{:S(2)}) %collective-permute-start.15) | collective-permute-done | bytes 262176 | tf_op jit(solution)/shard_map/ppermute | solution.py:339
  100.0 3.6 %collective-permute-start.20 = (bf16[8,32,128]{2,1,0:T(8,128)(2,1)S(1)}, bf16[8,32,128]{2,1,0:T(8,128)(2,1)S(1)}, u32[]{:S(2)}, u32[]{:S(2)}) collective-permute-start(bf16[8,32,128]{2,1,0:T(8,128)(2,1)S(1)} %get-tuple-element.41), channel_id=1, source_target_pairs={{0,1},{1,2},{2,3},{3,0},{4,5},{5,6},{6,7},{7,4},{8,9},{9,10},{10,1... | collective-permute-start | bytes 196616 | tf_op jit(solution)/shard_map/ppermute | solution.py:339
  103.7 2.1 %collective-permute-start.19 = (bf16[8,32,128]{2,1,0:T(8,128)(2,1)S(1)}, bf16[8,32,128]{2,1,0:T(8,128)(2,1)S(1)}, u32[]{:S(2)}, u32[]{:S(2)}) collective-permute-start(bf16[8,32,128]{2,1,0:T(8,128)(2,1)S(1)} %get-tuple-element.42), channel_id=1, source_target_pairs={{0,3},{1,0},{2,1},{3,2},{4,7},{5,4},{6,5},{7,6},{8,11},{9,8},{10,9... | collective-permute-start | bytes 196616 | tf_op jit(solution)/shard_map/ppermute | solution.py:339
  107.4 3.0 %collective-permute-done.18 = bf16[8,32,128]{2,1,0:T(8,128)(2,1)S(1)} collective-permute-done((bf16[8,32,128]{2,1,0:T(8,128)(2,1)S(1)}, bf16[8,32,128]{2,1,0:T(8,128)(2,1)S(1)}, u32[]{:S(2)}, u32[]{:S(2)}) %collective-permute-start.18) | collective-permute-done | bytes 65568 | tf_op jit(solution)/shard_map/ppermute | solution.py:339
  110.5 2.6 %collective-permute-start.23 = (bf16[8,32,128]{2,1,0:T(8,128)(2,1)S(1)}, bf16[8,32,128]{2,1,0:T(8,128)(2,1)S(1)}, u32[]{:S(2)}, u32[]{:S(2)}) collective-permute-start(bf16[8,32,128]{2,1,0:T(8,128)(2,1)S(1)} %add_convert_fusion.2), channel_id=1, source_target_pairs={{0,96},{16,112},{1,97},{17,113},{2,98},{18,114},{3,99},{19,115},{4... | collective-permute-start | bytes 196616 | tf_op jit(solution)/shard_map/ppermute | solution.py:339
  114.6 3.5 %collective-permute-done.22 = bf16[8,32,128]{2,1,0:T(8,128)(2,1)S(1)} collective-permute-done((bf16[8,32,128]{2,1,0:T(8,128)(2,1)S(1)}, bf16[8,32,128]{2,1,0:T(8,128)(2,1)S(1)}, u32[]{:S(2)}, u32[]{:S(2)}) %collective-permute-start.22) | collective-permute-done | bytes 65568 | tf_op jit(solution)/shard_map/ppermute | solution.py:339
  118.6 1.9 %collective-permute-start.26 = (bf16[8,32,128]{2,1,0:T(8,128)(2,1)S(1)}, bf16[8,32,128]{2,1,0:T(8,128)(2,1)S(1)}, u32[]{:S(2)}, u32[]{:S(2)}) collective-permute-start(bf16[8,32,128]{2,1,0:T(8,128)(2,1)S(1)} %pad_maximum_fusion.3), channel_id=1, source_target_pairs={{0,3},{1,0},{2,1},{3,2},{4,7},{5,4},{6,5},{7,6},{8,11},{9,8},{10,9... | collective-permute-start | bytes 196616 | tf_op jit(solution)/shard_map/ppermute | solution.py:339
  122.3 2.8 %collective-permute-done.25 = bf16[8,32,128]{2,1,0:T(8,128)(2,1)S(1)} collective-permute-done((bf16[8,32,128]{2,1,0:T(8,128)(2,1)S(1)}, bf16[8,32,128]{2,1,0:T(8,128)(2,1)S(1)}, u32[]{:S(2)}, u32[]{:S(2)}) %collective-permute-start.25) | collective-permute-done | bytes 65568 | tf_op jit(solution)/shard_map/ppermute | solution.py:339
  126.6 4.4 %collective-permute-start.30 = (bf16[32,32,128]{2,1,0:T(8,128)(2,1)S(1)}, bf16[32,32,128]{2,1,0:T(8,128)(2,1)S(1)}, u32[]{:S(2)}, u32[]{:S(2)}) collective-permute-start(bf16[32,32,128]{2,1,0:T(8,128)(2,1)S(1)} %pad_maximum_fusion.1.refs_1_), channel_id=1, source_target_pairs={{0,16},{16,0},{1,17},{17,1},{2,18},{18,2},{3,19},{19,3},{4,20},{20... | collective-permute-start | bytes 786440 | tf_op jit(solution)/shard_map/ppermute | solution.py:339
  131.7 2.3 %collective-permute-start.28 = (bf16[32,32,128]{2,1,0:T(8,128)(2,1)S(1)}, bf16[32,32,128]{2,1,0:T(8,128)(2,1)S(1)}, u32[]{:S(2)}, u32[]{:S(2)}) collective-permute-start(bf16[32,32,128]{2,1,0:T(8,128)(2,1)S(1)} %pad_maximum_fusion.1.refs_1_), channel_id=1, source_target_pairs={{0,8},{1,9},{2,10},{3,11},{4,12},{5,13},{6,14},{7,15},{8,0},{9,1},... | collective-permute-start | bytes 786440 | tf_op jit(solution)/shard_map/ppermute | solution.py:339
  134.5 3.4 %collective-permute-done.27.refs_2_ = bf16[32,32,128]{2,1,0:T(8,128)(2,1)S(1)} collective-permute-done((bf16[32,32,128]{2,1,0:T(8,128)(2,1)S(1)}, bf16[32,32,128]{2,1,0:T(8,128)(2,1)S(1)}, u32[]{:S(2)}, u32[]{:S(2)}) %collective-permute-start.27) | collective-permute-done | bytes 262176 | tf_op jit(solution)/shard_map/ppermute | solution.py:339
  140.9 2.8 %collective-permute-start.32 = (bf16[32,32,128]{2,1,0:T(8,128)(2,1)S(1)}, bf16[32,32,128]{2,1,0:T(8,128)(2,1)S(1)}, u32[]{:S(2)}, u32[]{:S(2)}) collective-permute-start(bf16[32,32,128]{2,1,0:T(8,128)(2,1)S(1)} %collective-permute-done.28.refs_3_), channel_id=1, source_target_pairs={{0,16},{16,0},{1,17},{17,1},{2,18},{18,2},{3,19},{19,3},{4,20},{20... | collective-permute-start | bytes 786440 | tf_op jit(solution)/shard_map/ppermute | solution.py:339
  146.0 9.5 %final_mask.1 = f32[1024,1024]{1,0:T(8,128)} custom-call(s32[653]{0:T(1024)} %pad_add_fusion.2.refs_0_, bf16[32,32,128]{2,1,0:T(8,128)(2,1)} %copy-done.1, bf16[32,32,128]{2,1,0:T(8,128)(2,1)} %copy-done.13, bf16[32,32,128]{2,1,0:T(8,128)(2,1)} %copy-done.14, bf16[32,32,128]{2,1,0:T(8,128)(2,1)} %copy-done.15, bf16[32,32,128]{2,1,0:T(8,128)(2,1)} %copy-done.3, ...), custom_call_target="tpu_custom_call" | custom-call | tf_op jit(solution)/shard_map/final_mask/pallas_call | solution.py:470
  (161 shorter events, 36.2 us)
Async XLA Ops:
  1.9 9.4 %collective-permute-start.2 = (bf16[8,32,128]{2,1,0:T(8,128)(2,1)S(1)}, bf16[8,32,128]{2,1,0:T(8,128)(2,1)S(1)}, u32[]{:S(2)}, u32[]{:S(2)}) collective-permute-start(bf16[8,32,128]{2,1,0:T(8,128)(2,1)S(1)} %pad_maximum_fusion.2), channel_id=1, source_target_pairs={{0,3},{1,0},{2,1},{3,2},{4,7},{5,4},{6,5},{7,6},{8,11},{9,8},{10,9... | collective-permute-start | bytes 196616 | tf_op jit(solution)/shard_map/ppermute | solution.py:339
  5.5 5.8 %collective-permute-start.1 = (bf16[8,32,128]{2,1,0:T(8,128)(2,1)S(1)}, bf16[8,32,128]{2,1,0:T(8,128)(2,1)S(1)}, u32[]{:S(2)}, u32[]{:S(2)}) collective-permute-start(bf16[8,32,128]{2,1,0:T(8,128)(2,1)S(1)} %pad_maximum_fusion.2), channel_id=1, source_target_pairs={{0,2},{1,3},{2,0},{3,1},{4,6},{5,7},{6,4},{7,5},{8,10},{9,11},{10,... | collective-permute-start | bytes 196616 | tf_op jit(solution)/shard_map/ppermute | solution.py:339
  5.9 5.4 %collective-permute-start = (bf16[8,32,128]{2,1,0:T(8,128)(2,1)S(1)}, bf16[8,32,128]{2,1,0:T(8,128)(2,1)S(1)}, u32[]{:S(2)}, u32[]{:S(2)}) collective-permute-start(bf16[8,32,128]{2,1,0:T(8,128)(2,1)S(1)} %pad_maximum_fusion.2), channel_id=1, source_target_pairs={{0,1},{1,2},{2,3},{3,0},{4,5},{5,6},{6,7},{7,4},{8,9},{9,10},{10,1... | collective-permute-start | bytes 196616 | tf_op jit(solution)/shard_map/ppermute | solution.py:339
  11.4 11.3 %collective-permute-start.4 = (bf16[80,1024]{1,0:T(8,128)(2,1)S(1)}, bf16[80,1024]{1,0:T(8,128)(2,1)S(1)}, u32[]{:S(2)}, u32[]{:S(2)}) collective-permute-start(bf16[80,1024]{1,0:T(8,128)(2,1)S(1)} %get-tuple-element.11), channel_id=1, source_target_pairs={{0,16},{16,0},{1,17},{17,1},{2,18},{18,2},{3,19},{19,3},{4,20},{20... | collective-permute-start | bytes 491528 | tf_op jit(solution)/shard_map/ppermute | solution.py:339
  13.9 8.9 %collective-permute-start.3 = (bf16[80,1024]{1,0:T(8,128)(2,1)}, bf16[80,1024]{1,0:T(8,128)(2,1)S(1)}, u32[]{:S(2)}, u32[]{:S(2)}) collective-permute-start(bf16[80,1024]{1,0:T(8,128)(2,1)} %get-tuple-element.10), channel_id=1, source_target_pairs={{32,16},{33,17},{34,18},{35,19},{36,20},{37,21},{38,22},{39,23},{4... | collective-permute-start | bytes 491528 | tf_op jit(solution)/shard_map/ppermute | solution.py:339
  18.4 6.7 %collective-permute-start.7 = (bf16[32,32,128]{2,1,0:T(8,128)(2,1)S(1)}, bf16[32,32,128]{2,1,0:T(8,128)(2,1)S(1)}, u32[]{:S(2)}, u32[]{:S(2)}) collective-permute-start(bf16[32,32,128]{2,1,0:T(8,128)(2,1)S(1)} %pad_maximum_fusion.refs_2_), channel_id=1, source_target_pairs={{0,4},{1,5},{2,6},{3,7},{4,8},{5,9},{6,10},{7,11},{8,12},{9,13},{1... | collective-permute-start | bytes 786440 | tf_op jit(solution)/shard_map/ppermute | solution.py:339
  20.2 8.9 %collective-permute-start.8 = (bf16[32,32,128]{2,1,0:T(8,128)(2,1)S(1)}, bf16[32,32,128]{2,1,0:T(8,128)(2,1)S(1)}, u32[]{:S(2)}, u32[]{:S(2)}) collective-permute-start(bf16[32,32,128]{2,1,0:T(8,128)(2,1)S(1)} %pad_maximum_fusion.refs_2_), channel_id=1, source_target_pairs={{0,8},{1,9},{2,10},{3,11},{4,12},{5,13},{6,14},{7,15},{8,0},{9,1},... | collective-permute-start | bytes 786440 | tf_op jit(solution)/shard_map/ppermute | solution.py:339
  21.5 8.8 %collective-permute-start.9 = (bf16[32,32,128]{2,1,0:T(8,128)(2,1)S(1)}, bf16[32,32,128]{2,1,0:T(8,128)(2,1)S(1)}, u32[]{:S(2)}, u32[]{:S(2)}) collective-permute-start(bf16[32,32,128]{2,1,0:T(8,128)(2,1)S(1)} %pad_maximum_fusion.refs_2_), channel_id=1, source_target_pairs={{0,12},{1,13},{2,14},{3,15},{4,0},{5,1},{6,2},{7,3},{8,4},{9,5},{1... | collective-permute-start | bytes 786440 | tf_op jit(solution)/shard_map/ppermute | solution.py:339
  22.7 15.0 %collective-permute-start.10 = (bf16[32,32,128]{2,1,0:T(8,128)(2,1)S(1)}, bf16[32,32,128]{2,1,0:T(8,128)(2,1)S(1)}, u32[]{:S(2)}, u32[]{:S(2)}) collective-permute-start(bf16[32,32,128]{2,1,0:T(8,128)(2,1)S(1)} %pad_maximum_fusion.refs_2_), channel_id=1, source_target_pairs={{0,16},{16,0},{1,17},{17,1},{2,18},{18,2},{3,19},{19,3},{4,20},{20... | collective-permute-start | bytes 786440 | tf_op jit(solution)/shard_map/ppermute | solution.py:339
  23.6 10.9 %collective-permute-start.6 = (bf16[1184,64]{1,0:T(8,128)(2,1)S(1)}, bf16[1184,64]{1,0:T(8,128)(2,1)S(1)}, u32[]{:S(2)}, u32[]{:S(2)}) collective-permute-start(bf16[1184,64]{1,0:T(8,128)(2,1)S(1)} %fusion.5), channel_id=1, source_target_pairs={{1,0},{2,1},{3,2},{4,3},{5,4},{6,5},{7,6},{8,7},{9,8},{10,9},{11,1... | collective-permute-start | bytes 454664 | tf_op jit(solution)/shard_map/ppermute | solution.py:422
  25.2 10.5 %collective-permute-start.5 = (bf16[1184,64]{1,0:T(8,128)(2,1)S(1)}, bf16[1184,64]{1,0:T(8,128)(2,1)S(1)}, u32[]{:S(2)}, u32[]{:S(2)}) collective-permute-start(bf16[1184,64]{1,0:T(8,128)(2,1)S(1)} %fusion.4), channel_id=1, source_target_pairs={{0,1},{1,2},{2,3},{3,4},{4,5},{5,6},{6,7},{7,8},{8,9},{9,10},{10,1... | collective-permute-start | bytes 454664 | tf_op jit(solution)/shard_map/ppermute | solution.py:421
  29.1 8.6 %collective-permute-start.11 = (bf16[32,32,128]{2,1,0:T(8,128)(2,1)S(1)}, bf16[32,32,128]{2,1,0:T(8,128)(2,1)S(1)}, u32[]{:S(2)}, u32[]{:S(2)}) collective-permute-start(bf16[32,32,128]{2,1,0:T(8,128)(2,1)S(1)} %collective-permute-done.7.refs_3_), channel_id=1, source_target_pairs={{0,16},{16,0},{1,17},{17,1},{2,18},{18,2},{3,19},{19,3},{4,20},{20... | collective-permute-start | bytes 786440 | tf_op jit(solution)/shard_map/ppermute | solution.py:339
  30.3 7.5 %collective-permute-start.12 = (bf16[32,32,128]{2,1,0:T(8,128)(2,1)S(1)}, bf16[32,32,128]{2,1,0:T(8,128)(2,1)S(1)}, u32[]{:S(2)}, u32[]{:S(2)}) collective-permute-start(bf16[32,32,128]{2,1,0:T(8,128)(2,1)S(1)} %collective-permute-done.8.refs_4_), channel_id=1, source_target_pairs={{0,16},{16,0},{1,17},{17,1},{2,18},{18,2},{3,19},{19,3},{4,20},{20... | collective-permute-start | bytes 786440 | tf_op jit(solution)/shard_map/ppermute | solution.py:339
  89.2 6.7 %collective-permute-start.17 = (bf16[32,32,128]{2,1,0:T(8,128)(2,1)S(1)}, bf16[32,32,128]{2,1,0:T(8,128)(2,1)S(1)}, u32[]{:S(2)}, u32[]{:S(2)}) collective-permute-start(bf16[32,32,128]{2,1,0:T(8,128)(2,1)S(1)} %get-tuple-element.24), channel_id=1, source_target_pairs={{0,4},{1,5},{2,6},{3,7},{4,8},{5,9},{6,10},{7,11},{8,12},{9,13},{1... | collective-permute-start | bytes 786440 | tf_op jit(solution)/shard_map/ppermute | solution.py:339
  91.4 5.2 %collective-permute-start.16 = (bf16[32,32,128]{2,1,0:T(8,128)(2,1)S(1)}, bf16[32,32,128]{2,1,0:T(8,128)(2,1)S(1)}, u32[]{:S(2)}, u32[]{:S(2)}) collective-permute-start(bf16[32,32,128]{2,1,0:T(8,128)(2,1)S(1)} %get-tuple-element.25), channel_id=1, source_target_pairs={{0,12},{1,13},{2,14},{3,15},{4,0},{5,1},{6,2},{7,3},{8,4},{9,5},{1... | collective-permute-start | bytes 786440 | tf_op jit(solution)/shard_map/ppermute | solution.py:339
  92.2 7.7 %collective-permute-start.15 = (bf16[32,32,128]{2,1,0:T(8,128)(2,1)S(1)}, bf16[32,32,128]{2,1,0:T(8,128)(2,1)S(1)}, u32[]{:S(2)}, u32[]{:S(2)}) collective-permute-start(bf16[32,32,128]{2,1,0:T(8,128)(2,1)S(1)} %get-tuple-element.23), channel_id=1, source_target_pairs={{0,8},{1,9},{2,10},{3,11},{4,12},{5,13},{6,14},{7,15},{8,0},{9,1},... | collective-permute-start | bytes 786440 | tf_op jit(solution)/shard_map/ppermute | solution.py:339
  100.0 7.3 %collective-permute-start.20 = (bf16[8,32,128]{2,1,0:T(8,128)(2,1)S(1)}, bf16[8,32,128]{2,1,0:T(8,128)(2,1)S(1)}, u32[]{:S(2)}, u32[]{:S(2)}) collective-permute-start(bf16[8,32,128]{2,1,0:T(8,128)(2,1)S(1)} %get-tuple-element.41), channel_id=1, source_target_pairs={{0,1},{1,2},{2,3},{3,0},{4,5},{5,6},{6,7},{7,4},{8,9},{9,10},{10,1... | collective-permute-start | bytes 196616 | tf_op jit(solution)/shard_map/ppermute | solution.py:339
  113.0 5.0 %collective-permute-start.22 = (bf16[8,32,128]{2,1,0:T(8,128)(2,1)S(1)}, bf16[8,32,128]{2,1,0:T(8,128)(2,1)S(1)}, u32[]{:S(2)}, u32[]{:S(2)}) collective-permute-start(bf16[8,32,128]{2,1,0:T(8,128)(2,1)S(1)} %add_convert_fusion.2), channel_id=1, source_target_pairs={{0,32},{16,48},{1,33},{17,49},{2,34},{18,50},{3,35},{19,51},{4,36}... | collective-permute-start | bytes 196616 | tf_op jit(solution)/shard_map/ppermute | solution.py:339
  113.0 5.0 %collective-permute-start.21 = (bf16[8,32,128]{2,1,0:T(8,128)(2,1)S(1)}, bf16[8,32,128]{2,1,0:T(8,128)(2,1)S(1)}, u32[]{:S(2)}, u32[]{:S(2)}) collective-permute-start(bf16[8,32,128]{2,1,0:T(8,128)(2,1)S(1)} %add_convert_fusion.2), channel_id=1, source_target_pairs={{0,64},{16,80},{1,65},{17,81},{2,66},{18,82},{3,67},{19,83},{4,68}... | collective-permute-start | bytes 196616 | tf_op jit(solution)/shard_map/ppermute | solution.py:339
  126.6 7.7 %collective-permute-start.30 = (bf16[32,32,128]{2,1,0:T(8,128)(2,1)S(1)}, bf16[32,32,128]{2,1,0:T(8,128)(2,1)S(1)}, u32[]{:S(2)}, u32[]{:S(2)}) collective-permute-start(bf16[32,32,128]{2,1,0:T(8,128)(2,1)S(1)} %pad_maximum_fusion.1.refs_1_), channel_id=1, source_target_pairs={{0,16},{16,0},{1,17},{17,1},{2,18},{18,2},{3,19},{19,3},{4,20},{20... | collective-permute-start | bytes 786440 | tf_op jit(solution)/shard_map/ppermute | solution.py:339
  131.1 6.8 %collective-permute-start.27 = (bf16[32,32,128]{2,1,0:T(8,128)(2,1)S(1)}, bf16[32,32,128]{2,1,0:T(8,128)(2,1)S(1)}, u32[]{:S(2)}, u32[]{:S(2)}) collective-permute-start(bf16[32,32,128]{2,1,0:T(8,128)(2,1)S(1)} %pad_maximum_fusion.1.refs_1_), channel_id=1, source_target_pairs={{0,4},{1,5},{2,6},{3,7},{4,8},{5,9},{6,10},{7,11},{8,12},{9,13},{1... | collective-permute-start | bytes 786440 | tf_op jit(solution)/shard_map/ppermute | solution.py:339
  131.7 9.2 %collective-permute-start.28 = (bf16[32,32,128]{2,1,0:T(8,128)(2,1)S(1)}, bf16[32,32,128]{2,1,0:T(8,128)(2,1)S(1)}, u32[]{:S(2)}, u32[]{:S(2)}) collective-permute-start(bf16[32,32,128]{2,1,0:T(8,128)(2,1)S(1)} %pad_maximum_fusion.1.refs_1_), channel_id=1, source_target_pairs={{0,8},{1,9},{2,10},{3,11},{4,12},{5,13},{6,14},{7,15},{8,0},{9,1},... | collective-permute-start | bytes 786440 | tf_op jit(solution)/shard_map/ppermute | solution.py:339
  134.1 9.7 %collective-permute-start.29 = (bf16[32,32,128]{2,1,0:T(8,128)(2,1)S(1)}, bf16[32,32,128]{2,1,0:T(8,128)(2,1)S(1)}, u32[]{:S(2)}, u32[]{:S(2)}) collective-permute-start(bf16[32,32,128]{2,1,0:T(8,128)(2,1)S(1)} %pad_maximum_fusion.1.refs_1_), channel_id=1, source_target_pairs={{0,12},{1,13},{2,14},{3,15},{4,0},{5,1},{6,2},{7,3},{8,4},{9,5},{1... | collective-permute-start | bytes 786440 | tf_op jit(solution)/shard_map/ppermute | solution.py:339
  137.9 6.7 %collective-permute-start.31 = (bf16[32,32,128]{2,1,0:T(8,128)(2,1)S(1)}, bf16[32,32,128]{2,1,0:T(8,128)(2,1)S(1)}, u32[]{:S(2)}, u32[]{:S(2)}) collective-permute-start(bf16[32,32,128]{2,1,0:T(8,128)(2,1)S(1)} %collective-permute-done.27.refs_2_), channel_id=1, source_target_pairs={{0,16},{16,0},{1,17},{17,1},{2,18},{18,2},{3,19},{19,3},{4,20},{20... | collective-permute-start | bytes 786440 | tf_op jit(solution)/shard_map/ppermute | solution.py:339
  (34 other events, 190.6 us)

commit v3 on v2

--- a/solution.py
+++ b/solution.py
@@ -96,8 +96,9 @@
     return jnp.concatenate(turned(groups, turn_a, turn_b), axis=0)
 
 
-def fill_cells(parts, cells):
+def fill_cells(parts, cells, loads):
     for n, part in enumerate(parts):
+        loads[n].wait()
         value = part[...].astype(F32)
         cells[pl.ds(32 * n, 32)] = value
         cells[pl.ds(256 + 32 * n, 32)] = pltpu.roll(value.reshape(1024, 128), 64, 1).reshape(32, 32, 128)
@@ -105,16 +106,20 @@
 
 def main_kernel(*refs):
     codes, weights = refs[0:2]
-    parts = refs[2:10]
+    part_in = refs[2:10]
     near_strip, far_strip, before, after = refs[10:14]
     free_in, target_in = refs[14:16]
     table_in = refs[16:30]
     resist_out, free_out, own_out, other_out = refs[30:34]
     cells, mask, shading, fields, amps, halves, sums, free, target = refs[34:43]
     tables = refs[43:57]
-    free_sems, table_sems, target_sem, resist_sems, out_sems = refs[57:62]
+    parts = refs[57:65]
+    free_sems, table_sems, target_sem, resist_sems, out_sems, part_sems = refs[65:71]
     (spectra, gain, first, second, up_u, up_ut, up_v, up_vt, fine, fine_lo, fine_t, fine_tlo, out_v, out_u) = tables
 
+    part_loads = [pltpu.make_async_copy(a, b, part_sems.at[n]) for n, (a, b) in enumerate(zip(part_in, parts))]
+    for load in part_loads:
+        load.start()
     loads = [
         pltpu.make_async_copy(free_in.at[pl.ds(256 * n, 256)], free.at[pl.ds(256 * n, 256)], free_sems.at[n])
         for n in range(4)
@@ -130,7 +135,7 @@
     def code(a, b):
         return codes[a * 18 + b], codes[324 + a * 18 + b]
 
-    fill_cells(parts, cells)
+    fill_cells(parts, cells, part_loads)
     core = codes[652]
     for a, flag, own_core in ((0, 648, 1), (17, 649, 0)):
         for p in range(8):
@@ -260,9 +265,10 @@
             groups = turned([shading[pl.ds(rows + 8 * i, 8), cols] for i in range(8)], turn_a, turn_b)
             for loc, turn, right, keep in ((loc_a, turn_a, False, left), (loc_b, turn_b, True, ~left)):
                 top, low, at = places(loc, turn, right)
-                for i in range(4):
-                    sums[top, at[i], :] = sums[top, at[i], :] + jnp.where(keep, groups[i], 0.0)
-                    sums[low, at[i], :] = sums[low, at[i], :] + jnp.where(keep, groups[4 + i], 0.0)
+                spots = [(top, at[i]) for i in range(4)] + [(low, at[i]) for i in range(4)]
+                totals = [sums[n, r, :] + jnp.where(keep, g, 0.0) for (n, r), g in zip(spots, groups)]
+                for (n, r), total in zip(spots, totals):
+                    sums[n, r, :] = total
         return 0
 
     lax.fori_loop(0, 16, collect, 0)
@@ -284,24 +290,31 @@
 
 def final_kernel(*refs):
     codes = refs[0]
-    parts = refs[1:9]
-    free, out, cells = refs[9:12]
-    step = pl.program_id(0)
-
-    @pl.when(step == 0)
-    def _():
-        fill_cells(parts, cells)
-
-    def interior(r, _):
-        rows = pl.ds(pl.multiple_of(r * 64, 64), 64)
+    part_in, (free_in, out), cells, free = refs[1:9], refs[9:11], refs[11], refs[12]
+    parts, (part_sems, free_sems, out_sems) = refs[13:21], refs[21:24]
+    part_loads = [pltpu.make_async_copy(a, b, part_sems.at[n]) for n, (a, b) in enumerate(zip(part_in, parts))]
+    strips = [pl.ds(128 * n, 128) for n in range(8)]
+    loads = [pltpu.make_async_copy(free_in.at[r], free.at[r], free_sems.at[n]) for n, r in enumerate(strips)]
+    stores = [pltpu.make_async_copy(free.at[r], out.at[r], out_sems.at[n]) for n, r in enumerate(strips)]
+    for load in part_loads + loads:
+        load.start()
+    fill_cells(parts, cells, part_loads)
+
+    def interior(a, _):
+        rows = pl.ds(pl.multiple_of(a * 64, 64), 64)
         for p in range(8):
             cols = slice(p * 128, p * 128 + 128)
-            at = (step * 2 + r + 1) * 18 + 2 * p
+            at = (a + 1) * 18 + 2 * p
             image = pair_image(cells, codes[at + 1], codes[325 + at], codes[at + 2], codes[326 + at])
-            out[rows, cols] = jnp.tanh(image + free[rows, cols])
+            free[rows, cols] = jnp.tanh(image + free[rows, cols])
         return 0
 
-    lax.fori_loop(0, 2, interior, 0)
+    for n in range(8):
+        loads[n].wait()
+        lax.fori_loop(2 * n, 2 * n + 2, interior, 0)
+        stores[n].start()
+    for store in stores:
+        store.wait()
 
 
 def flat(x, c, y, z):
@@ -392,13 +405,16 @@
 
     def strip(at, line):
         pad = jnp.concatenate([codes_of(inst_master[line : line + 1]), codes_of(inst_orient[line : line + 1])], 0)
-        return jnp.concatenate([tile_free[at : at + 64].astype(BF16), jnp.pad(pad, ((0, 14), (0, 0)))], 0)
-
-    top, bottom = strip(0, 0), strip(SIDE - 64, 15)
+        return jnp.concatenate([edges[at].astype(BF16), jnp.pad(pad, ((0, 14), (0, 0)))], 0)
+
+    edges = lax.optimization_barrier(
+        (tile_free[:64], tile_free[SIDE - 64 :], tile_free[:, :64], tile_free[:, SIDE - 64 :])
+    )
+    top, bottom = strip(0, 0), strip(1, 15)
     for_near, for_far = jnp.where(core == 0, bottom, top), jnp.where(core == 0, top, bottom)
-    group, for_near, for_far = lax.optimization_barrier((group, for_near, for_far))
+    near_strip, far_strip = send(for_near, SWAP), send(for_far, OVER)
     parts = gathered_far(group)
-    near_strip, far_strip = send(for_near, SWAP), send(for_far, OVER)
+    _, near_strip, far_strip = lax.optimization_barrier((group, near_strip, far_strip))
 
     def ints(a):
         return a.astype(F32).astype(jnp.int32)
@@ -413,7 +429,7 @@
 
     def side(at, line):
         over, under = above_below((slice(0, 64), slice(at, at + 64)))
-        pixels = jnp.concatenate([over, tile_free[:, at : at + 64].astype(BF16), under], 0)
+        pixels = jnp.concatenate([over, edges[2 if at == 0 else 3].astype(BF16), under], 0)
         lines = jnp.stack([tall_master[:, line], tall_orient[:, line]], 1).astype(BF16)
         return jnp.concatenate([pixels, jnp.pad(lines, ((0, 14), (0, 62)))], 0)
 
@@ -440,7 +456,7 @@
     resist, free_new, own, other = pl.pallas_call(
         main_kernel,
         out_shape=(wide, wide, sums_shape, sums_shape),
-        in_specs=[smem] * 2 + [vmem] * 12 + [anywhere] * (2 + len(tables)),
+        in_specs=[smem] * 2 + [anywhere] * 8 + [vmem] * 4 + [anywhere] * (2 + len(tables)),
         out_specs=(anywhere, anywhere, vmem, vmem),
         scratch_shapes=[
             pltpu.VMEM((512, 32, 128), F32),
@@ -453,13 +469,15 @@
             pltpu.VMEM((SIDE, SIDE), F32),
             pltpu.VMEM((SIDE, SIDE), F32),
             *(pltpu.VMEM(t.shape, t.dtype) for t in tables),
+            *[pltpu.VMEM((32, 32, 128), BF16)] * 8,
             pltpu.SemaphoreType.DMA((4,)),
             pltpu.SemaphoreType.DMA((len(tables),)),
             pltpu.SemaphoreType.DMA((1,)),
             pltpu.SemaphoreType.DMA((4,)),
             pltpu.SemaphoreType.DMA((4,)),
+            pltpu.SemaphoreType.DMA((8,)),
         ],
-        compiler_params=pltpu.CompilerParams(vmem_limit_bytes=60 * 1024 * 1024),
+        compiler_params=pltpu.CompilerParams(vmem_limit_bytes=52 * 1024 * 1024),
         name="image_and_gradient",
     )(codes, weights, *parts, near_strip, far_strip, before, after, tile_free, target, *tables)
 
@@ -470,11 +488,15 @@
     new_mask = pl.pallas_call(
         final_kernel,
         out_shape=wide,
-        grid=(8,),
-        in_specs=[smem] + [vmem] * 8 + [pl.BlockSpec((128, SIDE), lambda s: (s, 0))],
-        out_specs=pl.BlockSpec((128, SIDE), lambda s: (s, 0)),
-        scratch_shapes=[pltpu.VMEM((512, 32, 128), F32)],
-        compiler_params=pltpu.CompilerParams(vmem_limit_bytes=58 * 1024 * 1024),
+        in_specs=[smem] + [anywhere] * 9,
+        out_specs=anywhere,
+        scratch_shapes=[
+            pltpu.VMEM((512, 32, 128), F32),
+            pltpu.VMEM((SIDE, SIDE), F32),
+            *[pltpu.VMEM((32, 32, 128), BF16)] * 8,
+            *[pltpu.SemaphoreType.DMA((8,))] * 3,
+        ],
+        compiler_params=pltpu.CompilerParams(vmem_limit_bytes=52 * 1024 * 1024),
         name="final_mask",
     )(codes, *parts, free_new)
     mine = from_wire(parts[0][:8]).reshape(8, CELL * CELL).astype(F32)

time: 156 us -> 158 us (1.013)
  waiting for transfers between devices: 29.3 us -> 42.6 us
  Pallas kernels: 54.4 us -> 45.8 us
  local copies, waits for them, and re-layouts: 5.85 us -> 10.2 us
  other arithmetic: 10.7 us -> 6.9 us
  starting transfers between devices: 54.3 us -> 50.8 us
    pallas_call x1, Pallas kernels: 44.8 us -> 38.1 us  [per_device(): pl.pallas_call(main_kernel, out_shape=(wide, wide, sums_shape, sums_shape...]
    ppermute x1, waiting for transfers between devices: 0.01 us -> 5.96 us  [per_device(): before = lax.ppermute(side(SIDE - 64, 15), 'col', up)]
    ppermute x1, waiting for transfers between devices: 4.07 us -> 9.07 us  [per_device(): after = lax.ppermute(side(0, 0), 'col', down)]
    ppermute x32, starting transfers between devices: 49 us -> 45.5 us  [send(): return lax.ppermute(value, BOTH, pairs)]
    another operation x4 -> x3, other arithmetic: 4.12 us -> 1.62 us
    ppermute x32, waiting for transfers between devices: 25.2 us -> 27.5 us  [send(): return lax.ppermute(value, BOTH, pairs)]
    slice x2, local copies, waits for them, and re-layouts: 0.18 us -> 2.41 us  [the longest x1 1.35 us: per_device(): tile_free[:, SIDE - 64:]]
    pallas_call x1, Pallas kernels: 9.53 us -> 7.7 us  [per_device(): pl.pallas_call(final_kernel, out_shape=wide, in_specs=[smem] + [anywhere]...]
  transfers between devices with their start and end apart: 34 -> 34, of which waited for: 16 -> 18; matrix products, arithmetic and copies ran while one was open for 7% -> 7% of each run, Pallas kernels for 0% -> 0%
where the time goes in v3:
time: 158 us; the launch traced here: 157 us
  starting transfers between devices  50.8 us (32%)
  Pallas kernels  45.8 us (29%)
  waiting for transfers between devices  42.6 us (27%)
  local copies, waits for them, and re-layouts  10.2 us (6%)
  other arithmetic  6.9 us (4%)
    ppermute x32, starting transfers between devices, send(): return lax.ppermute(value, BOTH, pairs)  45.5 us
    pallas_call x1, Pallas kernels, per_device(): pl.pallas_call(main_kernel, out_shape=(wide, wide, sums_shape, sums_shape...  38.1 us
    ppermute x32, waiting for transfers between devices, send(): return lax.ppermute(value, BOTH, pairs)  27.5 us
    ppermute x1, waiting for transfers between devices, per_device(): after = lax.ppermute(side(0, 0), 'col', down)  9.07 us
    pallas_call x1, Pallas kernels, per_device(): pl.pallas_call(final_kernel, out_shape=wide, in_specs=[smem] + [anywhere]...  7.7 us
    ppermute x1, waiting for transfers between devices, per_device(): before = lax.ppermute(side(SIDE - 64, 15), 'col', up)  5.96 us
    ppermute x1, starting transfers between devices, per_device(): before = lax.ppermute(side(SIDE - 64, 15), 'col', up)  3.98 us
    unnamed x18, local copies, waits for them, and re-layouts  3.29 us
  transfers between devices with their start and end apart: 34, of which 18 were waited for; matrix products, arithmetic and copies ran while one was open for 7% of the time, Pallas kernels for 0%

profile of v3, /device:TPU:1, one launch (start us, length us, event | category | flops | bytes accessed | tf_op | source)
XLA Modules:
  0.0 157.4 jit_solution(14424458087820885467)
XLA Ops:
  1.9 3.6 %collective-permute-start.2 = (bf16[8,32,128]{2,1,0:T(8,128)(2,1)S(1)}, bf16[8,32,128]{2,1,0:T(8,128)(2,1)S(1)}, u32[]{:S(2)}, u32[]{:S(2)}) collective-permute-start(bf16[8,32,128]{2,1,0:T(8,128)(2,1)S(1)} %pad_maximum_fusion.2), channel_id=1, source_target_pairs={{0,3},{1,0},{2,1},{3,2},{4,7},{5,4},{6,5},{7,6},{8,11},{9,8},{10,9... | collective-permute-start | bytes 196616 | tf_op jit(solution)/shard_map/ppermute | solution.py:352
  10.5 2.3 %collective-permute-start.3 = (bf16[80,1024]{1,0:T(8,128)(2,1)S(1)}, bf16[80,1024]{1,0:T(8,128)(2,1)S(1)}, u32[]{:S(2)}, u32[]{:S(2)}) collective-permute-start(bf16[80,1024]{1,0:T(8,128)(2,1)S(1)} %get-tuple-element.43), channel_id=1, source_target_pairs={{0,16},{16,0},{1,17},{17,1},{2,18},{18,2},{3,19},{19,3},{4,20},{20... | collective-permute-start | bytes 491528 | tf_op jit(solution)/shard_map/ppermute | solution.py:352
  12.8 3.0 %collective-permute-start.4 = (bf16[80,1024]{1,0:T(8,128)(2,1)S(1)}, bf16[80,1024]{1,0:T(8,128)(2,1)S(1)}, u32[]{:S(2)}, u32[]{:S(2)}) collective-permute-start(bf16[80,1024]{1,0:T(8,128)(2,1)S(1)} %get-tuple-element.42), channel_id=1, source_target_pairs={{32,16},{33,17},{34,18},{35,19},{36,20},{37,21},{38,22},{39,23},{4... | collective-permute-start | bytes 491528 | tf_op jit(solution)/shard_map/ppermute | solution.py:352
  17.4 2.4 %reshape.51.refs_16_ = f32[2,128,1024]{2,1,0:T(8,128)} reshape(f32[2,128,8,128]{3,2,1,0:T(8,128)} %param.27) | data formatting | bytes 2097152 | tf_op jit(solution)/shard_map/reshape | solution.py:455
  19.9 2.0 %collective-permute-start.7 = (bf16[32,32,128]{2,1,0:T(8,128)(2,1)S(1)}, bf16[32,32,128]{2,1,0:T(8,128)(2,1)S(1)}, u32[]{:S(2)}, u32[]{:S(2)}) collective-permute-start(bf16[32,32,128]{2,1,0:T(8,128)(2,1)S(1)} %pad_maximum_fusion.refs_2_), channel_id=1, source_target_pairs={{0,4},{1,5},{2,6},{3,7},{4,8},{5,9},{6,10},{7,11},{8,12},{9,13},{1... | collective-permute-start | bytes 786440 | tf_op jit(solution)/shard_map/ppermute | solution.py:352
  26.7 9.1 %collective-permute-done.6.refs_13_ = bf16[1184,64]{1,0:T(8,128)(2,1)S(1)} collective-permute-done((bf16[1184,64]{1,0:T(8,128)(2,1)S(1)}, bf16[1184,64]{1,0:T(8,128)(2,1)S(1)}, u32[]{:S(2)}, u32[]{:S(2)}) %collective-permute-start.6) | collective-permute-done | bytes 151584 | tf_op jit(solution)/shard_map/ppermute | solution.py:438
  35.8 4.0 %collective-permute-start.5 = (bf16[1184,64]{1,0:T(8,128)(2,1)S(1)}, bf16[1184,64]{1,0:T(8,128)(2,1)S(1)}, u32[]{:S(2)}, u32[]{:S(2)}) collective-permute-start(bf16[1184,64]{1,0:T(8,128)(2,1)S(1)} %fusion.4), channel_id=1, source_target_pairs={{0,1},{1,2},{2,3},{3,4},{4,5},{5,6},{6,7},{7,8},{8,9},{9,10},{10,1... | collective-permute-start | bytes 454664 | tf_op jit(solution)/shard_map/ppermute | solution.py:437
  40.0 6.0 %collective-permute-done.5.refs_12_ = bf16[1184,64]{1,0:T(8,128)(2,1)S(1)} collective-permute-done((bf16[1184,64]{1,0:T(8,128)(2,1)S(1)}, bf16[1184,64]{1,0:T(8,128)(2,1)S(1)}, u32[]{:S(2)}, u32[]{:S(2)}) %collective-permute-start.5) | collective-permute-done | bytes 151584 | tf_op jit(solution)/shard_map/ppermute | solution.py:437
  51.6 38.1 %image_and_gradient.1 = (f32[1024,1024]{1,0:T(8,128)}, f32[1024,1024]{1,0:T(8,128)}, bf16[128,32,128]{2,1,0:T(8,128)(2,1)}, bf16[128,32,128]{2,1,0:T(8,128)(2,1)}) custom-call(s32[653]{0:T(1024)S(1)} %pad_add_fusion.2.refs_0_, f32[8]{0:T(128)S(1)} %copy-done.1, bf16[32,32,128]{2,1,0:T(8,128)(2,1)S(1)} %pad_maximum_fusion.refs_2_, ...), custom_call_target="tpu_custom_call" | custom-call | tf_op jit(solution)/shard_map/image_and_gradient/pallas_call | solution.py:456
  90.1 2.5 %collective-permute-done.14 = bf16[128,32,128]{2,1,0:T(8,128)(2,1)S(1)} collective-permute-done((bf16[128,32,128]{2,1,0:T(8,128)(2,1)}, bf16[128,32,128]{2,1,0:T(8,128)(2,1)S(1)}, u32[]{:S(2)}, u32[]{:S(2)}) %collective-permute-start.14) | collective-permute-done | bytes 1048608 | tf_op jit(solution)/shard_map/ppermute | solution.py:352
  94.2 2.3 %collective-permute-start.17 = (bf16[32,32,128]{2,1,0:T(8,128)(2,1)S(1)}, bf16[32,32,128]{2,1,0:T(8,128)(2,1)S(1)}, u32[]{:S(2)}, u32[]{:S(2)}) collective-permute-start(bf16[32,32,128]{2,1,0:T(8,128)(2,1)S(1)} %get-tuple-element.30), channel_id=1, source_target_pairs={{0,4},{1,5},{2,6},{3,7},{4,8},{5,9},{6,10},{7,11},{8,12},{9,13},{1... | collective-permute-start | bytes 786440 | tf_op jit(solution)/shard_map/ppermute | solution.py:352
  96.9 1.8 %collective-permute-start.15 = (bf16[32,32,128]{2,1,0:T(8,128)(2,1)S(1)}, bf16[32,32,128]{2,1,0:T(8,128)(2,1)S(1)}, u32[]{:S(2)}, u32[]{:S(2)}) collective-permute-start(bf16[32,32,128]{2,1,0:T(8,128)(2,1)S(1)} %get-tuple-element.29), channel_id=1, source_target_pairs={{0,8},{1,9},{2,10},{3,11},{4,12},{5,13},{6,14},{7,15},{8,0},{9,1},... | collective-permute-start | bytes 786440 | tf_op jit(solution)/shard_map/ppermute | solution.py:352
  98.7 1.9 %collective-permute-done.17 = bf16[32,32,128]{2,1,0:T(8,128)(2,1)S(1)} collective-permute-done((bf16[32,32,128]{2,1,0:T(8,128)(2,1)S(1)}, bf16[32,32,128]{2,1,0:T(8,128)(2,1)S(1)}, u32[]{:S(2)}, u32[]{:S(2)}) %collective-permute-start.17) | collective-permute-done | bytes 262176 | tf_op jit(solution)/shard_map/ppermute | solution.py:352
  102.0 2.6 %collective-permute-done.15 = bf16[32,32,128]{2,1,0:T(8,128)(2,1)S(1)} collective-permute-done((bf16[32,32,128]{2,1,0:T(8,128)(2,1)S(1)}, bf16[32,32,128]{2,1,0:T(8,128)(2,1)S(1)}, u32[]{:S(2)}, u32[]{:S(2)}) %collective-permute-start.15) | collective-permute-done | bytes 262176 | tf_op jit(solution)/shard_map/ppermute | solution.py:352
  104.8 2.7 %collective-permute-start.20 = (bf16[8,32,128]{2,1,0:T(8,128)(2,1)S(1)}, bf16[8,32,128]{2,1,0:T(8,128)(2,1)S(1)}, u32[]{:S(2)}, u32[]{:S(2)}) collective-permute-start(bf16[8,32,128]{2,1,0:T(8,128)(2,1)S(1)} %get-tuple-element.47), channel_id=1, source_target_pairs={{0,1},{1,2},{2,3},{3,0},{4,5},{5,6},{6,7},{7,4},{8,9},{9,10},{10,1... | collective-permute-start | bytes 196616 | tf_op jit(solution)/shard_map/ppermute | solution.py:352
  107.4 1.8 %collective-permute-start.19 = (bf16[8,32,128]{2,1,0:T(8,128)(2,1)S(1)}, bf16[8,32,128]{2,1,0:T(8,128)(2,1)S(1)}, u32[]{:S(2)}, u32[]{:S(2)}) collective-permute-start(bf16[8,32,128]{2,1,0:T(8,128)(2,1)S(1)} %get-tuple-element.48), channel_id=1, source_target_pairs={{0,3},{1,0},{2,1},{3,2},{4,7},{5,4},{6,5},{7,6},{8,11},{9,8},{10,9... | collective-permute-start | bytes 196616 | tf_op jit(solution)/shard_map/ppermute | solution.py:352
  110.8 3.0 %collective-permute-done.18 = bf16[8,32,128]{2,1,0:T(8,128)(2,1)S(1)} collective-permute-done((bf16[8,32,128]{2,1,0:T(8,128)(2,1)S(1)}, bf16[8,32,128]{2,1,0:T(8,128)(2,1)S(1)}, u32[]{:S(2)}, u32[]{:S(2)}) %collective-permute-start.18) | collective-permute-done | bytes 65568 | tf_op jit(solution)/shard_map/ppermute | solution.py:352
  113.9 3.7 %collective-permute-start.23 = (bf16[8,32,128]{2,1,0:T(8,128)(2,1)S(1)}, bf16[8,32,128]{2,1,0:T(8,128)(2,1)S(1)}, u32[]{:S(2)}, u32[]{:S(2)}) collective-permute-start(bf16[8,32,128]{2,1,0:T(8,128)(2,1)S(1)} %add_convert_fusion.2), channel_id=1, source_target_pairs={{0,96},{16,112},{1,97},{17,113},{2,98},{18,114},{3,99},{19,115},{4... | collective-permute-start | bytes 196616 | tf_op jit(solution)/shard_map/ppermute | solution.py:352
  119.3 3.4 %collective-permute-done.22 = bf16[8,32,128]{2,1,0:T(8,128)(2,1)S(1)} collective-permute-done((bf16[8,32,128]{2,1,0:T(8,128)(2,1)S(1)}, bf16[8,32,128]{2,1,0:T(8,128)(2,1)S(1)}, u32[]{:S(2)}, u32[]{:S(2)}) %collective-permute-start.22) | collective-permute-done | bytes 65568 | tf_op jit(solution)/shard_map/ppermute | solution.py:352
  126.6 1.9 %collective-permute-done.25 = bf16[8,32,128]{2,1,0:T(8,128)(2,1)S(1)} collective-permute-done((bf16[8,32,128]{2,1,0:T(8,128)(2,1)S(1)}, bf16[8,32,128]{2,1,0:T(8,128)(2,1)S(1)}, u32[]{:S(2)}, u32[]{:S(2)}) %collective-permute-start.25) | collective-permute-done | bytes 65568 | tf_op jit(solution)/shard_map/ppermute | solution.py:352
  129.7 6.1 %collective-permute-start.30 = (bf16[32,32,128]{2,1,0:T(8,128)(2,1)S(1)}, bf16[32,32,128]{2,1,0:T(8,128)(2,1)S(1)}, u32[]{:S(2)}, u32[]{:S(2)}) collective-permute-start(bf16[32,32,128]{2,1,0:T(8,128)(2,1)S(1)} %pad_maximum_fusion.1.refs_1_), channel_id=1, source_target_pairs={{0,16},{16,0},{1,17},{17,1},{2,18},{18,2},{3,19},{19,3},{4,20},{20... | collective-permute-start | bytes 786440 | tf_op jit(solution)/shard_map/ppermute | solution.py:352
  139.4 6.1 %collective-permute-done.27.refs_2_ = bf16[32,32,128]{2,1,0:T(8,128)(2,1)S(1)} collective-permute-done((bf16[32,32,128]{2,1,0:T(8,128)(2,1)S(1)}, bf16[32,32,128]{2,1,0:T(8,128)(2,1)S(1)}, u32[]{:S(2)}, u32[]{:S(2)}) %collective-permute-start.27) | collective-permute-done | bytes 262176 | tf_op jit(solution)/shard_map/ppermute | solution.py:352
  145.5 1.7 %collective-permute-start.32 = (bf16[32,32,128]{2,1,0:T(8,128)(2,1)S(1)}, bf16[32,32,128]{2,1,0:T(8,128)(2,1)S(1)}, u32[]{:S(2)}, u32[]{:S(2)}) collective-permute-start(bf16[32,32,128]{2,1,0:T(8,128)(2,1)S(1)} %collective-permute-done.28.refs_3_), channel_id=1, source_target_pairs={{0,16},{16,0},{1,17},{17,1},{2,18},{18,2},{3,19},{19,3},{4,20},{20... | collective-permute-start | bytes 786440 | tf_op jit(solution)/shard_map/ppermute | solution.py:352
  149.5 7.7 %final_mask.1 = f32[1024,1024]{1,0:T(8,128)} custom-call(s32[653]{0:T(1024)S(1)} %pad_add_fusion.2.refs_0_, bf16[32,32,128]{2,1,0:T(8,128)(2,1)S(1)} %pad_maximum_fusion.1.refs_1_, bf16[32,32,128]{2,1,0:T(8,128)(2,1)S(1)} %collective-permute-done.27.refs_2_, bf16[32,32,128]{2,1,0:T(8,128)(2,1)S(1)} %collective-permute-done.28.refs_3_, ...), custom_call_target="tpu_custom_call" | custom-call | tf_op jit(solution)/shard_map/final_mask/pallas_call | solution.py:488
  (128 shorter events, 36.6 us)
Async XLA Ops:
  1.9 17.9 %collective-permute-start.2 = (bf16[8,32,128]{2,1,0:T(8,128)(2,1)S(1)}, bf16[8,32,128]{2,1,0:T(8,128)(2,1)S(1)}, u32[]{:S(2)}, u32[]{:S(2)}) collective-permute-start(bf16[8,32,128]{2,1,0:T(8,128)(2,1)S(1)} %pad_maximum_fusion.2), channel_id=1, source_target_pairs={{0,3},{1,0},{2,1},{3,2},{4,7},{5,4},{6,5},{7,6},{8,11},{9,8},{10,9... | collective-permute-start | bytes 196616 | tf_op jit(solution)/shard_map/ppermute | solution.py:352
  5.5 14.3 %collective-permute-start.1 = (bf16[8,32,128]{2,1,0:T(8,128)(2,1)S(1)}, bf16[8,32,128]{2,1,0:T(8,128)(2,1)S(1)}, u32[]{:S(2)}, u32[]{:S(2)}) collective-permute-start(bf16[8,32,128]{2,1,0:T(8,128)(2,1)S(1)} %pad_maximum_fusion.2), channel_id=1, source_target_pairs={{0,2},{1,3},{2,0},{3,1},{4,6},{5,7},{6,4},{7,5},{8,10},{9,11},{10,... | collective-permute-start | bytes 196616 | tf_op jit(solution)/shard_map/ppermute | solution.py:352
  5.9 13.9 %collective-permute-start = (bf16[8,32,128]{2,1,0:T(8,128)(2,1)S(1)}, bf16[8,32,128]{2,1,0:T(8,128)(2,1)S(1)}, u32[]{:S(2)}, u32[]{:S(2)}) collective-permute-start(bf16[8,32,128]{2,1,0:T(8,128)(2,1)S(1)} %pad_maximum_fusion.2), channel_id=1, source_target_pairs={{0,1},{1,2},{2,3},{3,0},{4,5},{5,6},{6,7},{7,4},{8,9},{9,10},{10,1... | collective-permute-start | bytes 196616 | tf_op jit(solution)/shard_map/ppermute | solution.py:352
  10.5 13.9 %collective-permute-start.3 = (bf16[80,1024]{1,0:T(8,128)(2,1)S(1)}, bf16[80,1024]{1,0:T(8,128)(2,1)S(1)}, u32[]{:S(2)}, u32[]{:S(2)}) collective-permute-start(bf16[80,1024]{1,0:T(8,128)(2,1)S(1)} %get-tuple-element.43), channel_id=1, source_target_pairs={{0,16},{16,0},{1,17},{17,1},{2,18},{18,2},{3,19},{19,3},{4,20},{20... | collective-permute-start | bytes 491528 | tf_op jit(solution)/shard_map/ppermute | solution.py:352
  12.8 11.6 %collective-permute-start.4 = (bf16[80,1024]{1,0:T(8,128)(2,1)S(1)}, bf16[80,1024]{1,0:T(8,128)(2,1)S(1)}, u32[]{:S(2)}, u32[]{:S(2)}) collective-permute-start(bf16[80,1024]{1,0:T(8,128)(2,1)S(1)} %get-tuple-element.42), channel_id=1, source_target_pairs={{32,16},{33,17},{34,18},{35,19},{36,20},{37,21},{38,22},{39,23},{4... | collective-permute-start | bytes 491528 | tf_op jit(solution)/shard_map/ppermute | solution.py:352
  19.9 27.4 %collective-permute-start.7 = (bf16[32,32,128]{2,1,0:T(8,128)(2,1)S(1)}, bf16[32,32,128]{2,1,0:T(8,128)(2,1)S(1)}, u32[]{:S(2)}, u32[]{:S(2)}) collective-permute-start(bf16[32,32,128]{2,1,0:T(8,128)(2,1)S(1)} %pad_maximum_fusion.refs_2_), channel_id=1, source_target_pairs={{0,4},{1,5},{2,6},{3,7},{4,8},{5,9},{6,10},{7,11},{8,12},{9,13},{1... | collective-permute-start | bytes 786440 | tf_op jit(solution)/shard_map/ppermute | solution.py:352
  21.9 26.7 %collective-permute-start.8 = (bf16[32,32,128]{2,1,0:T(8,128)(2,1)S(1)}, bf16[32,32,128]{2,1,0:T(8,128)(2,1)S(1)}, u32[]{:S(2)}, u32[]{:S(2)}) collective-permute-start(bf16[32,32,128]{2,1,0:T(8,128)(2,1)S(1)} %pad_maximum_fusion.refs_2_), channel_id=1, source_target_pairs={{0,8},{1,9},{2,10},{3,11},{4,12},{5,13},{6,14},{7,15},{8,0},{9,1},... | collective-permute-start | bytes 786440 | tf_op jit(solution)/shard_map/ppermute | solution.py:352
  23.2 25.5 %collective-permute-start.9 = (bf16[32,32,128]{2,1,0:T(8,128)(2,1)S(1)}, bf16[32,32,128]{2,1,0:T(8,128)(2,1)S(1)}, u32[]{:S(2)}, u32[]{:S(2)}) collective-permute-start(bf16[32,32,128]{2,1,0:T(8,128)(2,1)S(1)} %pad_maximum_fusion.refs_2_), channel_id=1, source_target_pairs={{0,12},{1,13},{2,14},{3,15},{4,0},{5,1},{6,2},{7,3},{8,4},{9,5},{1... | collective-permute-start | bytes 786440 | tf_op jit(solution)/shard_map/ppermute | solution.py:352
  24.4 24.8 %collective-permute-start.10 = (bf16[32,32,128]{2,1,0:T(8,128)(2,1)S(1)}, bf16[32,32,128]{2,1,0:T(8,128)(2,1)S(1)}, u32[]{:S(2)}, u32[]{:S(2)}) collective-permute-start(bf16[32,32,128]{2,1,0:T(8,128)(2,1)S(1)} %pad_maximum_fusion.refs_2_), channel_id=1, source_target_pairs={{0,16},{16,0},{1,17},{17,1},{2,18},{18,2},{3,19},{19,3},{4,20},{20... | collective-permute-start | bytes 786440 | tf_op jit(solution)/shard_map/ppermute | solution.py:352
  25.2 10.6 %collective-permute-start.6 = (bf16[1184,64]{1,0:T(8,128)(2,1)S(1)}, bf16[1184,64]{1,0:T(8,128)(2,1)S(1)}, u32[]{:S(2)}, u32[]{:S(2)}) collective-permute-start(bf16[1184,64]{1,0:T(8,128)(2,1)S(1)} %fusion.5), channel_id=1, source_target_pairs={{1,0},{2,1},{3,2},{4,3},{5,4},{6,5},{7,6},{8,7},{9,8},{10,9},{11,1... | collective-permute-start | bytes 454664 | tf_op jit(solution)/shard_map/ppermute | solution.py:438
  35.8 10.1 %collective-permute-start.5 = (bf16[1184,64]{1,0:T(8,128)(2,1)S(1)}, bf16[1184,64]{1,0:T(8,128)(2,1)S(1)}, u32[]{:S(2)}, u32[]{:S(2)}) collective-permute-start(bf16[1184,64]{1,0:T(8,128)(2,1)S(1)} %fusion.4), channel_id=1, source_target_pairs={{0,1},{1,2},{2,3},{3,4},{4,5},{5,6},{6,7},{7,8},{8,9},{9,10},{10,1... | collective-permute-start | bytes 454664 | tf_op jit(solution)/shard_map/ppermute | solution.py:437
  94.2 6.5 %collective-permute-start.17 = (bf16[32,32,128]{2,1,0:T(8,128)(2,1)S(1)}, bf16[32,32,128]{2,1,0:T(8,128)(2,1)S(1)}, u32[]{:S(2)}, u32[]{:S(2)}) collective-permute-start(bf16[32,32,128]{2,1,0:T(8,128)(2,1)S(1)} %get-tuple-element.30), channel_id=1, source_target_pairs={{0,4},{1,5},{2,6},{3,7},{4,8},{5,9},{6,10},{7,11},{8,12},{9,13},{1... | collective-permute-start | bytes 786440 | tf_op jit(solution)/shard_map/ppermute | solution.py:352
  96.4 5.5 %collective-permute-start.16 = (bf16[32,32,128]{2,1,0:T(8,128)(2,1)S(1)}, bf16[32,32,128]{2,1,0:T(8,128)(2,1)S(1)}, u32[]{:S(2)}, u32[]{:S(2)}) collective-permute-start(bf16[32,32,128]{2,1,0:T(8,128)(2,1)S(1)} %get-tuple-element.31), channel_id=1, source_target_pairs={{0,12},{1,13},{2,14},{3,15},{4,0},{5,1},{6,2},{7,3},{8,4},{9,5},{1... | collective-permute-start | bytes 786440 | tf_op jit(solution)/shard_map/ppermute | solution.py:352
  96.9 7.7 %collective-permute-start.15 = (bf16[32,32,128]{2,1,0:T(8,128)(2,1)S(1)}, bf16[32,32,128]{2,1,0:T(8,128)(2,1)S(1)}, u32[]{:S(2)}, u32[]{:S(2)}) collective-permute-start(bf16[32,32,128]{2,1,0:T(8,128)(2,1)S(1)} %get-tuple-element.29), channel_id=1, source_target_pairs={{0,8},{1,9},{2,10},{3,11},{4,12},{5,13},{6,14},{7,15},{8,0},{9,1},... | collective-permute-start | bytes 786440 | tf_op jit(solution)/shard_map/ppermute | solution.py:352
  104.8 6.1 %collective-permute-start.20 = (bf16[8,32,128]{2,1,0:T(8,128)(2,1)S(1)}, bf16[8,32,128]{2,1,0:T(8,128)(2,1)S(1)}, u32[]{:S(2)}, u32[]{:S(2)}) collective-permute-start(bf16[8,32,128]{2,1,0:T(8,128)(2,1)S(1)} %get-tuple-element.47), channel_id=1, source_target_pairs={{0,1},{1,2},{2,3},{3,0},{4,5},{5,6},{6,7},{7,4},{8,9},{9,10},{10,1... | collective-permute-start | bytes 196616 | tf_op jit(solution)/shard_map/ppermute | solution.py:352
  109.2 4.6 %collective-permute-start.18 = (bf16[8,32,128]{2,1,0:T(8,128)(2,1)S(1)}, bf16[8,32,128]{2,1,0:T(8,128)(2,1)S(1)}, u32[]{:S(2)}, u32[]{:S(2)}) collective-permute-start(bf16[8,32,128]{2,1,0:T(8,128)(2,1)S(1)} %get-tuple-element.46), channel_id=1, source_target_pairs={{0,2},{1,3},{2,0},{3,1},{4,6},{5,7},{6,4},{7,5},{8,10},{9,11},{10,... | collective-permute-start | bytes 196616 | tf_op jit(solution)/shard_map/ppermute | solution.py:352
  113.9 5.3 %collective-permute-start.23 = (bf16[8,32,128]{2,1,0:T(8,128)(2,1)S(1)}, bf16[8,32,128]{2,1,0:T(8,128)(2,1)S(1)}, u32[]{:S(2)}, u32[]{:S(2)}) collective-permute-start(bf16[8,32,128]{2,1,0:T(8,128)(2,1)S(1)} %add_convert_fusion.2), channel_id=1, source_target_pairs={{0,96},{16,112},{1,97},{17,113},{2,98},{18,114},{3,99},{19,115},{4... | collective-permute-start | bytes 196616 | tf_op jit(solution)/shard_map/ppermute | solution.py:352
  117.6 5.0 %collective-permute-start.22 = (bf16[8,32,128]{2,1,0:T(8,128)(2,1)S(1)}, bf16[8,32,128]{2,1,0:T(8,128)(2,1)S(1)}, u32[]{:S(2)}, u32[]{:S(2)}) collective-permute-start(bf16[8,32,128]{2,1,0:T(8,128)(2,1)S(1)} %add_convert_fusion.2), channel_id=1, source_target_pairs={{0,32},{16,48},{1,33},{17,49},{2,34},{18,50},{3,35},{19,51},{4,36}... | collective-permute-start | bytes 196616 | tf_op jit(solution)/shard_map/ppermute | solution.py:352
  117.6 5.0 %collective-permute-start.21 = (bf16[8,32,128]{2,1,0:T(8,128)(2,1)S(1)}, bf16[8,32,128]{2,1,0:T(8,128)(2,1)S(1)}, u32[]{:S(2)}, u32[]{:S(2)}) collective-permute-start(bf16[8,32,128]{2,1,0:T(8,128)(2,1)S(1)} %add_convert_fusion.2), channel_id=1, source_target_pairs={{0,64},{16,80},{1,65},{17,81},{2,66},{18,82},{3,67},{19,83},{4,68}... | collective-permute-start | bytes 196616 | tf_op jit(solution)/shard_map/ppermute | solution.py:352
  123.9 4.6 %collective-permute-start.25 = (bf16[8,32,128]{2,1,0:T(8,128)(2,1)S(1)}, bf16[8,32,128]{2,1,0:T(8,128)(2,1)S(1)}, u32[]{:S(2)}, u32[]{:S(2)}) collective-permute-start(bf16[8,32,128]{2,1,0:T(8,128)(2,1)S(1)} %pad_maximum_fusion.3), channel_id=1, source_target_pairs={{0,2},{1,3},{2,0},{3,1},{4,6},{5,7},{6,4},{7,5},{8,10},{9,11},{10,... | collective-permute-start | bytes 196616 | tf_op jit(solution)/shard_map/ppermute | solution.py:352
  129.7 9.6 %collective-permute-start.30 = (bf16[32,32,128]{2,1,0:T(8,128)(2,1)S(1)}, bf16[32,32,128]{2,1,0:T(8,128)(2,1)S(1)}, u32[]{:S(2)}, u32[]{:S(2)}) collective-permute-start(bf16[32,32,128]{2,1,0:T(8,128)(2,1)S(1)} %pad_maximum_fusion.1.refs_1_), channel_id=1, source_target_pairs={{0,16},{16,0},{1,17},{17,1},{2,18},{18,2},{3,19},{19,3},{4,20},{20... | collective-permute-start | bytes 786440 | tf_op jit(solution)/shard_map/ppermute | solution.py:352
  135.9 9.6 %collective-permute-start.27 = (bf16[32,32,128]{2,1,0:T(8,128)(2,1)S(1)}, bf16[32,32,128]{2,1,0:T(8,128)(2,1)S(1)}, u32[]{:S(2)}, u32[]{:S(2)}) collective-permute-start(bf16[32,32,128]{2,1,0:T(8,128)(2,1)S(1)} %pad_maximum_fusion.1.refs_1_), channel_id=1, source_target_pairs={{0,4},{1,5},{2,6},{3,7},{4,8},{5,9},{6,10},{7,11},{8,12},{9,13},{1... | collective-permute-start | bytes 786440 | tf_op jit(solution)/shard_map/ppermute | solution.py:352
  136.0 9.5 %collective-permute-start.28 = (bf16[32,32,128]{2,1,0:T(8,128)(2,1)S(1)}, bf16[32,32,128]{2,1,0:T(8,128)(2,1)S(1)}, u32[]{:S(2)}, u32[]{:S(2)}) collective-permute-start(bf16[32,32,128]{2,1,0:T(8,128)(2,1)S(1)} %pad_maximum_fusion.1.refs_1_), channel_id=1, source_target_pairs={{0,8},{1,9},{2,10},{3,11},{4,12},{5,13},{6,14},{7,15},{8,0},{9,1},... | collective-permute-start | bytes 786440 | tf_op jit(solution)/shard_map/ppermute | solution.py:352
  137.6 9.7 %collective-permute-start.29 = (bf16[32,32,128]{2,1,0:T(8,128)(2,1)S(1)}, bf16[32,32,128]{2,1,0:T(8,128)(2,1)S(1)}, u32[]{:S(2)}, u32[]{:S(2)}) collective-permute-start(bf16[32,32,128]{2,1,0:T(8,128)(2,1)S(1)} %pad_maximum_fusion.1.refs_1_), channel_id=1, source_target_pairs={{0,12},{1,13},{2,14},{3,15},{4,0},{5,1},{6,2},{7,3},{8,4},{9,5},{1... | collective-permute-start | bytes 786440 | tf_op jit(solution)/shard_map/ppermute | solution.py:352
  (18 other events, 196.2 us)

commit v4 on v3

--- a/solution.py
+++ b/solution.py
@@ -137,30 +137,36 @@
 
     fill_cells(parts, cells, part_loads)
     core = codes[652]
+    def edge_strip(lanes, own_core):
+        return jnp.where(core == own_core, near_strip[0:64, lanes].astype(F32), far_strip[0:64, lanes].astype(F32))
+
+    lane_w = lax.broadcasted_iota(jnp.int32, (64, 128), 1)
+    inside_cols = jnp.where(lane_w < 64, codes[650], codes[651]) > 0
     for a, flag, own_core in ((0, 648, 1), (17, 649, 0)):
-        for p in range(8):
+        for p in range(9):
             cols = slice(p * 128, p * 128 + 128)
-            image = pair_image(cells, *code(a, 2 * p + 1), *code(a, 2 * p + 2))
-            strip = jnp.where(core == own_core, near_strip[0:64, cols].astype(F32), far_strip[0:64, cols].astype(F32))
-            value = jnp.where(codes[flag] > 0, jnp.tanh(image + strip), 0.0)
+            ends = (2 * p + 1, 2 * p + 2) if p < 8 else (0, 17)
+            image = pair_image(cells, *code(a, ends[0]), *code(a, ends[1]))
+            value = jnp.where(codes[flag] > 0, jnp.tanh(image + edge_strip(cols, own_core)), 0.0)
+            if p == 8:
+                value = jnp.where(inside_cols, value, 0.0)
             mask[a * 64 : a * 64 + 64, cols] = value.astype(BF16)
 
-    def edge_cell(a):
-        rows = pl.ds(pl.multiple_of(a * 64, 64), 64)
-        image = pair_image(cells, *code(a, 0), *code(a, 17))
-        strips = jnp.concatenate([before[rows, :], after[rows, :]], axis=1)
-        value = jnp.tanh(image + strips.astype(F32))
-        lane = lax.broadcasted_iota(jnp.int32, (64, 128), 1)
-        at_row = jnp.where(a == 0, codes[648], jnp.where(a == 17, codes[649], 1))
-        keep = jnp.where(lane < 64, codes[650], codes[651]) * at_row
-        mask[rows, 1024:1152] = jnp.where(keep > 0, value, 0.0).astype(BF16)
-
-    def edge_cols(n, _):
-        for u in range(6):
-            edge_cell(n * 6 + u)
+    def edge_cols(r, _):
+        rows = pl.ds(pl.multiple_of(r * 64, 64), 64)
+        left, right = before[rows, :].astype(F32), after[rows, :].astype(F32)
+        strips = (
+            jnp.where(lane_w < 64, left, pltpu.roll(right, 64, 1)),
+            jnp.where(lane_w < 64, pltpu.roll(left, 64, 1), right),
+        )
+        for n in range(2):
+            a = r + 8 * n + 1
+            image = pair_image(cells, *code(a, 0), *code(a, 17))
+            value = jnp.where(inside_cols, jnp.tanh(image + strips[n]), 0.0)
+            mask[pl.ds(pl.multiple_of(a * 64, 64), 64), 1024:1152] = value.astype(BF16)
         return 0
 
-    lax.fori_loop(0, 3, edge_cols, 0)
+    lax.fori_loop(0, 8, edge_cols, 0, unroll=2)
 
     def interior(a, _):
         rows = pl.ds(pl.multiple_of(a * 64, 64), 64)
@@ -324,16 +330,20 @@
 CHIPS = [(x, y, z) for x in range(4) for y in range(4) for z in range(4)]
 
 
-def shift_first(d):
-    return [(flat(x, 0, y, z), flat(x, 0, y, z + d)) for x, y, z in CHIPS] + [
-        (flat(x, 1, y, z), flat(x, 1, y + d, z)) for x, y, z in CHIPS
+def mirrored(n, masks):
+    return [
+        (flat(x, c, y, z), flat(x, c, y ^ (masks[c] * (n % 2)), z ^ (masks[c] * (n // 2))))
+        for x, y, z in CHIPS
+        for c in range(2)
     ]
 
 
-def shift_second(d):
-    return [(flat(x, 0, y, z), flat(x, 0, y + d, z)) for x, y, z in CHIPS] + [
-        (flat(x, 1, y, z), flat(x, 1, y, z + d)) for x, y, z in CHIPS
-    ]
+def near(n):
+    return mirrored(n, (3, 1))
+
+
+def far(n):
+    return mirrored(n, (1, 3))
 
 
 def shift_x(d):
@@ -353,21 +363,21 @@
 
 
 def gathered_near(piece):
-    got = {d: send(piece, shift_first(d)) for d in (2, 1, 3)}
-    return jnp.concatenate([piece, got[1], got[2], got[3]], axis=0)
+    got = [send(piece, near(n)) for n in (3, 1, 2)]
+    return jnp.concatenate([piece, got[1], got[2], got[0]], axis=0)
 
 
 def gathered_far(group):
-    far = {d: send(group, shift_second(d)) for d in (2, 1, 3)}
-    mine = [group, far[1], far[2], far[3]]
+    got = [send(group, far(n)) for n in (3, 1, 2)]
+    mine = [group, got[1], got[2], got[0]]
     return mine + [send(part, SWAP) for part in mine]
 
 
 def scattered_sum(own, other):
     total = (own.astype(F32) + send(other, SWAP).astype(F32)).astype(BF16).reshape(4, 32, 32, 128)
-    got = [send(total[d], shift_second(-d)) for d in (2, 1, 3)]
+    got = [send(total[n], far(n)) for n in (3, 1, 2)]
     total = sum((g.astype(F32) for g in got), total[0].astype(F32)).astype(BF16).reshape(4, 8, 32, 128)
-    got = [send(total[d], shift_first(-d)) for d in (2, 1, 3)]
+    got = [send(total[n], near(n)) for n in (3, 1, 2)]
     total = sum((g.astype(F32) for g in got), total[0].astype(F32)).astype(BF16)
     got = [send(total, shift_x(d)) for d in (2, 1, 3)]
     return sum((g.astype(F32) for g in got), total.astype(F32))
@@ -400,51 +410,51 @@
     own_cells = lax.dynamic_slice_in_dim(masters, core * 8, 8, 0)
     group = gathered_near(to_wire(own_cells.astype(BF16)))
 
-    def codes_of(a):
-        return jnp.pad(a.astype(BF16), ((0, 0), (0, SIDE - a.shape[1])))
-
-    def strip(at, line):
-        pad = jnp.concatenate([codes_of(inst_master[line : line + 1]), codes_of(inst_orient[line : line + 1])], 0)
-        return jnp.concatenate([edges[at].astype(BF16), jnp.pad(pad, ((0, 14), (0, 0)))], 0)
-
     edges = lax.optimization_barrier(
         (tile_free[:64], tile_free[SIDE - 64 :], tile_free[:, :64], tile_free[:, SIDE - 64 :])
     )
-    top, bottom = strip(0, 0), strip(1, 15)
-    for_near, for_far = jnp.where(core == 0, bottom, top), jnp.where(core == 0, top, bottom)
-    near_strip, far_strip = send(for_near, SWAP), send(for_far, OVER)
-    parts = gathered_far(group)
-    _, near_strip, far_strip = lax.optimization_barrier((group, near_strip, far_strip))
+    insts = jnp.stack([inst_master, inst_orient])
+
+    def side(pixels, line):
+        packed = jnp.concatenate([pixels[:512], pixels[512:]], 1).astype(BF16)
+        lines = jnp.pad(insts[:, :, line].astype(BF16), ((0, 14), (0, 112)))
+        return jnp.concatenate([packed, lines], 0)
+
+    up, down = steps("col")
+    before = lax.ppermute(side(edges[3], 15), "col", up)
+    after = lax.ppermute(side(edges[2], 0), "col", down)
 
     def ints(a):
         return a.astype(F32).astype(jnp.int32)
 
-    def above_below(at):
-        near, far = near_strip[at], far_strip[at]
-        return jnp.where(core == 0, far, near), jnp.where(core == 0, near, far)
-
-    above, below = above_below((slice(64, 66), slice(0, 16)))
-    tall_master = jnp.concatenate([ints(above[0:1]), inst_master, ints(below[0:1])], 0)
-    tall_orient = jnp.concatenate([ints(above[1:2]), inst_orient, ints(below[1:2])], 0)
-
-    def side(at, line):
-        over, under = above_below((slice(0, 64), slice(at, at + 64)))
-        pixels = jnp.concatenate([over, edges[2 if at == 0 else 3].astype(BF16), under], 0)
-        lines = jnp.stack([tall_master[:, line], tall_orient[:, line]], 1).astype(BF16)
-        return jnp.concatenate([pixels, jnp.pad(lines, ((0, 14), (0, 62)))], 0)
-
-    up, down = steps("col")
-    before = lax.ppermute(side(SIDE - 64, 15), "col", up)
-    after = lax.ppermute(side(0, 0), "col", down)
-    all_master = jnp.concatenate([ints(before[1152:1170, 0:1]), tall_master, ints(after[1152:1170, 0:1])], 1)
-    all_orient = jnp.concatenate([ints(before[1152:1170, 1:2]), tall_orient, ints(after[1152:1170, 1:2])], 1)
+    wide_insts = jnp.concatenate(
+        [ints(before[512:514, :16])[:, :, None], insts, ints(after[512:514, :16])[:, :, None]], 2
+    )
+
+    def strip(pixels, rows, lanes, line):
+        full = jnp.concatenate([pixels.astype(BF16), before[rows, lanes], after[rows, lanes]], 1)
+        lines = jnp.pad(wide_insts[:, line, :].astype(BF16), ((0, 14), (0, SIDE + 128 - 18)))
+        return jnp.concatenate([full, lines], 0)
+
+    top = strip(edges[0], slice(0, 64), slice(0, 64), 0)
+    bottom = strip(edges[1], slice(448, 512), slice(64, 128), 15)
+    near_strip = send(jnp.where(core == 0, bottom, top), SWAP)
+    far_strip = send(jnp.where(core == 0, top, bottom), OVER)
+    parts = gathered_far(group)
+
+    from_near, from_far = ints(near_strip[64:66, :18]), ints(far_strip[64:66, :18])
+    above, below = jnp.where(core == 0, from_far, from_near), jnp.where(core == 0, from_near, from_far)
+    all_insts = jnp.concatenate([above[:, None, :], wide_insts, below[:, None, :]], 1)
+    all_master, all_orient = all_insts[0], all_insts[1]
 
     matches = all_master[..., None] == jnp.arange(owner_map.shape[0], dtype=jnp.int32)
     slots = jnp.sum(jnp.where(matches, owner_map, 0), axis=-1)
-    at_y, at_z, half, entry = slots // 64, (slots // 16) % 4, (slots // 8) % 2, slots % 8
-    dy, dz = (y - at_y) % 4, (z - at_z) % 4
-    far, near = jnp.where(half == 0, dy, dz), jnp.where(half == 0, dz, dy)
-    locs = (jnp.where(half == core, 0, 1) * 16 + far * 4 + near) * 8 + entry
+    dy, dz = y ^ (slots // 64), z ^ ((slots // 16) % 4)
+    half, entry = (slots // 8) % 2, slots % 8
+    high = (dy // 2) + 2 * (dz // 2)
+    mixed = (dy // 2 ^ dy % 2) + 2 * (dz // 2 ^ dz % 2)
+    outer, inner = jnp.where(half == 0, mixed, high), jnp.where(half == 0, high, mixed)
+    locs = (jnp.where(half == core, 0, 1) * 16 + outer * 4 + inner) * 8 + entry
     inside = jnp.stack([row > 0, row < 7, col > 0, col < 15]).astype(jnp.int32)
     codes = jnp.concatenate([locs.reshape(-1), all_orient.reshape(-1), inside, core.reshape(1).astype(jnp.int32)])
 

time: 158 us -> 151 us (0.956)
  waiting for transfers between devices: 42.6 us -> 28.7 us
  starting transfers between devices: 50.8 us -> 62.5 us
  local copies, waits for them, and re-layouts: 10.2 us -> 7.19 us
    ppermute x2, waiting for transfers between devices: 15 us -> 0.69 us  [the longest x1 0.68 us: per_device(): before = lax.ppermute(side(edges[3], 15), 'col', up)]
    ppermute x32, starting transfers between devices: 45.5 us -> 59 us  [send(): return lax.ppermute(value, BOTH, pairs)]
    ppermute x2, starting transfers between devices: 5.27 us -> 3.58 us  [the longest x1 2.29 us: per_device(): before = lax.ppermute(side(edges[3], 15), 'col', up)]
    unnamed x18 -> x22, local copies, waits for them, and re-layouts: 3.29 us -> 1.79 us
  transfers between devices with their start and end apart: 34 -> 34, of which waited for: 18 -> 20; matrix products, arithmetic and copies ran while one was open for 7% -> 4% of each run, Pallas kernels for 0% -> 0%
where the time goes in v4:
time: 151 us
  starting transfers between devices  62.5 us (41%)
  Pallas kernels  45.4 us (30%)
  waiting for transfers between devices  28.7 us (19%)
  local copies, waits for them, and re-layouts  7.19 us (5%)
  other arithmetic  5.87 us (4%)
    ppermute x32, starting transfers between devices, send(): return lax.ppermute(value, BOTH, pairs)  59 us
    pallas_call x1, Pallas kernels, per_device(): pl.pallas_call(main_kernel, out_shape=(wide, wide, sums_shape, sums_shape...  37.7 us
    ppermute x32, waiting for transfers between devices, send(): return lax.ppermute(value, BOTH, pairs)  28 us
    pallas_call x1, Pallas kernels, per_device(): pl.pallas_call(final_kernel, out_shape=wide, in_specs=[smem] + [anywhere]...  7.7 us
  transfers between devices with their start and end apart: 34, of which 20 were waited for; matrix products, arithmetic and copies ran while one was open for 4% of the time, Pallas kernels for 0%

profile of v4, /device:TPU:1, one launch (start us, length us, event | category | flops | bytes accessed | tf_op | source)
XLA Modules:
  0.0 151.0 jit_solution(17937192588798563733)
XLA Ops:
  6.8 4.2 %collective-permute-start.6 = (bf16[8,32,128]{2,1,0:T(8,128)(2,1)S(1)}, bf16[8,32,128]{2,1,0:T(8,128)(2,1)S(1)}, u32[]{:S(2)}, u32[]{:S(2)}) collective-permute-start(bf16[8,32,128]{2,1,0:T(8,128)(2,1)S(1)} %pad_maximum_fusion.2), channel_id=1, source_target_pairs={{0,15},{16,21},{1,14},{17,20},{2,13},{18,23},{3,12},{19,22},{4,11}... | collective-permute-start | bytes 196616 | tf_op jit(solution)/shard_map/ppermute | solution.py:362
  11.0 3.5 %collective-permute-start.5 = (bf16[8,32,128]{2,1,0:T(8,128)(2,1)S(1)}, bf16[8,32,128]{2,1,0:T(8,128)(2,1)S(1)}, u32[]{:S(2)}, u32[]{:S(2)}) collective-permute-start(bf16[8,32,128]{2,1,0:T(8,128)(2,1)S(1)} %pad_maximum_fusion.2), channel_id=1, source_target_pairs={{0,3},{16,17},{1,2},{17,16},{2,1},{18,19},{3,0},{19,18},{4,7},{20,... | collective-permute-start | bytes 196616 | tf_op jit(solution)/shard_map/ppermute | solution.py:362
  14.6 2.3 %collective-permute-start = (bf16[528,128]{1,0:T(8,128)(2,1)S(1)}, bf16[528,128]{1,0:T(8,128)(2,1)S(1)}, u32[]{:S(2)}, u32[]{:S(2)}) collective-permute-start(bf16[528,128]{1,0:T(8,128)(2,1)S(1)} %fusion.13), channel_id=1, source_target_pairs={{0,1},{1,2},{2,3},{3,4},{4,5},{5,6},{6,7},{7,8},{8,9},{9,10},{10,1... | collective-permute-start | bytes 405512 | tf_op jit(solution)/shard_map/ppermute | solution.py:424
  19.5 4.1 %collective-permute-start.3 = (bf16[80,1152]{1,0:T(8,128)(2,1)S(1)}, bf16[80,1152]{1,0:T(8,128)(2,1)S(1)}, u32[]{:S(2)}, u32[]{:S(2)}) collective-permute-start(bf16[80,1152]{1,0:T(8,128)(2,1)S(1)} %get-tuple-element.33), channel_id=1, source_target_pairs={{0,16},{16,0},{1,17},{17,1},{2,18},{18,2},{3,19},{19,3},{4,20},{20... | collective-permute-start | bytes 552968 | tf_op jit(solution)/shard_map/ppermute | solution.py:362
  23.6 3.0 %collective-permute-start.2 = (bf16[80,1152]{1,0:T(8,128)(2,1)S(1)}, bf16[80,1152]{1,0:T(8,128)(2,1)S(1)}, u32[]{:S(2)}, u32[]{:S(2)}) collective-permute-start(bf16[80,1152]{1,0:T(8,128)(2,1)S(1)} %get-tuple-element.32), channel_id=1, source_target_pairs={{32,16},{33,17},{34,18},{35,19},{36,20},{37,21},{38,22},{39,23},{4... | collective-permute-start | bytes 552968 | tf_op jit(solution)/shard_map/ppermute | solution.py:362
  26.8 8.2 %collective-permute-start.7 = (bf16[32,32,128]{2,1,0:T(8,128)(2,1)S(1)}, bf16[32,32,128]{2,1,0:T(8,128)(2,1)S(1)}, u32[]{:S(2)}, u32[]{:S(2)}) collective-permute-start(bf16[32,32,128]{2,1,0:T(8,128)(2,1)S(1)} %pad_maximum_fusion.refs_2_), channel_id=1, source_target_pairs={{0,4},{16,28},{1,5},{17,29},{2,6},{18,30},{3,7},{19,31},{4,0},{20,... | collective-permute-start | bytes 786440 | tf_op jit(solution)/shard_map/ppermute | solution.py:362
  35.0 2.5 %collective-permute-start.9 = (bf16[32,32,128]{2,1,0:T(8,128)(2,1)S(1)}, bf16[32,32,128]{2,1,0:T(8,128)(2,1)S(1)}, u32[]{:S(2)}, u32[]{:S(2)}) collective-permute-start(bf16[32,32,128]{2,1,0:T(8,128)(2,1)S(1)} %pad_maximum_fusion.refs_2_), channel_id=1, source_target_pairs={{0,5},{16,31},{1,4},{17,30},{2,7},{18,29},{3,6},{19,28},{4,1},{20,... | collective-permute-start | bytes 786440 | tf_op jit(solution)/shard_map/ppermute | solution.py:362
  38.9 5.4 %collective-permute-done.8.refs_4_ = bf16[32,32,128]{2,1,0:T(8,128)(2,1)S(1)} collective-permute-done((bf16[32,32,128]{2,1,0:T(8,128)(2,1)S(1)}, bf16[32,32,128]{2,1,0:T(8,128)(2,1)S(1)}, u32[]{:S(2)}, u32[]{:S(2)}) %collective-permute-start.8) | collective-permute-done | bytes 262176 | tf_op jit(solution)/shard_map/ppermute | solution.py:362
  47.2 37.7 %image_and_gradient.1 = (f32[1024,1024]{1,0:T(8,128)}, f32[1024,1024]{1,0:T(8,128)}, bf16[128,32,128]{2,1,0:T(8,128)(2,1)}, bf16[128,32,128]{2,1,0:T(8,128)(2,1)}) custom-call(s32[653]{0:T(1024)S(1)} %pad_add_fusion.1.refs_0_, f32[8]{0:T(128)S(1)} %copy-done.1, bf16[32,32,128]{2,1,0:T(8,128)(2,1)S(1)} %pad_maximum_fusion.refs_2_, ...), custom_call_target="tpu_custom_call" | custom-call | tf_op jit(solution)/shard_map/image_and_gradient/pallas_call | solution.py:466
  85.2 2.7 %collective-permute-done.14 = bf16[128,32,128]{2,1,0:T(8,128)(2,1)S(1)} collective-permute-done((bf16[128,32,128]{2,1,0:T(8,128)(2,1)}, bf16[128,32,128]{2,1,0:T(8,128)(2,1)S(1)}, u32[]{:S(2)}, u32[]{:S(2)}) %collective-permute-start.14) | collective-permute-done | bytes 1048608 | tf_op jit(solution)/shard_map/ppermute | solution.py:362
  91.3 3.4 %collective-permute-start.15 = (bf16[32,32,128]{2,1,0:T(8,128)(2,1)S(1)}, bf16[32,32,128]{2,1,0:T(8,128)(2,1)S(1)}, u32[]{:S(2)}, u32[]{:S(2)}) collective-permute-start(bf16[32,32,128]{2,1,0:T(8,128)(2,1)S(1)} %get-tuple-element.27), channel_id=1, source_target_pairs={{0,5},{16,31},{1,4},{17,30},{2,7},{18,29},{3,6},{19,28},{4,1},{20,... | collective-permute-start | bytes 786440 | tf_op jit(solution)/shard_map/ppermute | solution.py:362
  97.4 3.8 %collective-permute-done.15 = bf16[32,32,128]{2,1,0:T(8,128)(2,1)S(1)} collective-permute-done((bf16[32,32,128]{2,1,0:T(8,128)(2,1)S(1)}, bf16[32,32,128]{2,1,0:T(8,128)(2,1)S(1)}, u32[]{:S(2)}, u32[]{:S(2)}) %collective-permute-start.15) | collective-permute-done | bytes 262176 | tf_op jit(solution)/shard_map/ppermute | solution.py:362
  101.5 2.5 %collective-permute-start.18 = (bf16[8,32,128]{2,1,0:T(8,128)(2,1)S(1)}, bf16[8,32,128]{2,1,0:T(8,128)(2,1)S(1)}, u32[]{:S(2)}, u32[]{:S(2)}) collective-permute-start(bf16[8,32,128]{2,1,0:T(8,128)(2,1)S(1)} %get-tuple-element.36), channel_id=1, source_target_pairs={{0,15},{16,21},{1,14},{17,20},{2,13},{18,23},{3,12},{19,22},{4,11}... | collective-permute-start | bytes 196616 | tf_op jit(solution)/shard_map/ppermute | solution.py:362
  104.6 2.1 %collective-permute-done.18 = bf16[8,32,128]{2,1,0:T(8,128)(2,1)S(1)} collective-permute-done((bf16[8,32,128]{2,1,0:T(8,128)(2,1)S(1)}, bf16[8,32,128]{2,1,0:T(8,128)(2,1)S(1)}, u32[]{:S(2)}, u32[]{:S(2)}) %collective-permute-start.18) | collective-permute-done | bytes 65568 | tf_op jit(solution)/shard_map/ppermute | solution.py:362
  108.3 2.5 %collective-permute-start.21 = (bf16[8,32,128]{2,1,0:T(8,128)(2,1)S(1)}, bf16[8,32,128]{2,1,0:T(8,128)(2,1)S(1)}, u32[]{:S(2)}, u32[]{:S(2)}) collective-permute-start(bf16[8,32,128]{2,1,0:T(8,128)(2,1)S(1)} %add_convert_fusion.2), channel_id=1, source_target_pairs={{0,64},{16,80},{1,65},{17,81},{2,66},{18,82},{3,67},{19,83},{4,68}... | collective-permute-start | bytes 196616 | tf_op jit(solution)/shard_map/ppermute | solution.py:362
  111.3 1.8 %collective-permute-done.21 = bf16[8,32,128]{2,1,0:T(8,128)(2,1)S(1)} collective-permute-done((bf16[8,32,128]{2,1,0:T(8,128)(2,1)S(1)}, bf16[8,32,128]{2,1,0:T(8,128)(2,1)S(1)}, u32[]{:S(2)}, u32[]{:S(2)}) %collective-permute-start.21) | collective-permute-done | bytes 65568 | tf_op jit(solution)/shard_map/ppermute | solution.py:362
  113.6 2.4 %collective-permute-start.26 = (bf16[8,32,128]{2,1,0:T(8,128)(2,1)S(1)}, bf16[8,32,128]{2,1,0:T(8,128)(2,1)S(1)}, u32[]{:S(2)}, u32[]{:S(2)}) collective-permute-start(bf16[8,32,128]{2,1,0:T(8,128)(2,1)S(1)} %pad_maximum_fusion.3), channel_id=1, source_target_pairs={{0,15},{16,21},{1,14},{17,20},{2,13},{18,23},{3,12},{19,22},{4,11}... | collective-permute-start | bytes 196616 | tf_op jit(solution)/shard_map/ppermute | solution.py:362
  116.4 1.5 %collective-permute-done.26 = bf16[8,32,128]{2,1,0:T(8,128)(2,1)S(1)} collective-permute-done((bf16[8,32,128]{2,1,0:T(8,128)(2,1)S(1)}, bf16[8,32,128]{2,1,0:T(8,128)(2,1)S(1)}, u32[]{:S(2)}, u32[]{:S(2)}) %collective-permute-start.26) | collective-permute-done | bytes 65568 | tf_op jit(solution)/shard_map/ppermute | solution.py:362
  119.3 10.6 %collective-permute-start.30 = (bf16[32,32,128]{2,1,0:T(8,128)(2,1)S(1)}, bf16[32,32,128]{2,1,0:T(8,128)(2,1)S(1)}, u32[]{:S(2)}, u32[]{:S(2)}) collective-permute-start(bf16[32,32,128]{2,1,0:T(8,128)(2,1)S(1)} %pad_maximum_fusion.1.refs_1_), channel_id=1, source_target_pairs={{0,16},{16,0},{1,17},{17,1},{2,18},{18,2},{3,19},{19,3},{4,20},{20... | collective-permute-start | bytes 786440 | tf_op jit(solution)/shard_map/ppermute | solution.py:362
  130.5 1.9 %collective-permute-start.28 = (bf16[32,32,128]{2,1,0:T(8,128)(2,1)S(1)}, bf16[32,32,128]{2,1,0:T(8,128)(2,1)S(1)}, u32[]{:S(2)}, u32[]{:S(2)}) collective-permute-start(bf16[32,32,128]{2,1,0:T(8,128)(2,1)S(1)} %pad_maximum_fusion.1.refs_1_), channel_id=1, source_target_pairs={{0,1},{16,19},{1,0},{17,18},{2,3},{18,17},{3,2},{19,16},{4,5},{20,... | collective-permute-start | bytes 786440 | tf_op jit(solution)/shard_map/ppermute | solution.py:362
  132.3 2.8 %collective-permute-start.29 = (bf16[32,32,128]{2,1,0:T(8,128)(2,1)S(1)}, bf16[32,32,128]{2,1,0:T(8,128)(2,1)S(1)}, u32[]{:S(2)}, u32[]{:S(2)}) collective-permute-start(bf16[32,32,128]{2,1,0:T(8,128)(2,1)S(1)} %pad_maximum_fusion.1.refs_1_), channel_id=1, source_target_pairs={{0,5},{16,31},{1,4},{17,30},{2,7},{18,29},{3,6},{19,28},{4,1},{20,... | collective-permute-start | bytes 786440 | tf_op jit(solution)/shard_map/ppermute | solution.py:362
  137.0 2.3 %collective-permute-start.32 = (bf16[32,32,128]{2,1,0:T(8,128)(2,1)S(1)}, bf16[32,32,128]{2,1,0:T(8,128)(2,1)S(1)}, u32[]{:S(2)}, u32[]{:S(2)}) collective-permute-start(bf16[32,32,128]{2,1,0:T(8,128)(2,1)S(1)} %collective-permute-done.28.refs_3_), channel_id=1, source_target_pairs={{0,16},{16,0},{1,17},{17,1},{2,18},{18,2},{3,19},{19,3},{4,20},{20... | collective-permute-start | bytes 786440 | tf_op jit(solution)/shard_map/ppermute | solution.py:362
  139.3 1.5 %collective-permute-done.29.refs_4_ = bf16[32,32,128]{2,1,0:T(8,128)(2,1)S(1)} collective-permute-done((bf16[32,32,128]{2,1,0:T(8,128)(2,1)S(1)}, bf16[32,32,128]{2,1,0:T(8,128)(2,1)S(1)}, u32[]{:S(2)}, u32[]{:S(2)}) %collective-permute-start.29) | collective-permute-done | bytes 262176 | tf_op jit(solution)/shard_map/ppermute | solution.py:362
  143.1 7.7 %final_mask.1 = f32[1024,1024]{1,0:T(8,128)} custom-call(s32[653]{0:T(1024)S(1)} %pad_add_fusion.1.refs_0_, bf16[32,32,128]{2,1,0:T(8,128)(2,1)S(1)} %pad_maximum_fusion.1.refs_1_, bf16[32,32,128]{2,1,0:T(8,128)(2,1)S(1)} %collective-permute-done.27.refs_2_, bf16[32,32,128]{2,1,0:T(8,128)(2,1)S(1)} %collective-permute-done.28.refs_3_, ...), custom_call_target="tpu_custom_call" | custom-call | tf_op jit(solution)/shard_map/final_mask/pallas_call | solution.py:498
  (118 shorter events, 29.5 us)
Async XLA Ops:
  4.3 13.8 %collective-permute-start.1 = (bf16[528,128]{1,0:T(8,128)(2,1)S(1)}, bf16[528,128]{1,0:T(8,128)(2,1)S(1)}, u32[]{:S(2)}, u32[]{:S(2)}) collective-permute-start(bf16[528,128]{1,0:T(8,128)(2,1)S(1)} %fusion.14), channel_id=1, source_target_pairs={{1,0},{2,1},{3,2},{4,3},{5,4},{6,5},{7,6},{8,7},{9,8},{10,9},{11,1... | collective-permute-start | bytes 405512 | tf_op jit(solution)/shard_map/ppermute | solution.py:425
  6.8 19.9 %collective-permute-start.6 = (bf16[8,32,128]{2,1,0:T(8,128)(2,1)S(1)}, bf16[8,32,128]{2,1,0:T(8,128)(2,1)S(1)}, u32[]{:S(2)}, u32[]{:S(2)}) collective-permute-start(bf16[8,32,128]{2,1,0:T(8,128)(2,1)S(1)} %pad_maximum_fusion.2), channel_id=1, source_target_pairs={{0,15},{16,21},{1,14},{17,20},{2,13},{18,23},{3,12},{19,22},{4,11}... | collective-permute-start | bytes 196616 | tf_op jit(solution)/shard_map/ppermute | solution.py:362
  11.0 15.7 %collective-permute-start.5 = (bf16[8,32,128]{2,1,0:T(8,128)(2,1)S(1)}, bf16[8,32,128]{2,1,0:T(8,128)(2,1)S(1)}, u32[]{:S(2)}, u32[]{:S(2)}) collective-permute-start(bf16[8,32,128]{2,1,0:T(8,128)(2,1)S(1)} %pad_maximum_fusion.2), channel_id=1, source_target_pairs={{0,3},{16,17},{1,2},{17,16},{2,1},{18,19},{3,0},{19,18},{4,7},{20,... | collective-permute-start | bytes 196616 | tf_op jit(solution)/shard_map/ppermute | solution.py:362
  14.5 12.2 %collective-permute-start.4 = (bf16[8,32,128]{2,1,0:T(8,128)(2,1)S(1)}, bf16[8,32,128]{2,1,0:T(8,128)(2,1)S(1)}, u32[]{:S(2)}, u32[]{:S(2)}) collective-permute-start(bf16[8,32,128]{2,1,0:T(8,128)(2,1)S(1)} %pad_maximum_fusion.2), channel_id=1, source_target_pairs={{0,12},{16,20},{1,13},{17,21},{2,14},{18,22},{3,15},{19,23},{4,8},... | collective-permute-start | bytes 196616 | tf_op jit(solution)/shard_map/ppermute | solution.py:362
  19.5 18.0 %collective-permute-start.3 = (bf16[80,1152]{1,0:T(8,128)(2,1)S(1)}, bf16[80,1152]{1,0:T(8,128)(2,1)S(1)}, u32[]{:S(2)}, u32[]{:S(2)}) collective-permute-start(bf16[80,1152]{1,0:T(8,128)(2,1)S(1)} %get-tuple-element.33), channel_id=1, source_target_pairs={{0,16},{16,0},{1,17},{17,1},{2,18},{18,2},{3,19},{19,3},{4,20},{20... | collective-permute-start | bytes 552968 | tf_op jit(solution)/shard_map/ppermute | solution.py:362
  23.6 13.9 %collective-permute-start.2 = (bf16[80,1152]{1,0:T(8,128)(2,1)S(1)}, bf16[80,1152]{1,0:T(8,128)(2,1)S(1)}, u32[]{:S(2)}, u32[]{:S(2)}) collective-permute-start(bf16[80,1152]{1,0:T(8,128)(2,1)S(1)} %get-tuple-element.32), channel_id=1, source_target_pairs={{32,16},{33,17},{34,18},{35,19},{36,20},{37,21},{38,22},{39,23},{4... | collective-permute-start | bytes 552968 | tf_op jit(solution)/shard_map/ppermute | solution.py:362
  26.8 12.0 %collective-permute-start.7 = (bf16[32,32,128]{2,1,0:T(8,128)(2,1)S(1)}, bf16[32,32,128]{2,1,0:T(8,128)(2,1)S(1)}, u32[]{:S(2)}, u32[]{:S(2)}) collective-permute-start(bf16[32,32,128]{2,1,0:T(8,128)(2,1)S(1)} %pad_maximum_fusion.refs_2_), channel_id=1, source_target_pairs={{0,4},{16,28},{1,5},{17,29},{2,6},{18,30},{3,7},{19,31},{4,0},{20,... | collective-permute-start | bytes 786440 | tf_op jit(solution)/shard_map/ppermute | solution.py:362
  35.0 9.2 %collective-permute-start.8 = (bf16[32,32,128]{2,1,0:T(8,128)(2,1)S(1)}, bf16[32,32,128]{2,1,0:T(8,128)(2,1)S(1)}, u32[]{:S(2)}, u32[]{:S(2)}) collective-permute-start(bf16[32,32,128]{2,1,0:T(8,128)(2,1)S(1)} %pad_maximum_fusion.refs_2_), channel_id=1, source_target_pairs={{0,1},{16,19},{1,0},{17,18},{2,3},{18,17},{3,2},{19,16},{4,5},{20,... | collective-permute-start | bytes 786440 | tf_op jit(solution)/shard_map/ppermute | solution.py:362
  35.0 9.2 %collective-permute-start.9 = (bf16[32,32,128]{2,1,0:T(8,128)(2,1)S(1)}, bf16[32,32,128]{2,1,0:T(8,128)(2,1)S(1)}, u32[]{:S(2)}, u32[]{:S(2)}) collective-permute-start(bf16[32,32,128]{2,1,0:T(8,128)(2,1)S(1)} %pad_maximum_fusion.refs_2_), channel_id=1, source_target_pairs={{0,5},{16,31},{1,4},{17,30},{2,7},{18,29},{3,6},{19,28},{4,1},{20,... | collective-permute-start | bytes 786440 | tf_op jit(solution)/shard_map/ppermute | solution.py:362
  37.5 7.4 %collective-permute-start.10 = (bf16[32,32,128]{2,1,0:T(8,128)(2,1)S(1)}, bf16[32,32,128]{2,1,0:T(8,128)(2,1)S(1)}, u32[]{:S(2)}, u32[]{:S(2)}) collective-permute-start(bf16[32,32,128]{2,1,0:T(8,128)(2,1)S(1)} %pad_maximum_fusion.refs_2_), channel_id=1, source_target_pairs={{0,16},{16,0},{1,17},{17,1},{2,18},{18,2},{3,19},{19,3},{4,20},{20... | collective-permute-start | bytes 786440 | tf_op jit(solution)/shard_map/ppermute | solution.py:362
  38.8 6.1 %collective-permute-start.11 = (bf16[32,32,128]{2,1,0:T(8,128)(2,1)S(1)}, bf16[32,32,128]{2,1,0:T(8,128)(2,1)S(1)}, u32[]{:S(2)}, u32[]{:S(2)}) collective-permute-start(bf16[32,32,128]{2,1,0:T(8,128)(2,1)S(1)} %collective-permute-done.7.refs_3_), channel_id=1, source_target_pairs={{0,16},{16,0},{1,17},{17,1},{2,18},{18,2},{3,19},{19,3},{4,20},{20... | collective-permute-start | bytes 786440 | tf_op jit(solution)/shard_map/ppermute | solution.py:362
  89.5 6.5 %collective-permute-start.17 = (bf16[32,32,128]{2,1,0:T(8,128)(2,1)S(1)}, bf16[32,32,128]{2,1,0:T(8,128)(2,1)S(1)}, u32[]{:S(2)}, u32[]{:S(2)}) collective-permute-start(bf16[32,32,128]{2,1,0:T(8,128)(2,1)S(1)} %get-tuple-element.28), channel_id=1, source_target_pairs={{0,1},{16,19},{1,0},{17,18},{2,3},{18,17},{3,2},{19,16},{4,5},{20,... | collective-permute-start | bytes 786440 | tf_op jit(solution)/shard_map/ppermute | solution.py:362
  90.8 6.6 %collective-permute-start.16 = (bf16[32,32,128]{2,1,0:T(8,128)(2,1)S(1)}, bf16[32,32,128]{2,1,0:T(8,128)(2,1)S(1)}, u32[]{:S(2)}, u32[]{:S(2)}) collective-permute-start(bf16[32,32,128]{2,1,0:T(8,128)(2,1)S(1)} %get-tuple-element.29), channel_id=1, source_target_pairs={{0,4},{16,28},{1,5},{17,29},{2,6},{18,30},{3,7},{19,31},{4,0},{20,... | collective-permute-start | bytes 786440 | tf_op jit(solution)/shard_map/ppermute | solution.py:362
  91.3 9.9 %collective-permute-start.15 = (bf16[32,32,128]{2,1,0:T(8,128)(2,1)S(1)}, bf16[32,32,128]{2,1,0:T(8,128)(2,1)S(1)}, u32[]{:S(2)}, u32[]{:S(2)}) collective-permute-start(bf16[32,32,128]{2,1,0:T(8,128)(2,1)S(1)} %get-tuple-element.27), channel_id=1, source_target_pairs={{0,5},{16,31},{1,4},{17,30},{2,7},{18,29},{3,6},{19,28},{4,1},{20,... | collective-permute-start | bytes 786440 | tf_op jit(solution)/shard_map/ppermute | solution.py:362
  101.5 5.2 %collective-permute-start.18 = (bf16[8,32,128]{2,1,0:T(8,128)(2,1)S(1)}, bf16[8,32,128]{2,1,0:T(8,128)(2,1)S(1)}, u32[]{:S(2)}, u32[]{:S(2)}) collective-permute-start(bf16[8,32,128]{2,1,0:T(8,128)(2,1)S(1)} %get-tuple-element.36), channel_id=1, source_target_pairs={{0,15},{16,21},{1,14},{17,20},{2,13},{18,23},{3,12},{19,22},{4,11}... | collective-permute-start | bytes 196616 | tf_op jit(solution)/shard_map/ppermute | solution.py:362
  107.0 4.3 %collective-permute-start.22 = (bf16[8,32,128]{2,1,0:T(8,128)(2,1)S(1)}, bf16[8,32,128]{2,1,0:T(8,128)(2,1)S(1)}, u32[]{:S(2)}, u32[]{:S(2)}) collective-permute-start(bf16[8,32,128]{2,1,0:T(8,128)(2,1)S(1)} %add_convert_fusion.2), channel_id=1, source_target_pairs={{0,32},{16,48},{1,33},{17,49},{2,34},{18,50},{3,35},{19,51},{4,36}... | collective-permute-start | bytes 196616 | tf_op jit(solution)/shard_map/ppermute | solution.py:362
  108.3 4.8 %collective-permute-start.21 = (bf16[8,32,128]{2,1,0:T(8,128)(2,1)S(1)}, bf16[8,32,128]{2,1,0:T(8,128)(2,1)S(1)}, u32[]{:S(2)}, u32[]{:S(2)}) collective-permute-start(bf16[8,32,128]{2,1,0:T(8,128)(2,1)S(1)} %add_convert_fusion.2), channel_id=1, source_target_pairs={{0,64},{16,80},{1,65},{17,81},{2,66},{18,82},{3,67},{19,83},{4,68}... | collective-permute-start | bytes 196616 | tf_op jit(solution)/shard_map/ppermute | solution.py:362
  113.6 4.3 %collective-permute-start.26 = (bf16[8,32,128]{2,1,0:T(8,128)(2,1)S(1)}, bf16[8,32,128]{2,1,0:T(8,128)(2,1)S(1)}, u32[]{:S(2)}, u32[]{:S(2)}) collective-permute-start(bf16[8,32,128]{2,1,0:T(8,128)(2,1)S(1)} %pad_maximum_fusion.3), channel_id=1, source_target_pairs={{0,15},{16,21},{1,14},{17,20},{2,13},{18,23},{3,12},{19,22},{4,11}... | collective-permute-start | bytes 196616 | tf_op jit(solution)/shard_map/ppermute | solution.py:362
  119.3 15.9 %collective-permute-start.30 = (bf16[32,32,128]{2,1,0:T(8,128)(2,1)S(1)}, bf16[32,32,128]{2,1,0:T(8,128)(2,1)S(1)}, u32[]{:S(2)}, u32[]{:S(2)}) collective-permute-start(bf16[32,32,128]{2,1,0:T(8,128)(2,1)S(1)} %pad_maximum_fusion.1.refs_1_), channel_id=1, source_target_pairs={{0,16},{16,0},{1,17},{17,1},{2,18},{18,2},{3,19},{19,3},{4,20},{20... | collective-permute-start | bytes 786440 | tf_op jit(solution)/shard_map/ppermute | solution.py:362
  130.0 6.6 %collective-permute-start.27 = (bf16[32,32,128]{2,1,0:T(8,128)(2,1)S(1)}, bf16[32,32,128]{2,1,0:T(8,128)(2,1)S(1)}, u32[]{:S(2)}, u32[]{:S(2)}) collective-permute-start(bf16[32,32,128]{2,1,0:T(8,128)(2,1)S(1)} %pad_maximum_fusion.1.refs_1_), channel_id=1, source_target_pairs={{0,4},{16,28},{1,5},{17,29},{2,6},{18,30},{3,7},{19,31},{4,0},{20,... | collective-permute-start | bytes 786440 | tf_op jit(solution)/shard_map/ppermute | solution.py:362
  130.5 6.6 %collective-permute-start.28 = (bf16[32,32,128]{2,1,0:T(8,128)(2,1)S(1)}, bf16[32,32,128]{2,1,0:T(8,128)(2,1)S(1)}, u32[]{:S(2)}, u32[]{:S(2)}) collective-permute-start(bf16[32,32,128]{2,1,0:T(8,128)(2,1)S(1)} %pad_maximum_fusion.1.refs_1_), channel_id=1, source_target_pairs={{0,1},{16,19},{1,0},{17,18},{2,3},{18,17},{3,2},{19,16},{4,5},{20,... | collective-permute-start | bytes 786440 | tf_op jit(solution)/shard_map/ppermute | solution.py:362
  132.3 8.5 %collective-permute-start.29 = (bf16[32,32,128]{2,1,0:T(8,128)(2,1)S(1)}, bf16[32,32,128]{2,1,0:T(8,128)(2,1)S(1)}, u32[]{:S(2)}, u32[]{:S(2)}) collective-permute-start(bf16[32,32,128]{2,1,0:T(8,128)(2,1)S(1)} %pad_maximum_fusion.1.refs_1_), channel_id=1, source_target_pairs={{0,5},{16,31},{1,4},{17,30},{2,7},{18,29},{3,6},{19,28},{4,1},{20,... | collective-permute-start | bytes 786440 | tf_op jit(solution)/shard_map/ppermute | solution.py:362
  136.6 5.0 %collective-permute-start.31 = (bf16[32,32,128]{2,1,0:T(8,128)(2,1)S(1)}, bf16[32,32,128]{2,1,0:T(8,128)(2,1)S(1)}, u32[]{:S(2)}, u32[]{:S(2)}) collective-permute-start(bf16[32,32,128]{2,1,0:T(8,128)(2,1)S(1)} %collective-permute-done.27.refs_2_), channel_id=1, source_target_pairs={{0,16},{16,0},{1,17},{17,1},{2,18},{18,2},{3,19},{19,3},{4,20},{20... | collective-permute-start | bytes 786440 | tf_op jit(solution)/shard_map/ppermute | solution.py:362
  137.0 4.6 %collective-permute-start.32 = (bf16[32,32,128]{2,1,0:T(8,128)(2,1)S(1)}, bf16[32,32,128]{2,1,0:T(8,128)(2,1)S(1)}, u32[]{:S(2)}, u32[]{:S(2)}) collective-permute-start(bf16[32,32,128]{2,1,0:T(8,128)(2,1)S(1)} %collective-permute-done.28.refs_3_), channel_id=1, source_target_pairs={{0,16},{16,0},{1,17},{17,1},{2,18},{18,2},{3,19},{19,3},{4,20},{20... | collective-permute-start | bytes 786440 | tf_op jit(solution)/shard_map/ppermute | solution.py:362
  (20 other events, 211.9 us)

commit v5 on v4

--- a/solution.py
+++ b/solution.py
@@ -110,11 +110,12 @@
     near_strip, far_strip, before, after = refs[10:14]
     free_in, target_in = refs[14:16]
     table_in = refs[16:30]
-    resist_out, free_out, own_out, other_out = refs[30:34]
-    cells, mask, shading, fields, amps, halves, sums, free, target = refs[34:43]
-    tables = refs[43:57]
-    parts = refs[57:65]
-    free_sems, table_sems, target_sem, resist_sems, out_sems, part_sems = refs[65:71]
+    resist_out, free_out = refs[30:32]
+    sum_outs = refs[32:40]
+    cells, mask, shading, fields, amps, halves, sums, free, target = refs[40:49]
+    tables = refs[49:63]
+    parts = refs[63:71]
+    free_sems, table_sems, target_sem, resist_sems, out_sems, part_sems = refs[71:77]
     (spectra, gain, first, second, up_u, up_ut, up_v, up_vt, fine, fine_lo, fine_t, fine_tlo, out_v, out_u) = tables
 
     part_loads = [pltpu.make_async_copy(a, b, part_sems.at[n]) for n, (a, b) in enumerate(zip(part_in, parts))]
@@ -202,16 +203,18 @@
             k_re, k_im = spectra[0, :, at], spectra[1, :, at]
             amps[0:128, at] = (k_re * spec_re - k_im * spec_im).astype(BF16)
             amps[128:256, at] = (k_re * spec_im + k_im * spec_re).astype(BF16)
-        halves[...] = dot(up_u[...], amps[...]).astype(BF16)
+        half = dot(up_u[...], amps[...]).astype(BF16)
+        left = jnp.concatenate(
+            [jnp.concatenate([half[0:256, k * 128 : k * 128 + 128], half[256:512, k * 128 : k * 128 + 128]], axis=1) for k in range(NK)],
+            axis=0,
+        )
+        fields[...] = dot(left, up_v[...]).reshape(NK, GRID, 2 * GRID)
         intensity = jnp.zeros((GRID, GRID), F32)
         for k in range(NK):
             at = slice(k * 128, k * 128 + 128)
-            left = jnp.concatenate([halves[0:256, at], halves[256:512, at]], axis=1)
-            field = dot(left, up_v[...]) * (1.0 / BAND)
-            fields[k] = field
-            re, im = field[:, :256], field[:, 256:]
+            re, im = fields[k, :, :256], fields[k, :, 256:]
             intensity = intensity + weights[k] * (re * re + im * im)
-        coarse = intensity.astype(BF16)
+        coarse = (intensity * (1.0 / BAND**2)).astype(BF16)
         half_fine = dot(fine[...], coarse) + dot(fine_lo[...], coarse)
         half_fine = half_fine.astype(BF16)
         image = dot(half_fine, fine_t[...]) + dot(half_fine, fine_tlo[...])
@@ -226,7 +229,7 @@
         back = dot(fine_t[...], dot(slopes, fine[...]).astype(BF16))
         for k in range(NK):
             at = slice(k * 128, k * 128 + 128)
-            scaled = back * (weights[k] * (2.0 / BAND))
+            scaled = back * (weights[k] * (2.0 / BAND**2))
             both = jnp.concatenate(
                 [(scaled * fields[k, :, :256]).astype(BF16), (scaled * fields[k, :, 256:]).astype(BF16)], axis=1
             )
@@ -278,15 +281,15 @@
         return 0
 
     lax.fori_loop(0, 16, collect, 0)
-    for out, base in ((own_out, 0), (other_out, 128)):
+    for part, out in enumerate(sum_outs):
 
         def join(n, _):
-            at = pl.ds(base + n * 8, 8)
-            rolled = pltpu.roll(sums[pl.ds(256 + base + n * 8, 8)].reshape(256, 128), 64, 1)
-            out[pl.ds(n * 8, 8)] = (sums[at].reshape(256, 128) + rolled).reshape(8, 32, 128).astype(BF16)
+            at = part * 32 + n * 8
+            rolled = pltpu.roll(sums[pl.ds(256 + at, 8)].reshape(256, 128), 64, 1)
+            out[pl.ds(n * 8, 8)] = (sums[pl.ds(at, 8)].reshape(256, 128) + rolled).reshape(8, 32, 128).astype(BF16)
             return 0
 
-        lax.fori_loop(0, 16, join, 0)
+        lax.fori_loop(0, 4, join, 0)
 
     for t in range(4):
         at = (pl.ds(t // 2 * TILE, TILE), pl.ds(t % 2 * TILE, TILE))
@@ -374,7 +377,8 @@
 
 
 def scattered_sum(own, other):
-    total = (own.astype(F32) + send(other, SWAP).astype(F32)).astype(BF16).reshape(4, 32, 32, 128)
+    swapped = {n: send(other[n], SWAP) for n in (3, 1, 2, 0)}
+    total = {n: (own[n].astype(F32) + swapped[n].astype(F32)).astype(BF16) for n in (3, 1, 2, 0)}
     got = [send(total[n], far(n)) for n in (3, 1, 2)]
     total = sum((g.astype(F32) for g in got), total[0].astype(F32)).astype(BF16).reshape(4, 8, 32, 128)
     got = [send(total[n], near(n)) for n in (3, 1, 2)]
@@ -408,10 +412,16 @@
     row, col = lax.axis_index("row"), lax.axis_index("col")
     core, y, z = row % 2, col // 4, col % 4
     own_cells = lax.dynamic_slice_in_dim(masters, core * 8, 8, 0)
-    group = gathered_near(to_wire(own_cells.astype(BF16)))
+    piece, tile_free_late = lax.optimization_barrier((to_wire(own_cells.astype(BF16)), tile_free))
+    group = gathered_near(piece)
 
     edges = lax.optimization_barrier(
-        (tile_free[:64], tile_free[SIDE - 64 :], tile_free[:, :64], tile_free[:, SIDE - 64 :])
+        (
+            tile_free_late[:64],
+            tile_free_late[SIDE - 64 :],
+            tile_free_late[:, :64],
+            tile_free_late[:, SIDE - 64 :],
+        )
     )
     insts = jnp.stack([inst_master, inst_orient])
 
@@ -461,13 +471,13 @@
     vmem, smem = pl.BlockSpec(memory_space=pltpu.VMEM), pl.BlockSpec(memory_space=pltpu.SMEM)
     anywhere = pl.BlockSpec(memory_space=pl.ANY)
     wide = jax.ShapeDtypeStruct((SIDE, SIDE), F32)
-    sums_shape = jax.ShapeDtypeStruct((128, 32, 128), BF16)
+    sums_shape = jax.ShapeDtypeStruct((32, 32, 128), BF16)
     tables = [spectra.reshape(2, BAND, NK * BAND), *constant_tables()]
-    resist, free_new, own, other = pl.pallas_call(
+    resist, free_new, *sums = pl.pallas_call(
         main_kernel,
-        out_shape=(wide, wide, sums_shape, sums_shape),
+        out_shape=(wide, wide, *[sums_shape] * 8),
         in_specs=[smem] * 2 + [anywhere] * 8 + [vmem] * 4 + [anywhere] * (2 + len(tables)),
-        out_specs=(anywhere, anywhere, vmem, vmem),
+        out_specs=(anywhere, anywhere, *[vmem] * 8),
         scratch_shapes=[
             pltpu.VMEM((512, 32, 128), F32),
             pltpu.VMEM((1152, 1152), BF16),
@@ -491,7 +501,7 @@
         name="image_and_gradient",
     )(codes, weights, *parts, near_strip, far_strip, before, after, tile_free, target, *tables)
 
-    summed = scattered_sum(own, other)
+    summed = scattered_sum(sums[:4], sums[4:])
     fresh = smooth(own_cells.reshape(8, CELL, CELL) - 0.05 * from_wire(summed))
     fresh_wire = jnp.concatenate([fresh[:, :32, :], fresh[:, 32:, :]], axis=2).astype(BF16)
     parts = gathered_far(gathered_near(fresh_wire))

time: 151 us -> 147 us (0.974)
  waiting for transfers between devices: 28.7 us -> 26.9 us
    ppermute x32 -> x35, starting transfers between devices: 59 us -> 56.9 us  [send(): return lax.ppermute(value, BOTH, pairs)]
    ppermute x1, starting transfers between devices: 2.29 us -> 3.99 us  [per_device(): before = lax.ppermute(side(edges[3], 15), 'col', up)]
    ppermute x32 -> x35, waiting for transfers between devices: 28 us -> 26.4 us  [send(): return lax.ppermute(value, BOTH, pairs)]
  transfers between devices with their start and end apart: 34 -> 37, of which waited for: 20 -> 20; matrix products, arithmetic and copies ran while one was open for 4% -> 5% of each run, Pallas kernels for 0% -> 0%
where the time goes in v5:
time: 147 us
  starting transfers between devices  62.2 us (42%)
  Pallas kernels  44.8 us (30%)
  waiting for transfers between devices  26.9 us (18%)
  local copies, waits for them, and re-layouts  7.03 us (5%)
  other arithmetic  4.62 us (3%)
    ppermute x35, starting transfers between devices, send(): return lax.ppermute(value, BOTH, pairs)  56.9 us
    pallas_call x1, Pallas kernels, per_device(): pl.pallas_call(main_kernel, out_shape=(wide, wide, *[sums_shape] * 8), in...  37.1 us
    ppermute x35, waiting for transfers between devices, send(): return lax.ppermute(value, BOTH, pairs)  26.4 us
    pallas_call x1, Pallas kernels, per_device(): pl.pallas_call(final_kernel, out_shape=wide, in_specs=[smem] + [anywhere]...  7.7 us
    ppermute x1, starting transfers between devices, per_device(): before = lax.ppermute(side(edges[3], 15), 'col', up)  3.99 us
  transfers between devices with their start and end apart: 37, of which 20 were waited for; matrix products, arithmetic and copies ran while one was open for 5% of the time, Pallas kernels for 0%

profile of v5, /device:TPU:1, one launch (start us, length us, event | category | flops | bytes accessed | tf_op | source)
XLA Modules:
  0.0 146.9 jit_solution(3840523517020527862)
XLA Ops:
  2.0 2.2 %collective-permute-start.4 = (bf16[8,32,128]{2,1,0:T(8,128)(2,1)S(1)}, bf16[8,32,128]{2,1,0:T(8,128)(2,1)S(1)}, u32[]{:S(2)}, u32[]{:S(2)}) collective-permute-start(bf16[8,32,128]{2,1,0:T(8,128)(2,1)S(1)} %pad_maximum_fusion.1), channel_id=1, source_target_pairs={{0,12},{16,20},{1,13},{17,21},{2,14},{18,22},{3,15},{19,23},{4,8},... | collective-permute-start | bytes 196616 | tf_op jit(solution)/shard_map/ppermute | solution.py:365
  4.2 1.6 %collective-permute-start.5 = (bf16[8,32,128]{2,1,0:T(8,128)(2,1)S(1)}, bf16[8,32,128]{2,1,0:T(8,128)(2,1)S(1)}, u32[]{:S(2)}, u32[]{:S(2)}) collective-permute-start(bf16[8,32,128]{2,1,0:T(8,128)(2,1)S(1)} %pad_maximum_fusion.1), channel_id=1, source_target_pairs={{0,3},{16,17},{1,2},{17,16},{2,1},{18,19},{3,0},{19,18},{4,7},{20,... | collective-permute-start | bytes 196616 | tf_op jit(solution)/shard_map/ppermute | solution.py:365
  10.8 4.0 %collective-permute-start = (bf16[528,128]{1,0:T(8,128)(2,1)S(1)}, bf16[528,128]{1,0:T(8,128)(2,1)S(1)}, u32[]{:S(2)}, u32[]{:S(2)}) collective-permute-start(bf16[528,128]{1,0:T(8,128)(2,1)S(1)} %fusion.13), channel_id=1, source_target_pairs={{0,1},{1,2},{2,3},{3,4},{4,5},{5,6},{6,7},{7,8},{8,9},{9,10},{10,1... | collective-permute-start | bytes 405512 | tf_op jit(solution)/shard_map/ppermute | solution.py:434
  17.3 6.0 %collective-permute-start.3 = (bf16[80,1152]{1,0:T(8,128)(2,1)S(1)}, bf16[80,1152]{1,0:T(8,128)(2,1)S(1)}, u32[]{:S(2)}, u32[]{:S(2)}) collective-permute-start(bf16[80,1152]{1,0:T(8,128)(2,1)S(1)} %get-tuple-element.46), channel_id=1, source_target_pairs={{0,16},{16,0},{1,17},{17,1},{2,18},{18,2},{3,19},{19,3},{4,20},{20... | collective-permute-start | bytes 552968 | tf_op jit(solution)/shard_map/ppermute | solution.py:365
  23.4 3.0 %collective-permute-start.2 = (bf16[80,1152]{1,0:T(8,128)(2,1)S(1)}, bf16[80,1152]{1,0:T(8,128)(2,1)S(1)}, u32[]{:S(2)}, u32[]{:S(2)}) collective-permute-start(bf16[80,1152]{1,0:T(8,128)(2,1)S(1)} %get-tuple-element.45), channel_id=1, source_target_pairs={{32,16},{33,17},{34,18},{35,19},{36,20},{37,21},{38,22},{39,23},{4... | collective-permute-start | bytes 552968 | tf_op jit(solution)/shard_map/ppermute | solution.py:365
  26.4 7.2 %collective-permute-start.7 = (bf16[32,32,128]{2,1,0:T(8,128)(2,1)S(1)}, bf16[32,32,128]{2,1,0:T(8,128)(2,1)S(1)}, u32[]{:S(2)}, u32[]{:S(2)}) collective-permute-start(bf16[32,32,128]{2,1,0:T(8,128)(2,1)S(1)} %constant_dynamic-update-slice_fusion.refs_2_), channel_id=1, source_target_pairs={{0,4},{16,28},{1,5},{17,29},{2,6},{18,30},{3,7},{19,31},{4,0},{20,... | collective-permute-start | bytes 786440 | tf_op jit(solution)/shard_map/ppermute | solution.py:365
  33.7 2.5 %collective-permute-start.9 = (bf16[32,32,128]{2,1,0:T(8,128)(2,1)S(1)}, bf16[32,32,128]{2,1,0:T(8,128)(2,1)S(1)}, u32[]{:S(2)}, u32[]{:S(2)}) collective-permute-start(bf16[32,32,128]{2,1,0:T(8,128)(2,1)S(1)} %constant_dynamic-update-slice_fusion.refs_2_), channel_id=1, source_target_pairs={{0,5},{16,31},{1,4},{17,30},{2,7},{18,29},{3,6},{19,28},{4,1},{20,... | collective-permute-start | bytes 786440 | tf_op jit(solution)/shard_map/ppermute | solution.py:365
  37.6 5.3 %collective-permute-done.8.refs_4_ = bf16[32,32,128]{2,1,0:T(8,128)(2,1)S(1)} collective-permute-done((bf16[32,32,128]{2,1,0:T(8,128)(2,1)S(1)}, bf16[32,32,128]{2,1,0:T(8,128)(2,1)S(1)}, u32[]{:S(2)}, u32[]{:S(2)}) %collective-permute-start.8) | collective-permute-done | bytes 262176 | tf_op jit(solution)/shard_map/ppermute | solution.py:365
  45.8 37.1 %image_and_gradient.1 = (f32[1024,1024]{1,0:T(8,128)}, f32[1024,1024]{1,0:T(8,128)}, bf16[32,32,128]{2,1,0:T(8,128)(2,1)S(1)}, bf16[32,32,128]{2,1,0:T(8,128)(2,...) custom-call(s32[653]{0:T(1024)S(1)} %pad_add_fusion.1.refs_0_, ...), custom_call_target="tpu_custom_call" | custom-call | tf_op jit(solution)/shard_map/image_and_gradient/pallas_call | solution.py:476
  86.9 3.4 %collective-permute-start.16 = (bf16[32,32,128]{2,1,0:T(8,128)(2,1)S(1)}, bf16[32,32,128]{2,1,0:T(8,128)(2,1)S(1)}, u32[]{:S(2)}, u32[]{:S(2)}) collective-permute-start(bf16[32,32,128]{2,1,0:T(8,128)(2,1)S(1)} %add_convert_fusion.3), channel_id=1, source_target_pairs={{0,5},{16,31},{1,4},{17,30},{2,7},{18,29},{3,6},{19,28},{4,1},{20,... | collective-permute-start | bytes 786440 | tf_op jit(solution)/shard_map/ppermute | solution.py:365
  91.4 1.6 %collective-permute-done.18 = bf16[32,32,128]{2,1,0:T(8,128)(2,1)S(1)} collective-permute-done((bf16[32,32,128]{2,1,0:T(8,128)(2,1)S(1)}, bf16[32,32,128]{2,1,0:T(8,128)(2,1)S(1)}, u32[]{:S(2)}, u32[]{:S(2)}) %collective-permute-start.18) | collective-permute-done | bytes 262176 | tf_op jit(solution)/shard_map/ppermute | solution.py:365
  93.0 3.7 %collective-permute-done.16 = bf16[32,32,128]{2,1,0:T(8,128)(2,1)S(1)} collective-permute-done((bf16[32,32,128]{2,1,0:T(8,128)(2,1)S(1)}, bf16[32,32,128]{2,1,0:T(8,128)(2,1)S(1)}, u32[]{:S(2)}, u32[]{:S(2)}) %collective-permute-start.16) | collective-permute-done | bytes 262176 | tf_op jit(solution)/shard_map/ppermute | solution.py:365
  97.1 2.5 %collective-permute-start.21 = (bf16[8,32,128]{2,1,0:T(8,128)(2,1)S(1)}, bf16[8,32,128]{2,1,0:T(8,128)(2,1)S(1)}, u32[]{:S(2)}, u32[]{:S(2)}) collective-permute-start(bf16[8,32,128]{2,1,0:T(8,128)(2,1)S(1)} %get-tuple-element.49), channel_id=1, source_target_pairs={{0,15},{16,21},{1,14},{17,20},{2,13},{18,23},{3,12},{19,22},{4,11}... | collective-permute-start | bytes 196616 | tf_op jit(solution)/shard_map/ppermute | solution.py:365
  100.2 2.1 %collective-permute-done.21 = bf16[8,32,128]{2,1,0:T(8,128)(2,1)S(1)} collective-permute-done((bf16[8,32,128]{2,1,0:T(8,128)(2,1)S(1)}, bf16[8,32,128]{2,1,0:T(8,128)(2,1)S(1)}, u32[]{:S(2)}, u32[]{:S(2)}) %collective-permute-start.21) | collective-permute-done | bytes 65568 | tf_op jit(solution)/shard_map/ppermute | solution.py:365
  103.9 2.4 %collective-permute-start.24 = (bf16[8,32,128]{2,1,0:T(8,128)(2,1)S(1)}, bf16[8,32,128]{2,1,0:T(8,128)(2,1)S(1)}, u32[]{:S(2)}, u32[]{:S(2)}) collective-permute-start(bf16[8,32,128]{2,1,0:T(8,128)(2,1)S(1)} %add_convert_fusion.5), channel_id=1, source_target_pairs={{0,64},{16,80},{1,65},{17,81},{2,66},{18,82},{3,67},{19,83},{4,68}... | collective-permute-start | bytes 196616 | tf_op jit(solution)/shard_map/ppermute | solution.py:365
  106.5 1.6 %collective-permute-done.25 = bf16[8,32,128]{2,1,0:T(8,128)(2,1)S(1)} collective-permute-done((bf16[8,32,128]{2,1,0:T(8,128)(2,1)S(1)}, bf16[8,32,128]{2,1,0:T(8,128)(2,1)S(1)}, u32[]{:S(2)}, u32[]{:S(2)}) %collective-permute-start.25) | collective-permute-done | bytes 65568 | tf_op jit(solution)/shard_map/ppermute | solution.py:365
  109.3 3.4 %collective-permute-start.29 = (bf16[8,32,128]{2,1,0:T(8,128)(2,1)S(1)}, bf16[8,32,128]{2,1,0:T(8,128)(2,1)S(1)}, u32[]{:S(2)}, u32[]{:S(2)}) collective-permute-start(bf16[8,32,128]{2,1,0:T(8,128)(2,1)S(1)} %pad_maximum_fusion.2), channel_id=1, source_target_pairs={{0,15},{16,21},{1,14},{17,20},{2,13},{18,23},{3,12},{19,22},{4,11}... | collective-permute-start | bytes 196616 | tf_op jit(solution)/shard_map/ppermute | solution.py:365
  114.4 1.5 collective-permute-done.28
  115.9 9.5 %collective-permute-start.33 = (bf16[32,32,128]{2,1,0:T(8,128)(2,1)S(1)}, bf16[32,32,128]{2,1,0:T(8,128)(2,1)S(1)}, u32[]{:S(2)}, u32[]{:S(2)}) collective-permute-start(bf16[32,32,128]{2,1,0:T(8,128)(2,1)S(1)} %pad_maximum_fusion.refs_1_), channel_id=1, source_target_pairs={{0,16},{16,0},{1,17},{17,1},{2,18},{18,2},{3,19},{19,3},{4,20},{20... | collective-permute-start | bytes 786440 | tf_op jit(solution)/shard_map/ppermute | solution.py:365
  126.1 2.1 %collective-permute-start.31 = (bf16[32,32,128]{2,1,0:T(8,128)(2,1)S(1)}, bf16[32,32,128]{2,1,0:T(8,128)(2,1)S(1)}, u32[]{:S(2)}, u32[]{:S(2)}) collective-permute-start(bf16[32,32,128]{2,1,0:T(8,128)(2,1)S(1)} %pad_maximum_fusion.refs_1_), channel_id=1, source_target_pairs={{0,1},{16,19},{1,0},{17,18},{2,3},{18,17},{3,2},{19,16},{4,5},{20,... | collective-permute-start | bytes 786440 | tf_op jit(solution)/shard_map/ppermute | solution.py:365
  128.2 2.5 %collective-permute-start.32 = (bf16[32,32,128]{2,1,0:T(8,128)(2,1)S(1)}, bf16[32,32,128]{2,1,0:T(8,128)(2,1)S(1)}, u32[]{:S(2)}, u32[]{:S(2)}) collective-permute-start(bf16[32,32,128]{2,1,0:T(8,128)(2,1)S(1)} %pad_maximum_fusion.refs_1_), channel_id=1, source_target_pairs={{0,5},{16,31},{1,4},{17,30},{2,7},{18,29},{3,6},{19,28},{4,1},{20,... | collective-permute-start | bytes 786440 | tf_op jit(solution)/shard_map/ppermute | solution.py:365
  132.7 2.3 %collective-permute-start.35 = (bf16[32,32,128]{2,1,0:T(8,128)(2,1)S(1)}, bf16[32,32,128]{2,1,0:T(8,128)(2,1)S(1)}, u32[]{:S(2)}, u32[]{:S(2)}) collective-permute-start(bf16[32,32,128]{2,1,0:T(8,128)(2,1)S(1)} %collective-permute-done.31.refs_3_), channel_id=1, source_target_pairs={{0,16},{16,0},{1,17},{17,1},{2,18},{18,2},{3,19},{19,3},{4,20},{20... | collective-permute-start | bytes 786440 | tf_op jit(solution)/shard_map/ppermute | solution.py:365
  135.0 1.8 %collective-permute-done.32.refs_4_ = bf16[32,32,128]{2,1,0:T(8,128)(2,1)S(1)} collective-permute-done((bf16[32,32,128]{2,1,0:T(8,128)(2,1)S(1)}, bf16[32,32,128]{2,1,0:T(8,128)(2,1)S(1)}, u32[]{:S(2)}, u32[]{:S(2)}) %collective-permute-start.32) | collective-permute-done | bytes 262176 | tf_op jit(solution)/shard_map/ppermute | solution.py:365
  139.0 7.7 %final_mask.1 = f32[1024,1024]{1,0:T(8,128)} custom-call(s32[653]{0:T(1024)S(1)} %pad_add_fusion.1.refs_0_, bf16[32,32,128]{2,1,0:T(8,128)(2,1)S(1)} %pad_maximum_fusion.refs_1_, bf16[32,32,128]{2,1,0:T(8,128)(2,1)S(1)} %collective-permute-done.30.refs_2_, bf16[32,32,128]{2,1,0:T(8,128)(2,1)S(1)} %collective-permute-done.31.refs_3_, ...), custom_call_target="tpu_custom_call" | custom-call | tf_op jit(solution)/shard_map/final_mask/pallas_call | solution.py:508
  (138 shorter events, 28.3 us)
Async XLA Ops:
  2.0 14.0 %collective-permute-start.4 = (bf16[8,32,128]{2,1,0:T(8,128)(2,1)S(1)}, bf16[8,32,128]{2,1,0:T(8,128)(2,1)S(1)}, u32[]{:S(2)}, u32[]{:S(2)}) collective-permute-start(bf16[8,32,128]{2,1,0:T(8,128)(2,1)S(1)} %pad_maximum_fusion.1), channel_id=1, source_target_pairs={{0,12},{16,20},{1,13},{17,21},{2,14},{18,22},{3,15},{19,23},{4,8},... | collective-permute-start | bytes 196616 | tf_op jit(solution)/shard_map/ppermute | solution.py:365
  4.2 22.1 %collective-permute-start.5 = (bf16[8,32,128]{2,1,0:T(8,128)(2,1)S(1)}, bf16[8,32,128]{2,1,0:T(8,128)(2,1)S(1)}, u32[]{:S(2)}, u32[]{:S(2)}) collective-permute-start(bf16[8,32,128]{2,1,0:T(8,128)(2,1)S(1)} %pad_maximum_fusion.1), channel_id=1, source_target_pairs={{0,3},{16,17},{1,2},{17,16},{2,1},{18,19},{3,0},{19,18},{4,7},{20,... | collective-permute-start | bytes 196616 | tf_op jit(solution)/shard_map/ppermute | solution.py:365
  5.9 20.5 %collective-permute-start.6 = (bf16[8,32,128]{2,1,0:T(8,128)(2,1)S(1)}, bf16[8,32,128]{2,1,0:T(8,128)(2,1)S(1)}, u32[]{:S(2)}, u32[]{:S(2)}) collective-permute-start(bf16[8,32,128]{2,1,0:T(8,128)(2,1)S(1)} %pad_maximum_fusion.1), channel_id=1, source_target_pairs={{0,15},{16,21},{1,14},{17,20},{2,13},{18,23},{3,12},{19,22},{4,11}... | collective-permute-start | bytes 196616 | tf_op jit(solution)/shard_map/ppermute | solution.py:365
  9.3 6.7 %collective-permute-start.1 = (bf16[528,128]{1,0:T(8,128)(2,1)S(1)}, bf16[528,128]{1,0:T(8,128)(2,1)S(1)}, u32[]{:S(2)}, u32[]{:S(2)}) collective-permute-start(bf16[528,128]{1,0:T(8,128)(2,1)S(1)} %fusion.14), channel_id=1, source_target_pairs={{1,0},{2,1},{3,2},{4,3},{5,4},{6,5},{7,6},{8,7},{9,8},{10,9},{11,1... | collective-permute-start | bytes 405512 | tf_op jit(solution)/shard_map/ppermute | solution.py:435
  10.8 6.0 %collective-permute-start = (bf16[528,128]{1,0:T(8,128)(2,1)S(1)}, bf16[528,128]{1,0:T(8,128)(2,1)S(1)}, u32[]{:S(2)}, u32[]{:S(2)}) collective-permute-start(bf16[528,128]{1,0:T(8,128)(2,1)S(1)} %fusion.13), channel_id=1, source_target_pairs={{0,1},{1,2},{2,3},{3,4},{4,5},{5,6},{6,7},{7,8},{8,9},{9,10},{10,1... | collective-permute-start | bytes 405512 | tf_op jit(solution)/shard_map/ppermute | solution.py:434
  17.3 18.8 %collective-permute-start.3 = (bf16[80,1152]{1,0:T(8,128)(2,1)S(1)}, bf16[80,1152]{1,0:T(8,128)(2,1)S(1)}, u32[]{:S(2)}, u32[]{:S(2)}) collective-permute-start(bf16[80,1152]{1,0:T(8,128)(2,1)S(1)} %get-tuple-element.46), channel_id=1, source_target_pairs={{0,16},{16,0},{1,17},{17,1},{2,18},{18,2},{3,19},{19,3},{4,20},{20... | collective-permute-start | bytes 552968 | tf_op jit(solution)/shard_map/ppermute | solution.py:365
  23.4 12.8 %collective-permute-start.2 = (bf16[80,1152]{1,0:T(8,128)(2,1)S(1)}, bf16[80,1152]{1,0:T(8,128)(2,1)S(1)}, u32[]{:S(2)}, u32[]{:S(2)}) collective-permute-start(bf16[80,1152]{1,0:T(8,128)(2,1)S(1)} %get-tuple-element.45), channel_id=1, source_target_pairs={{32,16},{33,17},{34,18},{35,19},{36,20},{37,21},{38,22},{39,23},{4... | collective-permute-start | bytes 552968 | tf_op jit(solution)/shard_map/ppermute | solution.py:365
  26.4 11.1 %collective-permute-start.7 = (bf16[32,32,128]{2,1,0:T(8,128)(2,1)S(1)}, bf16[32,32,128]{2,1,0:T(8,128)(2,1)S(1)}, u32[]{:S(2)}, u32[]{:S(2)}) collective-permute-start(bf16[32,32,128]{2,1,0:T(8,128)(2,1)S(1)} %constant_dynamic-update-slice_fusion.refs_2_), channel_id=1, source_target_pairs={{0,4},{16,28},{1,5},{17,29},{2,6},{18,30},{3,7},{19,31},{4,0},{20,... | collective-permute-start | bytes 786440 | tf_op jit(solution)/shard_map/ppermute | solution.py:365
  33.7 9.2 %collective-permute-start.8 = (bf16[32,32,128]{2,1,0:T(8,128)(2,1)S(1)}, bf16[32,32,128]{2,1,0:T(8,128)(2,1)S(1)}, u32[]{:S(2)}, u32[]{:S(2)}) collective-permute-start(bf16[32,32,128]{2,1,0:T(8,128)(2,1)S(1)} %constant_dynamic-update-slice_fusion.refs_2_), channel_id=1, source_target_pairs={{0,1},{16,19},{1,0},{17,18},{2,3},{18,17},{3,2},{19,16},{4,5},{20,... | collective-permute-start | bytes 786440 | tf_op jit(solution)/shard_map/ppermute | solution.py:365
  33.7 9.2 %collective-permute-start.9 = (bf16[32,32,128]{2,1,0:T(8,128)(2,1)S(1)}, bf16[32,32,128]{2,1,0:T(8,128)(2,1)S(1)}, u32[]{:S(2)}, u32[]{:S(2)}) collective-permute-start(bf16[32,32,128]{2,1,0:T(8,128)(2,1)S(1)} %constant_dynamic-update-slice_fusion.refs_2_), channel_id=1, source_target_pairs={{0,5},{16,31},{1,4},{17,30},{2,7},{18,29},{3,6},{19,28},{4,1},{20,... | collective-permute-start | bytes 786440 | tf_op jit(solution)/shard_map/ppermute | solution.py:365
  36.1 7.4 %collective-permute-start.10 = (bf16[32,32,128]{2,1,0:T(8,128)(2,1)S(1)}, bf16[32,32,128]{2,1,0:T(8,128)(2,1)S(1)}, u32[]{:S(2)}, u32[]{:S(2)}) collective-permute-start(bf16[32,32,128]{2,1,0:T(8,128)(2,1)S(1)} %constant_dynamic-update-slice_fusion.refs_2_), channel_id=1, source_target_pairs={{0,16},{16,0},{1,17},{17,1},{2,18},{18,2},{3,19},{19,3},{4,20},{20... | collective-permute-start | bytes 786440 | tf_op jit(solution)/shard_map/ppermute | solution.py:365
  37.6 6.0 %collective-permute-start.11 = (bf16[32,32,128]{2,1,0:T(8,128)(2,1)S(1)}, bf16[32,32,128]{2,1,0:T(8,128)(2,1)S(1)}, u32[]{:S(2)}, u32[]{:S(2)}) collective-permute-start(bf16[32,32,128]{2,1,0:T(8,128)(2,1)S(1)} %collective-permute-done.7.refs_3_), channel_id=1, source_target_pairs={{0,16},{16,0},{1,17},{17,1},{2,18},{18,2},{3,19},{19,3},{4,20},{20... | collective-permute-start | bytes 786440 | tf_op jit(solution)/shard_map/ppermute | solution.py:365
  83.7 6.7 %collective-permute-start.14 = (bf16[32,32,128]{2,1,0:T(8,128)(2,1)S(1)}, bf16[32,32,128]{2,1,0:T(8,128)(2,1)S(1)}, u32[]{:S(2)}, u32[]{:S(2)}) collective-permute-start(bf16[32,32,128]{2,1,0:T(8,128)(2,1)S(1)} %get-tuple-element.27), channel_id=1, source_target_pairs={{0,16},{16,0},{1,17},{17,1},{2,18},{18,2},{3,19},{19,3},{4,20},{20... | collective-permute-start | bytes 786440 | tf_op jit(solution)/shard_map/ppermute | solution.py:365
  84.9 6.5 %collective-permute-start.20 = (bf16[32,32,128]{2,1,0:T(8,128)(2,1)S(1)}, bf16[32,32,128]{2,1,0:T(8,128)(2,1)S(1)}, u32[]{:S(2)}, u32[]{:S(2)}) collective-permute-start(bf16[32,32,128]{2,1,0:T(8,128)(2,1)S(1)} %add_convert_fusion.1), channel_id=1, source_target_pairs={{0,1},{16,19},{1,0},{17,18},{2,3},{18,17},{3,2},{19,16},{4,5},{20,... | collective-permute-start | bytes 786440 | tf_op jit(solution)/shard_map/ppermute | solution.py:365
  86.4 6.7 %collective-permute-start.18 = (bf16[32,32,128]{2,1,0:T(8,128)(2,1)S(1)}, bf16[32,32,128]{2,1,0:T(8,128)(2,1)S(1)}, u32[]{:S(2)}, u32[]{:S(2)}) collective-permute-start(bf16[32,32,128]{2,1,0:T(8,128)(2,1)S(1)} %add_convert_fusion.2), channel_id=1, source_target_pairs={{0,4},{16,28},{1,5},{17,29},{2,6},{18,30},{3,7},{19,31},{4,0},{20,... | collective-permute-start | bytes 786440 | tf_op jit(solution)/shard_map/ppermute | solution.py:365
  86.9 9.8 %collective-permute-start.16 = (bf16[32,32,128]{2,1,0:T(8,128)(2,1)S(1)}, bf16[32,32,128]{2,1,0:T(8,128)(2,1)S(1)}, u32[]{:S(2)}, u32[]{:S(2)}) collective-permute-start(bf16[32,32,128]{2,1,0:T(8,128)(2,1)S(1)} %add_convert_fusion.3), channel_id=1, source_target_pairs={{0,5},{16,31},{1,4},{17,30},{2,7},{18,29},{3,6},{19,28},{4,1},{20,... | collective-permute-start | bytes 786440 | tf_op jit(solution)/shard_map/ppermute | solution.py:365
  97.1 5.2 %collective-permute-start.21 = (bf16[8,32,128]{2,1,0:T(8,128)(2,1)S(1)}, bf16[8,32,128]{2,1,0:T(8,128)(2,1)S(1)}, u32[]{:S(2)}, u32[]{:S(2)}) collective-permute-start(bf16[8,32,128]{2,1,0:T(8,128)(2,1)S(1)} %get-tuple-element.49), channel_id=1, source_target_pairs={{0,15},{16,21},{1,14},{17,20},{2,13},{18,23},{3,12},{19,22},{4,11}... | collective-permute-start | bytes 196616 | tf_op jit(solution)/shard_map/ppermute | solution.py:365
  103.9 4.9 %collective-permute-start.24 = (bf16[8,32,128]{2,1,0:T(8,128)(2,1)S(1)}, bf16[8,32,128]{2,1,0:T(8,128)(2,1)S(1)}, u32[]{:S(2)}, u32[]{:S(2)}) collective-permute-start(bf16[8,32,128]{2,1,0:T(8,128)(2,1)S(1)} %add_convert_fusion.5), channel_id=1, source_target_pairs={{0,64},{16,80},{1,65},{17,81},{2,66},{18,82},{3,67},{19,83},{4,68}... | collective-permute-start | bytes 196616 | tf_op jit(solution)/shard_map/ppermute | solution.py:365
  109.3 5.1 %collective-permute-start.29 = (bf16[8,32,128]{2,1,0:T(8,128)(2,1)S(1)}, bf16[8,32,128]{2,1,0:T(8,128)(2,1)S(1)}, u32[]{:S(2)}, u32[]{:S(2)}) collective-permute-start(bf16[8,32,128]{2,1,0:T(8,128)(2,1)S(1)} %pad_maximum_fusion.2), channel_id=1, source_target_pairs={{0,15},{16,21},{1,14},{17,20},{2,13},{18,23},{3,12},{19,22},{4,11}... | collective-permute-start | bytes 196616 | tf_op jit(solution)/shard_map/ppermute | solution.py:365
  115.9 14.8 %collective-permute-start.33 = (bf16[32,32,128]{2,1,0:T(8,128)(2,1)S(1)}, bf16[32,32,128]{2,1,0:T(8,128)(2,1)S(1)}, u32[]{:S(2)}, u32[]{:S(2)}) collective-permute-start(bf16[32,32,128]{2,1,0:T(8,128)(2,1)S(1)} %pad_maximum_fusion.refs_1_), channel_id=1, source_target_pairs={{0,16},{16,0},{1,17},{17,1},{2,18},{18,2},{3,19},{19,3},{4,20},{20... | collective-permute-start | bytes 786440 | tf_op jit(solution)/shard_map/ppermute | solution.py:365
  125.6 6.6 %collective-permute-start.30 = (bf16[32,32,128]{2,1,0:T(8,128)(2,1)S(1)}, bf16[32,32,128]{2,1,0:T(8,128)(2,1)S(1)}, u32[]{:S(2)}, u32[]{:S(2)}) collective-permute-start(bf16[32,32,128]{2,1,0:T(8,128)(2,1)S(1)} %pad_maximum_fusion.refs_1_), channel_id=1, source_target_pairs={{0,4},{16,28},{1,5},{17,29},{2,6},{18,30},{3,7},{19,31},{4,0},{20,... | collective-permute-start | bytes 786440 | tf_op jit(solution)/shard_map/ppermute | solution.py:365
  126.1 6.6 %collective-permute-start.31 = (bf16[32,32,128]{2,1,0:T(8,128)(2,1)S(1)}, bf16[32,32,128]{2,1,0:T(8,128)(2,1)S(1)}, u32[]{:S(2)}, u32[]{:S(2)}) collective-permute-start(bf16[32,32,128]{2,1,0:T(8,128)(2,1)S(1)} %pad_maximum_fusion.refs_1_), channel_id=1, source_target_pairs={{0,1},{16,19},{1,0},{17,18},{2,3},{18,17},{3,2},{19,16},{4,5},{20,... | collective-permute-start | bytes 786440 | tf_op jit(solution)/shard_map/ppermute | solution.py:365
  128.2 8.5 %collective-permute-start.32 = (bf16[32,32,128]{2,1,0:T(8,128)(2,1)S(1)}, bf16[32,32,128]{2,1,0:T(8,128)(2,1)S(1)}, u32[]{:S(2)}, u32[]{:S(2)}) collective-permute-start(bf16[32,32,128]{2,1,0:T(8,128)(2,1)S(1)} %pad_maximum_fusion.refs_1_), channel_id=1, source_target_pairs={{0,5},{16,31},{1,4},{17,30},{2,7},{18,29},{3,6},{19,28},{4,1},{20,... | collective-permute-start | bytes 786440 | tf_op jit(solution)/shard_map/ppermute | solution.py:365
  132.2 5.3 %collective-permute-start.34 = (bf16[32,32,128]{2,1,0:T(8,128)(2,1)S(1)}, bf16[32,32,128]{2,1,0:T(8,128)(2,1)S(1)}, u32[]{:S(2)}, u32[]{:S(2)}) collective-permute-start(bf16[32,32,128]{2,1,0:T(8,128)(2,1)S(1)} %collective-permute-done.30.refs_2_), channel_id=1, source_target_pairs={{0,16},{16,0},{1,17},{17,1},{2,18},{18,2},{3,19},{19,3},{4,20},{20... | collective-permute-start | bytes 786440 | tf_op jit(solution)/shard_map/ppermute | solution.py:365
  (28 other events, 242.2 us)

commit v6 on v5

--- a/solution.py
+++ b/solution.py
@@ -227,15 +227,19 @@
             target.at[rows_t, cols_t], resist_out.at[rows_t, cols_t], resist_sems.at[t]
         ).start()
         back = dot(fine_t[...], dot(slopes, fine[...]).astype(BF16))
+        both = []
+        for k in range(NK):
+            scaled = back * (weights[k] * (2.0 / BAND**2))
+            both.append(
+                jnp.concatenate(
+                    [(scaled * fields[k, :, :256]).astype(BF16), (scaled * fields[k, :, 256:]).astype(BF16)], axis=1
+                )
+            )
+        low = dot(jnp.concatenate(both, axis=0), up_vt[...]).astype(BF16)
         for k in range(NK):
             at = slice(k * 128, k * 128 + 128)
-            scaled = back * (weights[k] * (2.0 / BAND**2))
-            both = jnp.concatenate(
-                [(scaled * fields[k, :, :256]).astype(BF16), (scaled * fields[k, :, 256:]).astype(BF16)], axis=1
-            )
-            low = dot(both, up_vt[...]).astype(BF16)
-            halves[0:256, at] = low[:, :128]
-            halves[256:512, at] = low[:, 128:]
+            halves[0:256, at] = low[k * 256 : k * 256 + 256, :128]
+            halves[256:512, at] = low[k * 256 : k * 256 + 256, 128:]
         bspec_re = jnp.zeros((128, 128), F32)
         bspec_im = jnp.zeros((128, 128), F32)
         bamp = dot(up_ut[...], halves[...])
@@ -448,9 +452,10 @@
 
     top = strip(edges[0], slice(0, 64), slice(0, 64), 0)
     bottom = strip(edges[1], slice(448, 512), slice(64, 128), 15)
-    near_strip = send(jnp.where(core == 0, bottom, top), SWAP)
-    far_strip = send(jnp.where(core == 0, top, bottom), OVER)
+    for_near, for_far = jnp.where(core == 0, bottom, top), jnp.where(core == 0, top, bottom)
     parts = gathered_far(group)
+    _, for_near, for_far = lax.optimization_barrier((parts[1], for_near, for_far))
+    near_strip, far_strip = send(for_near, SWAP), send(for_far, OVER)
 
     from_near, from_far = ints(near_strip[64:66, :18]), ints(far_strip[64:66, :18])
     above, below = jnp.where(core == 0, from_far, from_near), jnp.where(core == 0, from_near, from_far)

time: 147 us -> 145 us (0.986)
  waiting for transfers between devices: 26.9 us -> 23.2 us
  Pallas kernels: 44.8 us -> 47.6 us
  starting transfers between devices: 62.2 us -> 59.4 us
    ppermute x35, waiting for transfers between devices: 26.4 us -> 23.2 us  [send(): return lax.ppermute(value, BOTH, pairs)]
    pallas_call x1, Pallas kernels: 37.1 us -> 39.9 us  [per_device(): pl.pallas_call(main_kernel, out_shape=(wide, wide, *[sums_shape] * 8), in...]
    ppermute x35, starting transfers between devices: 56.9 us -> 54.1 us  [send(): return lax.ppermute(value, BOTH, pairs)]
  transfers between devices with their start and end apart: 37 -> 37, of which waited for: 20 -> 15; matrix products, arithmetic and copies ran while one was open for 5% -> 6% of each run, Pallas kernels for 0% -> 0%
where the time goes in v6:
time: 145 us; the launch traced here: 144 us
  starting transfers between devices  59.4 us (41%)
  Pallas kernels  47.6 us (33%)
  waiting for transfers between devices  23.2 us (16%)
  local copies, waits for them, and re-layouts  7.53 us (5%)
  other arithmetic  5.29 us (4%)
    ppermute x35, starting transfers between devices, send(): return lax.ppermute(value, BOTH, pairs)  54.1 us
    pallas_call x1, Pallas kernels, per_device(): pl.pallas_call(main_kernel, out_shape=(wide, wide, *[sums_shape] * 8), in...  39.9 us
    ppermute x35, waiting for transfers between devices, send(): return lax.ppermute(value, BOTH, pairs)  23.2 us
    pallas_call x1, Pallas kernels, per_device(): pl.pallas_call(final_kernel, out_shape=wide, in_specs=[smem] + [anywhere]...  7.7 us
    ppermute x1, starting transfers between devices, per_device(): before = lax.ppermute(side(edges[3], 15), 'col', up)  3.99 us
  transfers between devices with their start and end apart: 37, of which 15 were waited for; matrix products, arithmetic and copies ran while one was open for 6% of the time, Pallas kernels for 0%

profile of v6, /device:TPU:1, one launch (start us, length us, event | category | flops | bytes accessed | tf_op | source)
XLA Modules:
  0.0 144.4 jit_solution(17792475675876335951)
XLA Ops:
  2.0 2.2 %collective-permute-start = (bf16[8,32,128]{2,1,0:T(8,128)(2,1)S(1)}, bf16[8,32,128]{2,1,0:T(8,128)(2,1)S(1)}, u32[]{:S(2)}, u32[]{:S(2)}) collective-permute-start(bf16[8,32,128]{2,1,0:T(8,128)(2,1)S(1)} %pad_maximum_fusion.1), channel_id=1, source_target_pairs={{0,12},{16,20},{1,13},{17,21},{2,14},{18,22},{3,15},{19,23},{4,8},... | collective-permute-start | bytes 196616 | tf_op jit(solution)/shard_map/ppermute | solution.py:369
  4.2 1.6 %collective-permute-start.1 = (bf16[8,32,128]{2,1,0:T(8,128)(2,1)S(1)}, bf16[8,32,128]{2,1,0:T(8,128)(2,1)S(1)}, u32[]{:S(2)}, u32[]{:S(2)}) collective-permute-start(bf16[8,32,128]{2,1,0:T(8,128)(2,1)S(1)} %pad_maximum_fusion.1), channel_id=1, source_target_pairs={{0,3},{16,17},{1,2},{17,16},{2,1},{18,19},{3,0},{19,18},{4,7},{20,... | collective-permute-start | bytes 196616 | tf_op jit(solution)/shard_map/ppermute | solution.py:369
  10.8 4.0 %collective-permute-start.4 = (bf16[528,128]{1,0:T(8,128)(2,1)S(1)}, bf16[528,128]{1,0:T(8,128)(2,1)S(1)}, u32[]{:S(2)}, u32[]{:S(2)}) collective-permute-start(bf16[528,128]{1,0:T(8,128)(2,1)S(1)} %fusion.13), channel_id=1, source_target_pairs={{0,1},{1,2},{2,3},{3,4},{4,5},{5,6},{6,7},{7,8},{8,9},{9,10},{10,1... | collective-permute-start | bytes 405512 | tf_op jit(solution)/shard_map/ppermute | solution.py:438
  14.9 5.0 %collective-permute-start.3 = (bf16[32,32,128]{2,1,0:T(8,128)(2,1)S(1)}, bf16[32,32,128]{2,1,0:T(8,128)(2,1)S(1)}, u32[]{:S(2)}, u32[]{:S(2)}) collective-permute-start(bf16[32,32,128]{2,1,0:T(8,128)(2,1)S(1)} %constant_dynamic-update-slice_fusion.refs_2_), channel_id=1, source_target_pairs={{0,4},{16,28},{1,5},{17,29},{2,6},{18,30},{3,7},{19,31},{4,0},{20,... | collective-permute-start | bytes 786440 | tf_op jit(solution)/shard_map/ppermute | solution.py:369
  20.6 2.3 %collective-permute-start.9 = (bf16[32,32,128]{2,1,0:T(8,128)(2,1)S(1)}, bf16[32,32,128]{2,1,0:T(8,128)(2,1)S(1)}, u32[]{:S(2)}, u32[]{:S(2)}) collective-permute-start(bf16[32,32,128]{2,1,0:T(8,128)(2,1)S(1)} %constant_dynamic-update-slice_fusion.refs_2_), channel_id=1, source_target_pairs={{0,5},{16,31},{1,4},{17,30},{2,7},{18,29},{3,6},{19,28},{4,1},{20,... | collective-permute-start | bytes 786440 | tf_op jit(solution)/shard_map/ppermute | solution.py:369
  24.3 2.7 %collective-permute-start.7 = (bf16[80,1152]{1,0:T(8,128)(2,1)}, bf16[80,1152]{1,0:T(8,128)(2,1)S(1)}, u32[]{:S(2)}, u32[]{:S(2)}) collective-permute-start(bf16[80,1152]{1,0:T(8,128)(2,1)} %get-tuple-element.28), channel_id=1, source_target_pairs={{0,16},{16,0},{1,17},{17,1},{2,18},{18,2},{3,19},{19,3},{4,20},{20... | collective-permute-start | bytes 552968 | tf_op jit(solution)/shard_map/ppermute | solution.py:369
  27.0 3.0 %collective-permute-start.6 = (bf16[80,1152]{1,0:T(8,128)(2,1)S(1)}, bf16[80,1152]{1,0:T(8,128)(2,1)S(1)}, u32[]{:S(2)}, u32[]{:S(2)}) collective-permute-start(bf16[80,1152]{1,0:T(8,128)(2,1)S(1)} %get-tuple-element.27), channel_id=1, source_target_pairs={{32,16},{33,17},{34,18},{35,19},{36,20},{37,21},{38,22},{39,23},{4... | collective-permute-start | bytes 552968 | tf_op jit(solution)/shard_map/ppermute | solution.py:369
  36.4 39.9 %image_and_gradient.1 = (f32[1024,1024]{1,0:T(8,128)}, f32[1024,1024]{1,0:T(8,128)}, bf16[32,32,128]{2,1,0:T(8,128)(2,1)S(1)}, bf16[32,32,128]{2,1,0:T(8,128)(2,...) custom-call(s32[653]{0:T(1024)S(1)} %pad_add_fusion.1.refs_0_, ...), custom_call_target="tpu_custom_call" | custom-call | tf_op jit(solution)/shard_map/image_and_gradient/pallas_call | solution.py:481
  78.2 4.5 %collective-permute-start.20 = (bf16[32,32,128]{2,1,0:T(8,128)(2,1)S(1)}, bf16[32,32,128]{2,1,0:T(8,128)(2,1)S(1)}, u32[]{:S(2)}, u32[]{:S(2)}) collective-permute-start(bf16[32,32,128]{2,1,0:T(8,128)(2,1)S(1)} %add_convert_fusion.1), channel_id=1, source_target_pairs={{0,1},{16,19},{1,0},{17,18},{2,3},{18,17},{3,2},{19,16},{4,5},{20,... | collective-permute-start | bytes 786440 | tf_op jit(solution)/shard_map/ppermute | solution.py:369
  82.8 1.6 %collective-permute-start.18 = (bf16[32,32,128]{2,1,0:T(8,128)(2,1)S(1)}, bf16[32,32,128]{2,1,0:T(8,128)(2,1)S(1)}, u32[]{:S(2)}, u32[]{:S(2)}) collective-permute-start(bf16[32,32,128]{2,1,0:T(8,128)(2,1)S(1)} %add_convert_fusion.2), channel_id=1, source_target_pairs={{0,4},{16,28},{1,5},{17,29},{2,6},{18,30},{3,7},{19,31},{4,0},{20,... | collective-permute-start | bytes 786440 | tf_op jit(solution)/shard_map/ppermute | solution.py:369
  86.4 3.0 %collective-permute-done.18 = bf16[32,32,128]{2,1,0:T(8,128)(2,1)S(1)} collective-permute-done((bf16[32,32,128]{2,1,0:T(8,128)(2,1)S(1)}, bf16[32,32,128]{2,1,0:T(8,128)(2,1)S(1)}, u32[]{:S(2)}, u32[]{:S(2)}) %collective-permute-start.18) | collective-permute-done | bytes 262176 | tf_op jit(solution)/shard_map/ppermute | solution.py:369
  89.4 3.6 %collective-permute-done.16 = bf16[32,32,128]{2,1,0:T(8,128)(2,1)S(1)} collective-permute-done((bf16[32,32,128]{2,1,0:T(8,128)(2,1)S(1)}, bf16[32,32,128]{2,1,0:T(8,128)(2,1)S(1)}, u32[]{:S(2)}, u32[]{:S(2)}) %collective-permute-start.16) | collective-permute-done | bytes 262176 | tf_op jit(solution)/shard_map/ppermute | solution.py:369
  93.7 2.3 %collective-permute-start.21 = (bf16[8,32,128]{2,1,0:T(8,128)(2,1)S(1)}, bf16[8,32,128]{2,1,0:T(8,128)(2,1)S(1)}, u32[]{:S(2)}, u32[]{:S(2)}) collective-permute-start(bf16[8,32,128]{2,1,0:T(8,128)(2,1)S(1)} %get-tuple-element.53), channel_id=1, source_target_pairs={{0,15},{16,21},{1,14},{17,20},{2,13},{18,23},{3,12},{19,22},{4,11}... | collective-permute-start | bytes 196616 | tf_op jit(solution)/shard_map/ppermute | solution.py:369
  96.8 1.8 %collective-permute-done.21 = bf16[8,32,128]{2,1,0:T(8,128)(2,1)S(1)} collective-permute-done((bf16[8,32,128]{2,1,0:T(8,128)(2,1)S(1)}, bf16[8,32,128]{2,1,0:T(8,128)(2,1)S(1)}, u32[]{:S(2)}, u32[]{:S(2)}) %collective-permute-start.21) | collective-permute-done | bytes 65568 | tf_op jit(solution)/shard_map/ppermute | solution.py:369
  98.7 1.9 %collective-permute-start.26 = (bf16[8,32,128]{2,1,0:T(8,128)(2,1)S(1)}, bf16[8,32,128]{2,1,0:T(8,128)(2,1)S(1)}, u32[]{:S(2)}, u32[]{:S(2)}) collective-permute-start(bf16[8,32,128]{2,1,0:T(8,128)(2,1)S(1)} %add_convert_fusion.5), channel_id=1, source_target_pairs={{0,96},{16,112},{1,97},{17,113},{2,98},{18,114},{3,99},{19,115},{4... | collective-permute-start | bytes 196616 | tf_op jit(solution)/shard_map/ppermute | solution.py:369
  100.6 2.4 %collective-permute-start.24 = (bf16[8,32,128]{2,1,0:T(8,128)(2,1)S(1)}, bf16[8,32,128]{2,1,0:T(8,128)(2,1)S(1)}, u32[]{:S(2)}, u32[]{:S(2)}) collective-permute-start(bf16[8,32,128]{2,1,0:T(8,128)(2,1)S(1)} %add_convert_fusion.5), channel_id=1, source_target_pairs={{0,64},{16,80},{1,65},{17,81},{2,66},{18,82},{3,67},{19,83},{4,68}... | collective-permute-start | bytes 196616 | tf_op jit(solution)/shard_map/ppermute | solution.py:369
  103.1 2.5 %collective-permute-done.25 = bf16[8,32,128]{2,1,0:T(8,128)(2,1)S(1)} collective-permute-done((bf16[8,32,128]{2,1,0:T(8,128)(2,1)S(1)}, bf16[8,32,128]{2,1,0:T(8,128)(2,1)S(1)}, u32[]{:S(2)}, u32[]{:S(2)}) %collective-permute-start.25) | collective-permute-done | bytes 65568 | tf_op jit(solution)/shard_map/ppermute | solution.py:369
  106.1 2.3 %collective-permute-start.29 = (bf16[8,32,128]{2,1,0:T(8,128)(2,1)S(1)}, bf16[8,32,128]{2,1,0:T(8,128)(2,1)S(1)}, u32[]{:S(2)}, u32[]{:S(2)}) collective-permute-start(bf16[8,32,128]{2,1,0:T(8,128)(2,1)S(1)} %pad_maximum_fusion.2), channel_id=1, source_target_pairs={{0,15},{16,21},{1,14},{17,20},{2,13},{18,23},{3,12},{19,22},{4,11}... | collective-permute-start | bytes 196616 | tf_op jit(solution)/shard_map/ppermute | solution.py:369
  110.2 1.6 %collective-permute-done.28 = bf16[8,32,128]{2,1,0:T(8,128)(2,1)S(1)} collective-permute-done((bf16[8,32,128]{2,1,0:T(8,128)(2,1)S(1)}, bf16[8,32,128]{2,1,0:T(8,128)(2,1)S(1)}, u32[]{:S(2)}, u32[]{:S(2)}) %collective-permute-start.28) | collective-permute-done | bytes 65568 | tf_op jit(solution)/shard_map/ppermute | solution.py:369
  112.0 10.9 %collective-permute-start.33 = (bf16[32,32,128]{2,1,0:T(8,128)(2,1)S(1)}, bf16[32,32,128]{2,1,0:T(8,128)(2,1)S(1)}, u32[]{:S(2)}, u32[]{:S(2)}) collective-permute-start(bf16[32,32,128]{2,1,0:T(8,128)(2,1)S(1)} %pad_maximum_fusion.refs_1_), channel_id=1, source_target_pairs={{0,16},{16,0},{1,17},{17,1},{2,18},{18,2},{3,19},{19,3},{4,20},{20... | collective-permute-start | bytes 786440 | tf_op jit(solution)/shard_map/ppermute | solution.py:369
  123.0 1.6 %collective-permute-start.30 = (bf16[32,32,128]{2,1,0:T(8,128)(2,1)S(1)}, bf16[32,32,128]{2,1,0:T(8,128)(2,1)S(1)}, u32[]{:S(2)}, u32[]{:S(2)}) collective-permute-start(bf16[32,32,128]{2,1,0:T(8,128)(2,1)S(1)} %pad_maximum_fusion.refs_1_), channel_id=1, source_target_pairs={{0,4},{16,28},{1,5},{17,29},{2,6},{18,30},{3,7},{19,31},{4,0},{20,... | collective-permute-start | bytes 786440 | tf_op jit(solution)/shard_map/ppermute | solution.py:369
  125.7 2.4 %collective-permute-start.32 = (bf16[32,32,128]{2,1,0:T(8,128)(2,1)S(1)}, bf16[32,32,128]{2,1,0:T(8,128)(2,1)S(1)}, u32[]{:S(2)}, u32[]{:S(2)}) collective-permute-start(bf16[32,32,128]{2,1,0:T(8,128)(2,1)S(1)} %pad_maximum_fusion.refs_1_), channel_id=1, source_target_pairs={{0,5},{16,31},{1,4},{17,30},{2,7},{18,29},{3,6},{19,28},{4,1},{20,... | collective-permute-start | bytes 786440 | tf_op jit(solution)/shard_map/ppermute | solution.py:369
  132.4 1.9 %collective-permute-done.32.refs_4_ = bf16[32,32,128]{2,1,0:T(8,128)(2,1)S(1)} collective-permute-done((bf16[32,32,128]{2,1,0:T(8,128)(2,1)S(1)}, bf16[32,32,128]{2,1,0:T(8,128)(2,1)S(1)}, u32[]{:S(2)}, u32[]{:S(2)}) %collective-permute-start.32) | collective-permute-done | bytes 262176 | tf_op jit(solution)/shard_map/ppermute | solution.py:369
  136.5 7.7 %final_mask.1 = f32[1024,1024]{1,0:T(8,128)} custom-call(s32[653]{0:T(1024)S(1)} %pad_add_fusion.1.refs_0_, bf16[32,32,128]{2,1,0:T(8,128)(2,1)S(1)} %pad_maximum_fusion.refs_1_, bf16[32,32,128]{2,1,0:T(8,128)(2,1)S(1)} %collective-permute-done.30.refs_2_, bf16[32,32,128]{2,1,0:T(8,128)(2,1)S(1)} %collective-permute-done.31.refs_3_, ...), custom_call_target="tpu_custom_call" | custom-call | tf_op jit(solution)/shard_map/final_mask/pallas_call | solution.py:513
  (138 shorter events, 30.3 us)
Async XLA Ops:
  2.0 12.8 %collective-permute-start = (bf16[8,32,128]{2,1,0:T(8,128)(2,1)S(1)}, bf16[8,32,128]{2,1,0:T(8,128)(2,1)S(1)}, u32[]{:S(2)}, u32[]{:S(2)}) collective-permute-start(bf16[8,32,128]{2,1,0:T(8,128)(2,1)S(1)} %pad_maximum_fusion.1), channel_id=1, source_target_pairs={{0,12},{16,20},{1,13},{17,21},{2,14},{18,22},{3,15},{19,23},{4,8},... | collective-permute-start | bytes 196616 | tf_op jit(solution)/shard_map/ppermute | solution.py:369
  4.2 10.6 %collective-permute-start.1 = (bf16[8,32,128]{2,1,0:T(8,128)(2,1)S(1)}, bf16[8,32,128]{2,1,0:T(8,128)(2,1)S(1)}, u32[]{:S(2)}, u32[]{:S(2)}) collective-permute-start(bf16[8,32,128]{2,1,0:T(8,128)(2,1)S(1)} %pad_maximum_fusion.1), channel_id=1, source_target_pairs={{0,3},{16,17},{1,2},{17,16},{2,1},{18,19},{3,0},{19,18},{4,7},{20,... | collective-permute-start | bytes 196616 | tf_op jit(solution)/shard_map/ppermute | solution.py:369
  5.9 9.0 %collective-permute-start.2 = (bf16[8,32,128]{2,1,0:T(8,128)(2,1)S(1)}, bf16[8,32,128]{2,1,0:T(8,128)(2,1)S(1)}, u32[]{:S(2)}, u32[]{:S(2)}) collective-permute-start(bf16[8,32,128]{2,1,0:T(8,128)(2,1)S(1)} %pad_maximum_fusion.1), channel_id=1, source_target_pairs={{0,15},{16,21},{1,14},{17,20},{2,13},{18,23},{3,12},{19,22},{4,11}... | collective-permute-start | bytes 196616 | tf_op jit(solution)/shard_map/ppermute | solution.py:369
  9.3 13.6 %collective-permute-start.5 = (bf16[528,128]{1,0:T(8,128)(2,1)S(1)}, bf16[528,128]{1,0:T(8,128)(2,1)S(1)}, u32[]{:S(2)}, u32[]{:S(2)}) collective-permute-start(bf16[528,128]{1,0:T(8,128)(2,1)S(1)} %fusion.14), channel_id=1, source_target_pairs={{1,0},{2,1},{3,2},{4,3},{5,4},{6,5},{7,6},{8,7},{9,8},{10,9},{11,1... | collective-permute-start | bytes 405512 | tf_op jit(solution)/shard_map/ppermute | solution.py:439
  10.8 12.3 %collective-permute-start.4 = (bf16[528,128]{1,0:T(8,128)(2,1)S(1)}, bf16[528,128]{1,0:T(8,128)(2,1)S(1)}, u32[]{:S(2)}, u32[]{:S(2)}) collective-permute-start(bf16[528,128]{1,0:T(8,128)(2,1)S(1)} %fusion.13), channel_id=1, source_target_pairs={{0,1},{1,2},{2,3},{3,4},{4,5},{5,6},{6,7},{7,8},{8,9},{9,10},{10,1... | collective-permute-start | bytes 405512 | tf_op jit(solution)/shard_map/ppermute | solution.py:438
  14.9 9.4 %collective-permute-start.3 = (bf16[32,32,128]{2,1,0:T(8,128)(2,1)S(1)}, bf16[32,32,128]{2,1,0:T(8,128)(2,1)S(1)}, u32[]{:S(2)}, u32[]{:S(2)}) collective-permute-start(bf16[32,32,128]{2,1,0:T(8,128)(2,1)S(1)} %constant_dynamic-update-slice_fusion.refs_2_), channel_id=1, source_target_pairs={{0,4},{16,28},{1,5},{17,29},{2,6},{18,30},{3,7},{19,31},{4,0},{20,... | collective-permute-start | bytes 786440 | tf_op jit(solution)/shard_map/ppermute | solution.py:369
  19.9 11.4 %collective-permute-start.8 = (bf16[32,32,128]{2,1,0:T(8,128)(2,1)S(1)}, bf16[32,32,128]{2,1,0:T(8,128)(2,1)S(1)}, u32[]{:S(2)}, u32[]{:S(2)}) collective-permute-start(bf16[32,32,128]{2,1,0:T(8,128)(2,1)S(1)} %constant_dynamic-update-slice_fusion.refs_2_), channel_id=1, source_target_pairs={{0,1},{16,19},{1,0},{17,18},{2,3},{18,17},{3,2},{19,16},{4,5},{20,... | collective-permute-start | bytes 786440 | tf_op jit(solution)/shard_map/ppermute | solution.py:369
  20.6 11.2 %collective-permute-start.9 = (bf16[32,32,128]{2,1,0:T(8,128)(2,1)S(1)}, bf16[32,32,128]{2,1,0:T(8,128)(2,1)S(1)}, u32[]{:S(2)}, u32[]{:S(2)}) collective-permute-start(bf16[32,32,128]{2,1,0:T(8,128)(2,1)S(1)} %constant_dynamic-update-slice_fusion.refs_2_), channel_id=1, source_target_pairs={{0,5},{16,31},{1,4},{17,30},{2,7},{18,29},{3,6},{19,28},{4,1},{20,... | collective-permute-start | bytes 786440 | tf_op jit(solution)/shard_map/ppermute | solution.py:369
  24.3 7.6 %collective-permute-start.7 = (bf16[80,1152]{1,0:T(8,128)(2,1)}, bf16[80,1152]{1,0:T(8,128)(2,1)S(1)}, u32[]{:S(2)}, u32[]{:S(2)}) collective-permute-start(bf16[80,1152]{1,0:T(8,128)(2,1)} %get-tuple-element.28), channel_id=1, source_target_pairs={{0,16},{16,0},{1,17},{17,1},{2,18},{18,2},{3,19},{19,3},{4,20},{20... | collective-permute-start | bytes 552968 | tf_op jit(solution)/shard_map/ppermute | solution.py:369
  27.0 6.8 %collective-permute-start.6 = (bf16[80,1152]{1,0:T(8,128)(2,1)S(1)}, bf16[80,1152]{1,0:T(8,128)(2,1)S(1)}, u32[]{:S(2)}, u32[]{:S(2)}) collective-permute-start(bf16[80,1152]{1,0:T(8,128)(2,1)S(1)} %get-tuple-element.27), channel_id=1, source_target_pairs={{32,16},{33,17},{34,18},{35,19},{36,20},{37,21},{38,22},{39,23},{4... | collective-permute-start | bytes 552968 | tf_op jit(solution)/shard_map/ppermute | solution.py:369
  76.4 6.3 %collective-permute-start.17 = (bf16[32,32,128]{2,1,0:T(8,128)(2,1)}, bf16[32,32,128]{2,1,0:T(8,128)(2,1)S(1)}, u32[]{:S(2)}, u32[]{:S(2)}) collective-permute-start(bf16[32,32,128]{2,1,0:T(8,128)(2,1)} %get-tuple-element.35), channel_id=1, source_target_pairs={{0,16},{16,0},{1,17},{17,1},{2,18},{18,2},{3,19},{19,3},{4,20},{20... | collective-permute-start | bytes 786440 | tf_op jit(solution)/shard_map/ppermute | solution.py:369
  76.9 7.5 %collective-permute-start.15 = (bf16[32,32,128]{2,1,0:T(8,128)(2,1)}, bf16[32,32,128]{2,1,0:T(8,128)(2,1)S(1)}, u32[]{:S(2)}, u32[]{:S(2)}) collective-permute-start(bf16[32,32,128]{2,1,0:T(8,128)(2,1)} %get-tuple-element.33), channel_id=1, source_target_pairs={{0,16},{16,0},{1,17},{17,1},{2,18},{18,2},{3,19},{19,3},{4,20},{20... | collective-permute-start | bytes 786440 | tf_op jit(solution)/shard_map/ppermute | solution.py:369
  77.0 8.6 %collective-permute-start.14 = (bf16[32,32,128]{2,1,0:T(8,128)(2,1)S(1)}, bf16[32,32,128]{2,1,0:T(8,128)(2,1)S(1)}, u32[]{:S(2)}, u32[]{:S(2)}) collective-permute-start(bf16[32,32,128]{2,1,0:T(8,128)(2,1)S(1)} %get-tuple-element.31), channel_id=1, source_target_pairs={{0,16},{16,0},{1,17},{17,1},{2,18},{18,2},{3,19},{19,3},{4,20},{20... | collective-permute-start | bytes 786440 | tf_op jit(solution)/shard_map/ppermute | solution.py:369
  78.2 8.2 %collective-permute-start.20 = (bf16[32,32,128]{2,1,0:T(8,128)(2,1)S(1)}, bf16[32,32,128]{2,1,0:T(8,128)(2,1)S(1)}, u32[]{:S(2)}, u32[]{:S(2)}) collective-permute-start(bf16[32,32,128]{2,1,0:T(8,128)(2,1)S(1)} %add_convert_fusion.1), channel_id=1, source_target_pairs={{0,1},{16,19},{1,0},{17,18},{2,3},{18,17},{3,2},{19,16},{4,5},{20,... | collective-permute-start | bytes 786440 | tf_op jit(solution)/shard_map/ppermute | solution.py:369
  82.8 6.7 %collective-permute-start.18 = (bf16[32,32,128]{2,1,0:T(8,128)(2,1)S(1)}, bf16[32,32,128]{2,1,0:T(8,128)(2,1)S(1)}, u32[]{:S(2)}, u32[]{:S(2)}) collective-permute-start(bf16[32,32,128]{2,1,0:T(8,128)(2,1)S(1)} %add_convert_fusion.2), channel_id=1, source_target_pairs={{0,4},{16,28},{1,5},{17,29},{2,6},{18,30},{3,7},{19,31},{4,0},{20,... | collective-permute-start | bytes 786440 | tf_op jit(solution)/shard_map/ppermute | solution.py:369
  84.4 8.6 %collective-permute-start.16 = (bf16[32,32,128]{2,1,0:T(8,128)(2,1)S(1)}, bf16[32,32,128]{2,1,0:T(8,128)(2,1)S(1)}, u32[]{:S(2)}, u32[]{:S(2)}) collective-permute-start(bf16[32,32,128]{2,1,0:T(8,128)(2,1)S(1)} %add_convert_fusion.3), channel_id=1, source_target_pairs={{0,5},{16,31},{1,4},{17,30},{2,7},{18,29},{3,6},{19,28},{4,1},{20,... | collective-permute-start | bytes 786440 | tf_op jit(solution)/shard_map/ppermute | solution.py:369
  93.7 4.9 %collective-permute-start.21 = (bf16[8,32,128]{2,1,0:T(8,128)(2,1)S(1)}, bf16[8,32,128]{2,1,0:T(8,128)(2,1)S(1)}, u32[]{:S(2)}, u32[]{:S(2)}) collective-permute-start(bf16[8,32,128]{2,1,0:T(8,128)(2,1)S(1)} %get-tuple-element.53), channel_id=1, source_target_pairs={{0,15},{16,21},{1,14},{17,20},{2,13},{18,23},{3,12},{19,22},{4,11}... | collective-permute-start | bytes 196616 | tf_op jit(solution)/shard_map/ppermute | solution.py:369
  100.6 5.0 %collective-permute-start.25 = (bf16[8,32,128]{2,1,0:T(8,128)(2,1)S(1)}, bf16[8,32,128]{2,1,0:T(8,128)(2,1)S(1)}, u32[]{:S(2)}, u32[]{:S(2)}) collective-permute-start(bf16[8,32,128]{2,1,0:T(8,128)(2,1)S(1)} %add_convert_fusion.5), channel_id=1, source_target_pairs={{0,32},{16,48},{1,33},{17,49},{2,34},{18,50},{3,35},{19,51},{4,36}... | collective-permute-start | bytes 196616 | tf_op jit(solution)/shard_map/ppermute | solution.py:369
  100.6 5.0 %collective-permute-start.24 = (bf16[8,32,128]{2,1,0:T(8,128)(2,1)S(1)}, bf16[8,32,128]{2,1,0:T(8,128)(2,1)S(1)}, u32[]{:S(2)}, u32[]{:S(2)}) collective-permute-start(bf16[8,32,128]{2,1,0:T(8,128)(2,1)S(1)} %add_convert_fusion.5), channel_id=1, source_target_pairs={{0,64},{16,80},{1,65},{17,81},{2,66},{18,82},{3,67},{19,83},{4,68}... | collective-permute-start | bytes 196616 | tf_op jit(solution)/shard_map/ppermute | solution.py:369
  112.0 16.2 %collective-permute-start.33 = (bf16[32,32,128]{2,1,0:T(8,128)(2,1)S(1)}, bf16[32,32,128]{2,1,0:T(8,128)(2,1)S(1)}, u32[]{:S(2)}, u32[]{:S(2)}) collective-permute-start(bf16[32,32,128]{2,1,0:T(8,128)(2,1)S(1)} %pad_maximum_fusion.refs_1_), channel_id=1, source_target_pairs={{0,16},{16,0},{1,17},{17,1},{2,18},{18,2},{3,19},{19,3},{4,20},{20... | collective-permute-start | bytes 786440 | tf_op jit(solution)/shard_map/ppermute | solution.py:369
  123.0 6.6 %collective-permute-start.30 = (bf16[32,32,128]{2,1,0:T(8,128)(2,1)S(1)}, bf16[32,32,128]{2,1,0:T(8,128)(2,1)S(1)}, u32[]{:S(2)}, u32[]{:S(2)}) collective-permute-start(bf16[32,32,128]{2,1,0:T(8,128)(2,1)S(1)} %pad_maximum_fusion.refs_1_), channel_id=1, source_target_pairs={{0,4},{16,28},{1,5},{17,29},{2,6},{18,30},{3,7},{19,31},{4,0},{20,... | collective-permute-start | bytes 786440 | tf_op jit(solution)/shard_map/ppermute | solution.py:369
  124.6 6.4 %collective-permute-start.31 = (bf16[32,32,128]{2,1,0:T(8,128)(2,1)S(1)}, bf16[32,32,128]{2,1,0:T(8,128)(2,1)S(1)}, u32[]{:S(2)}, u32[]{:S(2)}) collective-permute-start(bf16[32,32,128]{2,1,0:T(8,128)(2,1)S(1)} %pad_maximum_fusion.refs_1_), channel_id=1, source_target_pairs={{0,1},{16,19},{1,0},{17,18},{2,3},{18,17},{3,2},{19,16},{4,5},{20,... | collective-permute-start | bytes 786440 | tf_op jit(solution)/shard_map/ppermute | solution.py:369
  125.7 8.5 %collective-permute-start.32 = (bf16[32,32,128]{2,1,0:T(8,128)(2,1)S(1)}, bf16[32,32,128]{2,1,0:T(8,128)(2,1)S(1)}, u32[]{:S(2)}, u32[]{:S(2)}) collective-permute-start(bf16[32,32,128]{2,1,0:T(8,128)(2,1)S(1)} %pad_maximum_fusion.refs_1_), channel_id=1, source_target_pairs={{0,5},{16,31},{1,4},{17,30},{2,7},{18,29},{3,6},{19,28},{4,1},{20,... | collective-permute-start | bytes 786440 | tf_op jit(solution)/shard_map/ppermute | solution.py:369
  129.7 5.3 %collective-permute-start.34 = (bf16[32,32,128]{2,1,0:T(8,128)(2,1)S(1)}, bf16[32,32,128]{2,1,0:T(8,128)(2,1)S(1)}, u32[]{:S(2)}, u32[]{:S(2)}) collective-permute-start(bf16[32,32,128]{2,1,0:T(8,128)(2,1)S(1)} %collective-permute-done.30.refs_2_), channel_id=1, source_target_pairs={{0,16},{16,0},{1,17},{17,1},{2,18},{18,2},{3,19},{19,3},{4,20},{20... | collective-permute-start | bytes 786440 | tf_op jit(solution)/shard_map/ppermute | solution.py:369
  (28 other events, 258.9 us)

commit v7 on v5

--- a/solution.py
+++ b/solution.py
@@ -448,9 +448,10 @@
 
     top = strip(edges[0], slice(0, 64), slice(0, 64), 0)
     bottom = strip(edges[1], slice(448, 512), slice(64, 128), 15)
-    near_strip = send(jnp.where(core == 0, bottom, top), SWAP)
-    far_strip = send(jnp.where(core == 0, top, bottom), OVER)
+    for_near, for_far = jnp.where(core == 0, bottom, top), jnp.where(core == 0, top, bottom)
     parts = gathered_far(group)
+    _, for_near, for_far = lax.optimization_barrier((parts[1], for_near, for_far))
+    near_strip, far_strip = send(for_near, SWAP), send(for_far, OVER)
 
     from_near, from_far = ints(near_strip[64:66, :18]), ints(far_strip[64:66, :18])
     above, below = jnp.where(core == 0, from_far, from_near), jnp.where(core == 0, from_near, from_far)

time: 147 us -> 142 us (0.966)
  waiting for transfers between devices: 26.9 us -> 23.2 us
  starting transfers between devices: 62.2 us -> 59.4 us
    ppermute x35, waiting for transfers between devices: 26.4 us -> 23.2 us  [send(): return lax.ppermute(value, BOTH, pairs)]
    ppermute x35, starting transfers between devices: 56.9 us -> 54.1 us  [send(): return lax.ppermute(value, BOTH, pairs)]
  transfers between devices with their start and end apart: 37 -> 37, of which waited for: 20 -> 15; matrix products, arithmetic and copies ran while one was open for 5% -> 6% of each run, Pallas kernels for 0% -> 0%
where the time goes in v7:
time: 142 us
  starting transfers between devices  59.4 us (42%)
  Pallas kernels  44.8 us (32%)
  waiting for transfers between devices  23.2 us (16%)
  local copies, waits for them, and re-layouts  7.53 us (5%)
  other arithmetic  5.29 us (4%)
    ppermute x35, starting transfers between devices, send(): return lax.ppermute(value, BOTH, pairs)  54.1 us
    pallas_call x1, Pallas kernels, per_device(): pl.pallas_call(main_kernel, out_shape=(wide, wide, *[sums_shape] * 8), in...  37.1 us
    ppermute x35, waiting for transfers between devices, send(): return lax.ppermute(value, BOTH, pairs)  23.2 us
    pallas_call x1, Pallas kernels, per_device(): pl.pallas_call(final_kernel, out_shape=wide, in_specs=[smem] + [anywhere]...  7.7 us
    ppermute x1, starting transfers between devices, per_device(): before = lax.ppermute(side(edges[3], 15), 'col', up)  3.99 us
  transfers between devices with their start and end apart: 37, of which 15 were waited for; matrix products, arithmetic and copies ran while one was open for 6% of the time, Pallas kernels for 0%

profile of v7, /device:TPU:1, one launch (start us, length us, event | category | flops | bytes accessed | tf_op | source)
XLA Modules:
  0.0 141.6 jit_solution(4705692224683854961)
XLA Ops:
  2.0 2.2 %collective-permute-start = (bf16[8,32,128]{2,1,0:T(8,128)(2,1)S(1)}, bf16[8,32,128]{2,1,0:T(8,128)(2,1)S(1)}, u32[]{:S(2)}, u32[]{:S(2)}) collective-permute-start(bf16[8,32,128]{2,1,0:T(8,128)(2,1)S(1)} %pad_maximum_fusion.1), channel_id=1, source_target_pairs={{0,12},{16,20},{1,13},{17,21},{2,14},{18,22},{3,15},{19,23},{4,8},... | collective-permute-start | bytes 196616 | tf_op jit(solution)/shard_map/ppermute | solution.py:365
  4.2 1.6 %collective-permute-start.1 = (bf16[8,32,128]{2,1,0:T(8,128)(2,1)S(1)}, bf16[8,32,128]{2,1,0:T(8,128)(2,1)S(1)}, u32[]{:S(2)}, u32[]{:S(2)}) collective-permute-start(bf16[8,32,128]{2,1,0:T(8,128)(2,1)S(1)} %pad_maximum_fusion.1), channel_id=1, source_target_pairs={{0,3},{16,17},{1,2},{17,16},{2,1},{18,19},{3,0},{19,18},{4,7},{20,... | collective-permute-start | bytes 196616 | tf_op jit(solution)/shard_map/ppermute | solution.py:365
  10.8 4.0 %collective-permute-start.4 = (bf16[528,128]{1,0:T(8,128)(2,1)S(1)}, bf16[528,128]{1,0:T(8,128)(2,1)S(1)}, u32[]{:S(2)}, u32[]{:S(2)}) collective-permute-start(bf16[528,128]{1,0:T(8,128)(2,1)S(1)} %fusion.13), channel_id=1, source_target_pairs={{0,1},{1,2},{2,3},{3,4},{4,5},{5,6},{6,7},{7,8},{8,9},{9,10},{10,1... | collective-permute-start | bytes 405512 | tf_op jit(solution)/shard_map/ppermute | solution.py:434
  14.9 5.0 %collective-permute-start.3 = (bf16[32,32,128]{2,1,0:T(8,128)(2,1)S(1)}, bf16[32,32,128]{2,1,0:T(8,128)(2,1)S(1)}, u32[]{:S(2)}, u32[]{:S(2)}) collective-permute-start(bf16[32,32,128]{2,1,0:T(8,128)(2,1)S(1)} %constant_dynamic-update-slice_fusion.refs_2_), channel_id=1, source_target_pairs={{0,4},{16,28},{1,5},{17,29},{2,6},{18,30},{3,7},{19,31},{4,0},{20,... | collective-permute-start | bytes 786440 | tf_op jit(solution)/shard_map/ppermute | solution.py:365
  20.6 2.3 %collective-permute-start.9 = (bf16[32,32,128]{2,1,0:T(8,128)(2,1)S(1)}, bf16[32,32,128]{2,1,0:T(8,128)(2,1)S(1)}, u32[]{:S(2)}, u32[]{:S(2)}) collective-permute-start(bf16[32,32,128]{2,1,0:T(8,128)(2,1)S(1)} %constant_dynamic-update-slice_fusion.refs_2_), channel_id=1, source_target_pairs={{0,5},{16,31},{1,4},{17,30},{2,7},{18,29},{3,6},{19,28},{4,1},{20,... | collective-permute-start | bytes 786440 | tf_op jit(solution)/shard_map/ppermute | solution.py:365
  24.3 2.7 %collective-permute-start.7 = (bf16[80,1152]{1,0:T(8,128)(2,1)}, bf16[80,1152]{1,0:T(8,128)(2,1)S(1)}, u32[]{:S(2)}, u32[]{:S(2)}) collective-permute-start(bf16[80,1152]{1,0:T(8,128)(2,1)} %get-tuple-element.28), channel_id=1, source_target_pairs={{0,16},{16,0},{1,17},{17,1},{2,18},{18,2},{3,19},{19,3},{4,20},{20... | collective-permute-start | bytes 552968 | tf_op jit(solution)/shard_map/ppermute | solution.py:365
  27.0 3.0 %collective-permute-start.6 = (bf16[80,1152]{1,0:T(8,128)(2,1)S(1)}, bf16[80,1152]{1,0:T(8,128)(2,1)S(1)}, u32[]{:S(2)}, u32[]{:S(2)}) collective-permute-start(bf16[80,1152]{1,0:T(8,128)(2,1)S(1)} %get-tuple-element.27), channel_id=1, source_target_pairs={{32,16},{33,17},{34,18},{35,19},{36,20},{37,21},{38,22},{39,23},{4... | collective-permute-start | bytes 552968 | tf_op jit(solution)/shard_map/ppermute | solution.py:365
  36.4 37.1 %image_and_gradient.1 = (f32[1024,1024]{1,0:T(8,128)}, f32[1024,1024]{1,0:T(8,128)}, bf16[32,32,128]{2,1,0:T(8,128)(2,1)S(1)}, bf16[32,32,128]{2,1,0:T(8,128)(2,...) custom-call(s32[653]{0:T(1024)S(1)} %pad_add_fusion.1.refs_0_, ...), custom_call_target="tpu_custom_call" | custom-call | tf_op jit(solution)/shard_map/image_and_gradient/pallas_call | solution.py:477
  75.4 4.5 %collective-permute-start.20 = (bf16[32,32,128]{2,1,0:T(8,128)(2,1)S(1)}, bf16[32,32,128]{2,1,0:T(8,128)(2,1)S(1)}, u32[]{:S(2)}, u32[]{:S(2)}) collective-permute-start(bf16[32,32,128]{2,1,0:T(8,128)(2,1)S(1)} %add_convert_fusion.1), channel_id=1, source_target_pairs={{0,1},{16,19},{1,0},{17,18},{2,3},{18,17},{3,2},{19,16},{4,5},{20,... | collective-permute-start | bytes 786440 | tf_op jit(solution)/shard_map/ppermute | solution.py:365
  79.9 1.6 %collective-permute-start.18 = (bf16[32,32,128]{2,1,0:T(8,128)(2,1)S(1)}, bf16[32,32,128]{2,1,0:T(8,128)(2,1)S(1)}, u32[]{:S(2)}, u32[]{:S(2)}) collective-permute-start(bf16[32,32,128]{2,1,0:T(8,128)(2,1)S(1)} %add_convert_fusion.2), channel_id=1, source_target_pairs={{0,4},{16,28},{1,5},{17,29},{2,6},{18,30},{3,7},{19,31},{4,0},{20,... | collective-permute-start | bytes 786440 | tf_op jit(solution)/shard_map/ppermute | solution.py:365
  83.6 3.0 %collective-permute-done.18 = bf16[32,32,128]{2,1,0:T(8,128)(2,1)S(1)} collective-permute-done((bf16[32,32,128]{2,1,0:T(8,128)(2,1)S(1)}, bf16[32,32,128]{2,1,0:T(8,128)(2,1)S(1)}, u32[]{:S(2)}, u32[]{:S(2)}) %collective-permute-start.18) | collective-permute-done | bytes 262176 | tf_op jit(solution)/shard_map/ppermute | solution.py:365
  86.6 3.6 %collective-permute-done.16 = bf16[32,32,128]{2,1,0:T(8,128)(2,1)S(1)} collective-permute-done((bf16[32,32,128]{2,1,0:T(8,128)(2,1)S(1)}, bf16[32,32,128]{2,1,0:T(8,128)(2,1)S(1)}, u32[]{:S(2)}, u32[]{:S(2)}) %collective-permute-start.16) | collective-permute-done | bytes 262176 | tf_op jit(solution)/shard_map/ppermute | solution.py:365
  90.9 2.3 %collective-permute-start.21 = (bf16[8,32,128]{2,1,0:T(8,128)(2,1)S(1)}, bf16[8,32,128]{2,1,0:T(8,128)(2,1)S(1)}, u32[]{:S(2)}, u32[]{:S(2)}) collective-permute-start(bf16[8,32,128]{2,1,0:T(8,128)(2,1)S(1)} %get-tuple-element.53), channel_id=1, source_target_pairs={{0,15},{16,21},{1,14},{17,20},{2,13},{18,23},{3,12},{19,22},{4,11}... | collective-permute-start | bytes 196616 | tf_op jit(solution)/shard_map/ppermute | solution.py:365
  94.0 1.8 %collective-permute-done.21 = bf16[8,32,128]{2,1,0:T(8,128)(2,1)S(1)} collective-permute-done((bf16[8,32,128]{2,1,0:T(8,128)(2,1)S(1)}, bf16[8,32,128]{2,1,0:T(8,128)(2,1)S(1)}, u32[]{:S(2)}, u32[]{:S(2)}) %collective-permute-start.21) | collective-permute-done | bytes 65568 | tf_op jit(solution)/shard_map/ppermute | solution.py:365
  95.8 1.9 %collective-permute-start.26 = (bf16[8,32,128]{2,1,0:T(8,128)(2,1)S(1)}, bf16[8,32,128]{2,1,0:T(8,128)(2,1)S(1)}, u32[]{:S(2)}, u32[]{:S(2)}) collective-permute-start(bf16[8,32,128]{2,1,0:T(8,128)(2,1)S(1)} %add_convert_fusion.5), channel_id=1, source_target_pairs={{0,96},{16,112},{1,97},{17,113},{2,98},{18,114},{3,99},{19,115},{4... | collective-permute-start | bytes 196616 | tf_op jit(solution)/shard_map/ppermute | solution.py:365
  97.7 2.4 %collective-permute-start.24 = (bf16[8,32,128]{2,1,0:T(8,128)(2,1)S(1)}, bf16[8,32,128]{2,1,0:T(8,128)(2,1)S(1)}, u32[]{:S(2)}, u32[]{:S(2)}) collective-permute-start(bf16[8,32,128]{2,1,0:T(8,128)(2,1)S(1)} %add_convert_fusion.5), channel_id=1, source_target_pairs={{0,64},{16,80},{1,65},{17,81},{2,66},{18,82},{3,67},{19,83},{4,68}... | collective-permute-start | bytes 196616 | tf_op jit(solution)/shard_map/ppermute | solution.py:365
  100.2 2.5 %collective-permute-done.25 = bf16[8,32,128]{2,1,0:T(8,128)(2,1)S(1)} collective-permute-done((bf16[8,32,128]{2,1,0:T(8,128)(2,1)S(1)}, bf16[8,32,128]{2,1,0:T(8,128)(2,1)S(1)}, u32[]{:S(2)}, u32[]{:S(2)}) %collective-permute-start.25) | collective-permute-done | bytes 65568 | tf_op jit(solution)/shard_map/ppermute | solution.py:365
  103.3 2.3 %collective-permute-start.29 = (bf16[8,32,128]{2,1,0:T(8,128)(2,1)S(1)}, bf16[8,32,128]{2,1,0:T(8,128)(2,1)S(1)}, u32[]{:S(2)}, u32[]{:S(2)}) collective-permute-start(bf16[8,32,128]{2,1,0:T(8,128)(2,1)S(1)} %pad_maximum_fusion.2), channel_id=1, source_target_pairs={{0,15},{16,21},{1,14},{17,20},{2,13},{18,23},{3,12},{19,22},{4,11}... | collective-permute-start | bytes 196616 | tf_op jit(solution)/shard_map/ppermute | solution.py:365
  107.4 1.6 %collective-permute-done.28 = bf16[8,32,128]{2,1,0:T(8,128)(2,1)S(1)} collective-permute-done((bf16[8,32,128]{2,1,0:T(8,128)(2,1)S(1)}, bf16[8,32,128]{2,1,0:T(8,128)(2,1)S(1)}, u32[]{:S(2)}, u32[]{:S(2)}) %collective-permute-start.28) | collective-permute-done | bytes 65568 | tf_op jit(solution)/shard_map/ppermute | solution.py:365
  109.1 10.9 %collective-permute-start.33 = (bf16[32,32,128]{2,1,0:T(8,128)(2,1)S(1)}, bf16[32,32,128]{2,1,0:T(8,128)(2,1)S(1)}, u32[]{:S(2)}, u32[]{:S(2)}) collective-permute-start(bf16[32,32,128]{2,1,0:T(8,128)(2,1)S(1)} %pad_maximum_fusion.refs_1_), channel_id=1, source_target_pairs={{0,16},{16,0},{1,17},{17,1},{2,18},{18,2},{3,19},{19,3},{4,20},{20... | collective-permute-start | bytes 786440 | tf_op jit(solution)/shard_map/ppermute | solution.py:365
  120.2 1.6 %collective-permute-start.30 = (bf16[32,32,128]{2,1,0:T(8,128)(2,1)S(1)}, bf16[32,32,128]{2,1,0:T(8,128)(2,1)S(1)}, u32[]{:S(2)}, u32[]{:S(2)}) collective-permute-start(bf16[32,32,128]{2,1,0:T(8,128)(2,1)S(1)} %pad_maximum_fusion.refs_1_), channel_id=1, source_target_pairs={{0,4},{16,28},{1,5},{17,29},{2,6},{18,30},{3,7},{19,31},{4,0},{20,... | collective-permute-start | bytes 786440 | tf_op jit(solution)/shard_map/ppermute | solution.py:365
  122.9 2.4 %collective-permute-start.32 = (bf16[32,32,128]{2,1,0:T(8,128)(2,1)S(1)}, bf16[32,32,128]{2,1,0:T(8,128)(2,1)S(1)}, u32[]{:S(2)}, u32[]{:S(2)}) collective-permute-start(bf16[32,32,128]{2,1,0:T(8,128)(2,1)S(1)} %pad_maximum_fusion.refs_1_), channel_id=1, source_target_pairs={{0,5},{16,31},{1,4},{17,30},{2,7},{18,29},{3,6},{19,28},{4,1},{20,... | collective-permute-start | bytes 786440 | tf_op jit(solution)/shard_map/ppermute | solution.py:365
  129.6 1.9 %collective-permute-done.32.refs_4_ = bf16[32,32,128]{2,1,0:T(8,128)(2,1)S(1)} collective-permute-done((bf16[32,32,128]{2,1,0:T(8,128)(2,1)S(1)}, bf16[32,32,128]{2,1,0:T(8,128)(2,1)S(1)}, u32[]{:S(2)}, u32[]{:S(2)}) %collective-permute-start.32) | collective-permute-done | bytes 262176 | tf_op jit(solution)/shard_map/ppermute | solution.py:365
  133.7 7.7 %final_mask.1 = f32[1024,1024]{1,0:T(8,128)} custom-call(s32[653]{0:T(1024)S(1)} %pad_add_fusion.1.refs_0_, bf16[32,32,128]{2,1,0:T(8,128)(2,1)S(1)} %pad_maximum_fusion.refs_1_, bf16[32,32,128]{2,1,0:T(8,128)(2,1)S(1)} %collective-permute-done.30.refs_2_, bf16[32,32,128]{2,1,0:T(8,128)(2,1)S(1)} %collective-permute-done.31.refs_3_, ...), custom_call_target="tpu_custom_call" | custom-call | tf_op jit(solution)/shard_map/final_mask/pallas_call | solution.py:509
  (138 shorter events, 30.3 us)
Async XLA Ops:
  2.0 12.8 %collective-permute-start = (bf16[8,32,128]{2,1,0:T(8,128)(2,1)S(1)}, bf16[8,32,128]{2,1,0:T(8,128)(2,1)S(1)}, u32[]{:S(2)}, u32[]{:S(2)}) collective-permute-start(bf16[8,32,128]{2,1,0:T(8,128)(2,1)S(1)} %pad_maximum_fusion.1), channel_id=1, source_target_pairs={{0,12},{16,20},{1,13},{17,21},{2,14},{18,22},{3,15},{19,23},{4,8},... | collective-permute-start | bytes 196616 | tf_op jit(solution)/shard_map/ppermute | solution.py:365
  4.2 10.6 %collective-permute-start.1 = (bf16[8,32,128]{2,1,0:T(8,128)(2,1)S(1)}, bf16[8,32,128]{2,1,0:T(8,128)(2,1)S(1)}, u32[]{:S(2)}, u32[]{:S(2)}) collective-permute-start(bf16[8,32,128]{2,1,0:T(8,128)(2,1)S(1)} %pad_maximum_fusion.1), channel_id=1, source_target_pairs={{0,3},{16,17},{1,2},{17,16},{2,1},{18,19},{3,0},{19,18},{4,7},{20,... | collective-permute-start | bytes 196616 | tf_op jit(solution)/shard_map/ppermute | solution.py:365
  5.9 9.0 %collective-permute-start.2 = (bf16[8,32,128]{2,1,0:T(8,128)(2,1)S(1)}, bf16[8,32,128]{2,1,0:T(8,128)(2,1)S(1)}, u32[]{:S(2)}, u32[]{:S(2)}) collective-permute-start(bf16[8,32,128]{2,1,0:T(8,128)(2,1)S(1)} %pad_maximum_fusion.1), channel_id=1, source_target_pairs={{0,15},{16,21},{1,14},{17,20},{2,13},{18,23},{3,12},{19,22},{4,11}... | collective-permute-start | bytes 196616 | tf_op jit(solution)/shard_map/ppermute | solution.py:365
  9.3 13.6 %collective-permute-start.5 = (bf16[528,128]{1,0:T(8,128)(2,1)S(1)}, bf16[528,128]{1,0:T(8,128)(2,1)S(1)}, u32[]{:S(2)}, u32[]{:S(2)}) collective-permute-start(bf16[528,128]{1,0:T(8,128)(2,1)S(1)} %fusion.14), channel_id=1, source_target_pairs={{1,0},{2,1},{3,2},{4,3},{5,4},{6,5},{7,6},{8,7},{9,8},{10,9},{11,1... | collective-permute-start | bytes 405512 | tf_op jit(solution)/shard_map/ppermute | solution.py:435
  10.8 12.3 %collective-permute-start.4 = (bf16[528,128]{1,0:T(8,128)(2,1)S(1)}, bf16[528,128]{1,0:T(8,128)(2,1)S(1)}, u32[]{:S(2)}, u32[]{:S(2)}) collective-permute-start(bf16[528,128]{1,0:T(8,128)(2,1)S(1)} %fusion.13), channel_id=1, source_target_pairs={{0,1},{1,2},{2,3},{3,4},{4,5},{5,6},{6,7},{7,8},{8,9},{9,10},{10,1... | collective-permute-start | bytes 405512 | tf_op jit(solution)/shard_map/ppermute | solution.py:434
  14.9 9.4 %collective-permute-start.3 = (bf16[32,32,128]{2,1,0:T(8,128)(2,1)S(1)}, bf16[32,32,128]{2,1,0:T(8,128)(2,1)S(1)}, u32[]{:S(2)}, u32[]{:S(2)}) collective-permute-start(bf16[32,32,128]{2,1,0:T(8,128)(2,1)S(1)} %constant_dynamic-update-slice_fusion.refs_2_), channel_id=1, source_target_pairs={{0,4},{16,28},{1,5},{17,29},{2,6},{18,30},{3,7},{19,31},{4,0},{20,... | collective-permute-start | bytes 786440 | tf_op jit(solution)/shard_map/ppermute | solution.py:365
  19.9 11.4 %collective-permute-start.8 = (bf16[32,32,128]{2,1,0:T(8,128)(2,1)S(1)}, bf16[32,32,128]{2,1,0:T(8,128)(2,1)S(1)}, u32[]{:S(2)}, u32[]{:S(2)}) collective-permute-start(bf16[32,32,128]{2,1,0:T(8,128)(2,1)S(1)} %constant_dynamic-update-slice_fusion.refs_2_), channel_id=1, source_target_pairs={{0,1},{16,19},{1,0},{17,18},{2,3},{18,17},{3,2},{19,16},{4,5},{20,... | collective-permute-start | bytes 786440 | tf_op jit(solution)/shard_map/ppermute | solution.py:365
  20.6 11.2 %collective-permute-start.9 = (bf16[32,32,128]{2,1,0:T(8,128)(2,1)S(1)}, bf16[32,32,128]{2,1,0:T(8,128)(2,1)S(1)}, u32[]{:S(2)}, u32[]{:S(2)}) collective-permute-start(bf16[32,32,128]{2,1,0:T(8,128)(2,1)S(1)} %constant_dynamic-update-slice_fusion.refs_2_), channel_id=1, source_target_pairs={{0,5},{16,31},{1,4},{17,30},{2,7},{18,29},{3,6},{19,28},{4,1},{20,... | collective-permute-start | bytes 786440 | tf_op jit(solution)/shard_map/ppermute | solution.py:365
  24.3 7.6 %collective-permute-start.7 = (bf16[80,1152]{1,0:T(8,128)(2,1)}, bf16[80,1152]{1,0:T(8,128)(2,1)S(1)}, u32[]{:S(2)}, u32[]{:S(2)}) collective-permute-start(bf16[80,1152]{1,0:T(8,128)(2,1)} %get-tuple-element.28), channel_id=1, source_target_pairs={{0,16},{16,0},{1,17},{17,1},{2,18},{18,2},{3,19},{19,3},{4,20},{20... | collective-permute-start | bytes 552968 | tf_op jit(solution)/shard_map/ppermute | solution.py:365
  27.0 6.8 %collective-permute-start.6 = (bf16[80,1152]{1,0:T(8,128)(2,1)S(1)}, bf16[80,1152]{1,0:T(8,128)(2,1)S(1)}, u32[]{:S(2)}, u32[]{:S(2)}) collective-permute-start(bf16[80,1152]{1,0:T(8,128)(2,1)S(1)} %get-tuple-element.27), channel_id=1, source_target_pairs={{32,16},{33,17},{34,18},{35,19},{36,20},{37,21},{38,22},{39,23},{4... | collective-permute-start | bytes 552968 | tf_op jit(solution)/shard_map/ppermute | solution.py:365
  73.6 6.3 %collective-permute-start.17 = (bf16[32,32,128]{2,1,0:T(8,128)(2,1)}, bf16[32,32,128]{2,1,0:T(8,128)(2,1)S(1)}, u32[]{:S(2)}, u32[]{:S(2)}) collective-permute-start(bf16[32,32,128]{2,1,0:T(8,128)(2,1)} %get-tuple-element.35), channel_id=1, source_target_pairs={{0,16},{16,0},{1,17},{17,1},{2,18},{18,2},{3,19},{19,3},{4,20},{20... | collective-permute-start | bytes 786440 | tf_op jit(solution)/shard_map/ppermute | solution.py:365
  74.1 7.5 %collective-permute-start.15 = (bf16[32,32,128]{2,1,0:T(8,128)(2,1)}, bf16[32,32,128]{2,1,0:T(8,128)(2,1)S(1)}, u32[]{:S(2)}, u32[]{:S(2)}) collective-permute-start(bf16[32,32,128]{2,1,0:T(8,128)(2,1)} %get-tuple-element.33), channel_id=1, source_target_pairs={{0,16},{16,0},{1,17},{17,1},{2,18},{18,2},{3,19},{19,3},{4,20},{20... | collective-permute-start | bytes 786440 | tf_op jit(solution)/shard_map/ppermute | solution.py:365
  74.1 8.6 %collective-permute-start.14 = (bf16[32,32,128]{2,1,0:T(8,128)(2,1)S(1)}, bf16[32,32,128]{2,1,0:T(8,128)(2,1)S(1)}, u32[]{:S(2)}, u32[]{:S(2)}) collective-permute-start(bf16[32,32,128]{2,1,0:T(8,128)(2,1)S(1)} %get-tuple-element.31), channel_id=1, source_target_pairs={{0,16},{16,0},{1,17},{17,1},{2,18},{18,2},{3,19},{19,3},{4,20},{20... | collective-permute-start | bytes 786440 | tf_op jit(solution)/shard_map/ppermute | solution.py:365
  75.4 8.2 %collective-permute-start.20 = (bf16[32,32,128]{2,1,0:T(8,128)(2,1)S(1)}, bf16[32,32,128]{2,1,0:T(8,128)(2,1)S(1)}, u32[]{:S(2)}, u32[]{:S(2)}) collective-permute-start(bf16[32,32,128]{2,1,0:T(8,128)(2,1)S(1)} %add_convert_fusion.1), channel_id=1, source_target_pairs={{0,1},{16,19},{1,0},{17,18},{2,3},{18,17},{3,2},{19,16},{4,5},{20,... | collective-permute-start | bytes 786440 | tf_op jit(solution)/shard_map/ppermute | solution.py:365
  79.9 6.7 %collective-permute-start.18 = (bf16[32,32,128]{2,1,0:T(8,128)(2,1)S(1)}, bf16[32,32,128]{2,1,0:T(8,128)(2,1)S(1)}, u32[]{:S(2)}, u32[]{:S(2)}) collective-permute-start(bf16[32,32,128]{2,1,0:T(8,128)(2,1)S(1)} %add_convert_fusion.2), channel_id=1, source_target_pairs={{0,4},{16,28},{1,5},{17,29},{2,6},{18,30},{3,7},{19,31},{4,0},{20,... | collective-permute-start | bytes 786440 | tf_op jit(solution)/shard_map/ppermute | solution.py:365
  81.6 8.6 %collective-permute-start.16 = (bf16[32,32,128]{2,1,0:T(8,128)(2,1)S(1)}, bf16[32,32,128]{2,1,0:T(8,128)(2,1)S(1)}, u32[]{:S(2)}, u32[]{:S(2)}) collective-permute-start(bf16[32,32,128]{2,1,0:T(8,128)(2,1)S(1)} %add_convert_fusion.3), channel_id=1, source_target_pairs={{0,5},{16,31},{1,4},{17,30},{2,7},{18,29},{3,6},{19,28},{4,1},{20,... | collective-permute-start | bytes 786440 | tf_op jit(solution)/shard_map/ppermute | solution.py:365
  90.9 4.9 %collective-permute-start.21 = (bf16[8,32,128]{2,1,0:T(8,128)(2,1)S(1)}, bf16[8,32,128]{2,1,0:T(8,128)(2,1)S(1)}, u32[]{:S(2)}, u32[]{:S(2)}) collective-permute-start(bf16[8,32,128]{2,1,0:T(8,128)(2,1)S(1)} %get-tuple-element.53), channel_id=1, source_target_pairs={{0,15},{16,21},{1,14},{17,20},{2,13},{18,23},{3,12},{19,22},{4,11}... | collective-permute-start | bytes 196616 | tf_op jit(solution)/shard_map/ppermute | solution.py:365
  97.7 5.0 %collective-permute-start.25 = (bf16[8,32,128]{2,1,0:T(8,128)(2,1)S(1)}, bf16[8,32,128]{2,1,0:T(8,128)(2,1)S(1)}, u32[]{:S(2)}, u32[]{:S(2)}) collective-permute-start(bf16[8,32,128]{2,1,0:T(8,128)(2,1)S(1)} %add_convert_fusion.5), channel_id=1, source_target_pairs={{0,32},{16,48},{1,33},{17,49},{2,34},{18,50},{3,35},{19,51},{4,36}... | collective-permute-start | bytes 196616 | tf_op jit(solution)/shard_map/ppermute | solution.py:365
  97.7 5.0 %collective-permute-start.24 = (bf16[8,32,128]{2,1,0:T(8,128)(2,1)S(1)}, bf16[8,32,128]{2,1,0:T(8,128)(2,1)S(1)}, u32[]{:S(2)}, u32[]{:S(2)}) collective-permute-start(bf16[8,32,128]{2,1,0:T(8,128)(2,1)S(1)} %add_convert_fusion.5), channel_id=1, source_target_pairs={{0,64},{16,80},{1,65},{17,81},{2,66},{18,82},{3,67},{19,83},{4,68}... | collective-permute-start | bytes 196616 | tf_op jit(solution)/shard_map/ppermute | solution.py:365
  109.1 16.2 %collective-permute-start.33 = (bf16[32,32,128]{2,1,0:T(8,128)(2,1)S(1)}, bf16[32,32,128]{2,1,0:T(8,128)(2,1)S(1)}, u32[]{:S(2)}, u32[]{:S(2)}) collective-permute-start(bf16[32,32,128]{2,1,0:T(8,128)(2,1)S(1)} %pad_maximum_fusion.refs_1_), channel_id=1, source_target_pairs={{0,16},{16,0},{1,17},{17,1},{2,18},{18,2},{3,19},{19,3},{4,20},{20... | collective-permute-start | bytes 786440 | tf_op jit(solution)/shard_map/ppermute | solution.py:365
  120.2 6.6 %collective-permute-start.30 = (bf16[32,32,128]{2,1,0:T(8,128)(2,1)S(1)}, bf16[32,32,128]{2,1,0:T(8,128)(2,1)S(1)}, u32[]{:S(2)}, u32[]{:S(2)}) collective-permute-start(bf16[32,32,128]{2,1,0:T(8,128)(2,1)S(1)} %pad_maximum_fusion.refs_1_), channel_id=1, source_target_pairs={{0,4},{16,28},{1,5},{17,29},{2,6},{18,30},{3,7},{19,31},{4,0},{20,... | collective-permute-start | bytes 786440 | tf_op jit(solution)/shard_map/ppermute | solution.py:365
  121.8 6.4 %collective-permute-start.31 = (bf16[32,32,128]{2,1,0:T(8,128)(2,1)S(1)}, bf16[32,32,128]{2,1,0:T(8,128)(2,1)S(1)}, u32[]{:S(2)}, u32[]{:S(2)}) collective-permute-start(bf16[32,32,128]{2,1,0:T(8,128)(2,1)S(1)} %pad_maximum_fusion.refs_1_), channel_id=1, source_target_pairs={{0,1},{16,19},{1,0},{17,18},{2,3},{18,17},{3,2},{19,16},{4,5},{20,... | collective-permute-start | bytes 786440 | tf_op jit(solution)/shard_map/ppermute | solution.py:365
  122.9 8.5 %collective-permute-start.32 = (bf16[32,32,128]{2,1,0:T(8,128)(2,1)S(1)}, bf16[32,32,128]{2,1,0:T(8,128)(2,1)S(1)}, u32[]{:S(2)}, u32[]{:S(2)}) collective-permute-start(bf16[32,32,128]{2,1,0:T(8,128)(2,1)S(1)} %pad_maximum_fusion.refs_1_), channel_id=1, source_target_pairs={{0,5},{16,31},{1,4},{17,30},{2,7},{18,29},{3,6},{19,28},{4,1},{20,... | collective-permute-start | bytes 786440 | tf_op jit(solution)/shard_map/ppermute | solution.py:365
  126.8 5.4 %collective-permute-start.34 = (bf16[32,32,128]{2,1,0:T(8,128)(2,1)S(1)}, bf16[32,32,128]{2,1,0:T(8,128)(2,1)S(1)}, u32[]{:S(2)}, u32[]{:S(2)}) collective-permute-start(bf16[32,32,128]{2,1,0:T(8,128)(2,1)S(1)} %collective-permute-done.30.refs_2_), channel_id=1, source_target_pairs={{0,16},{16,0},{1,17},{17,1},{2,18},{18,2},{3,19},{19,3},{4,20},{20... | collective-permute-start | bytes 786440 | tf_op jit(solution)/shard_map/ppermute | solution.py:365
  (28 other events, 258.9 us)

commit v8 on v7

--- a/solution.py
+++ b/solution.py
@@ -220,8 +220,9 @@
         image = dot(half_fine, fine_t[...]) + dot(half_fine, fine_tlo[...])
         rows_t = pl.ds(pl.multiple_of(i * TILE, TILE), TILE)
         cols_t = pl.ds(pl.multiple_of(j * TILE, TILE), TILE)
-        resist = jax.nn.sigmoid(2.0 * (image - 1.8))
-        slopes = (4.0 * (resist - target[rows_t, cols_t]) * resist * (1.0 - resist)).astype(BF16)
+        bend = jnp.tanh(image - 1.8)
+        resist = 0.5 + 0.5 * bend
+        slopes = ((resist - target[rows_t, cols_t]) * (1.0 - bend * bend)).astype(BF16)
         target[rows_t, cols_t] = resist
         pltpu.make_async_copy(
             target.at[rows_t, cols_t], resist_out.at[rows_t, cols_t], resist_sems.at[t]

time: 142 us -> 142 us (level)
  no operation moved by 1% of the time
where the time goes in v8:
time: 142 us; the launch traced here: 141 us
  starting transfers between devices  59.4 us (42%)
  Pallas kernels  44.7 us (31%)
  waiting for transfers between devices  23.2 us (16%)
  local copies, waits for them, and re-layouts  7.53 us (5%)
  other arithmetic  5.29 us (4%)
    ppermute x35, starting transfers between devices, send(): return lax.ppermute(value, BOTH, pairs)  54.1 us
    pallas_call x1, Pallas kernels, per_device(): pl.pallas_call(main_kernel, out_shape=(wide, wide, *[sums_shape] * 8), in...  37 us
    ppermute x35, waiting for transfers between devices, send(): return lax.ppermute(value, BOTH, pairs)  23.2 us
    pallas_call x1, Pallas kernels, per_device(): pl.pallas_call(final_kernel, out_shape=wide, in_specs=[smem] + [anywhere]...  7.69 us
    ppermute x1, starting transfers between devices, per_device(): before = lax.ppermute(side(edges[3], 15), 'col', up)  3.99 us
  transfers between devices with their start and end apart: 37, of which 15 were waited for; matrix products, arithmetic and copies ran while one was open for 6% of the time, Pallas kernels for 0%

profile of v8, /device:TPU:1, one launch (start us, length us, event | category | flops | bytes accessed | tf_op | source)
XLA Modules:
  0.0 141.5 jit_solution(7648468284111576869)
XLA Ops:
  2.0 2.2 %collective-permute-start = (bf16[8,32,128]{2,1,0:T(8,128)(2,1)S(1)}, bf16[8,32,128]{2,1,0:T(8,128)(2,1)S(1)}, u32[]{:S(2)}, u32[]{:S(2)}) collective-permute-start(bf16[8,32,128]{2,1,0:T(8,128)(2,1)S(1)} %pad_maximum_fusion.1), channel_id=1, source_target_pairs={{0,12},{16,20},{1,13},{17,21},{2,14},{18,22},{3,15},{19,23},{4,8},... | collective-permute-start | bytes 196616 | tf_op jit(solution)/shard_map/ppermute | solution.py:366
  4.2 1.6 %collective-permute-start.1 = (bf16[8,32,128]{2,1,0:T(8,128)(2,1)S(1)}, bf16[8,32,128]{2,1,0:T(8,128)(2,1)S(1)}, u32[]{:S(2)}, u32[]{:S(2)}) collective-permute-start(bf16[8,32,128]{2,1,0:T(8,128)(2,1)S(1)} %pad_maximum_fusion.1), channel_id=1, source_target_pairs={{0,3},{16,17},{1,2},{17,16},{2,1},{18,19},{3,0},{19,18},{4,7},{20,... | collective-permute-start | bytes 196616 | tf_op jit(solution)/shard_map/ppermute | solution.py:366
  10.8 4.0 %collective-permute-start.4 = (bf16[528,128]{1,0:T(8,128)(2,1)S(1)}, bf16[528,128]{1,0:T(8,128)(2,1)S(1)}, u32[]{:S(2)}, u32[]{:S(2)}) collective-permute-start(bf16[528,128]{1,0:T(8,128)(2,1)S(1)} %fusion.13), channel_id=1, source_target_pairs={{0,1},{1,2},{2,3},{3,4},{4,5},{5,6},{6,7},{7,8},{8,9},{9,10},{10,1... | collective-permute-start | bytes 405512 | tf_op jit(solution)/shard_map/ppermute | solution.py:435
  14.9 5.0 %collective-permute-start.3 = (bf16[32,32,128]{2,1,0:T(8,128)(2,1)S(1)}, bf16[32,32,128]{2,1,0:T(8,128)(2,1)S(1)}, u32[]{:S(2)}, u32[]{:S(2)}) collective-permute-start(bf16[32,32,128]{2,1,0:T(8,128)(2,1)S(1)} %constant_dynamic-update-slice_fusion.refs_2_), channel_id=1, source_target_pairs={{0,4},{16,28},{1,5},{17,29},{2,6},{18,30},{3,7},{19,31},{4,0},{20,... | collective-permute-start | bytes 786440 | tf_op jit(solution)/shard_map/ppermute | solution.py:366
  20.6 2.3 %collective-permute-start.9 = (bf16[32,32,128]{2,1,0:T(8,128)(2,1)S(1)}, bf16[32,32,128]{2,1,0:T(8,128)(2,1)S(1)}, u32[]{:S(2)}, u32[]{:S(2)}) collective-permute-start(bf16[32,32,128]{2,1,0:T(8,128)(2,1)S(1)} %constant_dynamic-update-slice_fusion.refs_2_), channel_id=1, source_target_pairs={{0,5},{16,31},{1,4},{17,30},{2,7},{18,29},{3,6},{19,28},{4,1},{20,... | collective-permute-start | bytes 786440 | tf_op jit(solution)/shard_map/ppermute | solution.py:366
  24.3 2.7 %collective-permute-start.7 = (bf16[80,1152]{1,0:T(8,128)(2,1)}, bf16[80,1152]{1,0:T(8,128)(2,1)S(1)}, u32[]{:S(2)}, u32[]{:S(2)}) collective-permute-start(bf16[80,1152]{1,0:T(8,128)(2,1)} %get-tuple-element.28), channel_id=1, source_target_pairs={{0,16},{16,0},{1,17},{17,1},{2,18},{18,2},{3,19},{19,3},{4,20},{20... | collective-permute-start | bytes 552968 | tf_op jit(solution)/shard_map/ppermute | solution.py:366
  27.0 3.0 %collective-permute-start.6 = (bf16[80,1152]{1,0:T(8,128)(2,1)S(1)}, bf16[80,1152]{1,0:T(8,128)(2,1)S(1)}, u32[]{:S(2)}, u32[]{:S(2)}) collective-permute-start(bf16[80,1152]{1,0:T(8,128)(2,1)S(1)} %get-tuple-element.27), channel_id=1, source_target_pairs={{32,16},{33,17},{34,18},{35,19},{36,20},{37,21},{38,22},{39,23},{4... | collective-permute-start | bytes 552968 | tf_op jit(solution)/shard_map/ppermute | solution.py:366
  36.4 37.0 %image_and_gradient.1 = (f32[1024,1024]{1,0:T(8,128)}, f32[1024,1024]{1,0:T(8,128)}, bf16[32,32,128]{2,1,0:T(8,128)(2,1)S(1)}, bf16[32,32,128]{2,1,0:T(8,128)(2,...) custom-call(s32[653]{0:T(1024)S(1)} %pad_add_fusion.1.refs_0_, ...), custom_call_target="tpu_custom_call" | custom-call | tf_op jit(solution)/shard_map/image_and_gradient/pallas_call | solution.py:478
  75.3 4.5 %collective-permute-start.20 = (bf16[32,32,128]{2,1,0:T(8,128)(2,1)S(1)}, bf16[32,32,128]{2,1,0:T(8,128)(2,1)S(1)}, u32[]{:S(2)}, u32[]{:S(2)}) collective-permute-start(bf16[32,32,128]{2,1,0:T(8,128)(2,1)S(1)} %add_convert_fusion.1), channel_id=1, source_target_pairs={{0,1},{16,19},{1,0},{17,18},{2,3},{18,17},{3,2},{19,16},{4,5},{20,... | collective-permute-start | bytes 786440 | tf_op jit(solution)/shard_map/ppermute | solution.py:366
  79.8 1.6 %collective-permute-start.18 = (bf16[32,32,128]{2,1,0:T(8,128)(2,1)S(1)}, bf16[32,32,128]{2,1,0:T(8,128)(2,1)S(1)}, u32[]{:S(2)}, u32[]{:S(2)}) collective-permute-start(bf16[32,32,128]{2,1,0:T(8,128)(2,1)S(1)} %add_convert_fusion.2), channel_id=1, source_target_pairs={{0,4},{16,28},{1,5},{17,29},{2,6},{18,30},{3,7},{19,31},{4,0},{20,... | collective-permute-start | bytes 786440 | tf_op jit(solution)/shard_map/ppermute | solution.py:366
  83.5 3.0 %collective-permute-done.18 = bf16[32,32,128]{2,1,0:T(8,128)(2,1)S(1)} collective-permute-done((bf16[32,32,128]{2,1,0:T(8,128)(2,1)S(1)}, bf16[32,32,128]{2,1,0:T(8,128)(2,1)S(1)}, u32[]{:S(2)}, u32[]{:S(2)}) %collective-permute-start.18) | collective-permute-done | bytes 262176 | tf_op jit(solution)/shard_map/ppermute | solution.py:366
  86.5 3.6 %collective-permute-done.16 = bf16[32,32,128]{2,1,0:T(8,128)(2,1)S(1)} collective-permute-done((bf16[32,32,128]{2,1,0:T(8,128)(2,1)S(1)}, bf16[32,32,128]{2,1,0:T(8,128)(2,1)S(1)}, u32[]{:S(2)}, u32[]{:S(2)}) %collective-permute-start.16) | collective-permute-done | bytes 262176 | tf_op jit(solution)/shard_map/ppermute | solution.py:366
  90.8 2.3 %collective-permute-start.21 = (bf16[8,32,128]{2,1,0:T(8,128)(2,1)S(1)}, bf16[8,32,128]{2,1,0:T(8,128)(2,1)S(1)}, u32[]{:S(2)}, u32[]{:S(2)}) collective-permute-start(bf16[8,32,128]{2,1,0:T(8,128)(2,1)S(1)} %get-tuple-element.53), channel_id=1, source_target_pairs={{0,15},{16,21},{1,14},{17,20},{2,13},{18,23},{3,12},{19,22},{4,11}... | collective-permute-start | bytes 196616 | tf_op jit(solution)/shard_map/ppermute | solution.py:366
  93.9 1.8 %collective-permute-done.21 = bf16[8,32,128]{2,1,0:T(8,128)(2,1)S(1)} collective-permute-done((bf16[8,32,128]{2,1,0:T(8,128)(2,1)S(1)}, bf16[8,32,128]{2,1,0:T(8,128)(2,1)S(1)}, u32[]{:S(2)}, u32[]{:S(2)}) %collective-permute-start.21) | collective-permute-done | bytes 65568 | tf_op jit(solution)/shard_map/ppermute | solution.py:366
  95.7 1.9 %collective-permute-start.26 = (bf16[8,32,128]{2,1,0:T(8,128)(2,1)S(1)}, bf16[8,32,128]{2,1,0:T(8,128)(2,1)S(1)}, u32[]{:S(2)}, u32[]{:S(2)}) collective-permute-start(bf16[8,32,128]{2,1,0:T(8,128)(2,1)S(1)} %add_convert_fusion.5), channel_id=1, source_target_pairs={{0,96},{16,112},{1,97},{17,113},{2,98},{18,114},{3,99},{19,115},{4... | collective-permute-start | bytes 196616 | tf_op jit(solution)/shard_map/ppermute | solution.py:366
  97.6 2.4 %collective-permute-start.24 = (bf16[8,32,128]{2,1,0:T(8,128)(2,1)S(1)}, bf16[8,32,128]{2,1,0:T(8,128)(2,1)S(1)}, u32[]{:S(2)}, u32[]{:S(2)}) collective-permute-start(bf16[8,32,128]{2,1,0:T(8,128)(2,1)S(1)} %add_convert_fusion.5), channel_id=1, source_target_pairs={{0,64},{16,80},{1,65},{17,81},{2,66},{18,82},{3,67},{19,83},{4,68}... | collective-permute-start | bytes 196616 | tf_op jit(solution)/shard_map/ppermute | solution.py:366
  100.1 2.5 %collective-permute-done.25 = bf16[8,32,128]{2,1,0:T(8,128)(2,1)S(1)} collective-permute-done((bf16[8,32,128]{2,1,0:T(8,128)(2,1)S(1)}, bf16[8,32,128]{2,1,0:T(8,128)(2,1)S(1)}, u32[]{:S(2)}, u32[]{:S(2)}) %collective-permute-start.25) | collective-permute-done | bytes 65568 | tf_op jit(solution)/shard_map/ppermute | solution.py:366
  103.2 2.3 %collective-permute-start.29 = (bf16[8,32,128]{2,1,0:T(8,128)(2,1)S(1)}, bf16[8,32,128]{2,1,0:T(8,128)(2,1)S(1)}, u32[]{:S(2)}, u32[]{:S(2)}) collective-permute-start(bf16[8,32,128]{2,1,0:T(8,128)(2,1)S(1)} %pad_maximum_fusion.2), channel_id=1, source_target_pairs={{0,15},{16,21},{1,14},{17,20},{2,13},{18,23},{3,12},{19,22},{4,11}... | collective-permute-start | bytes 196616 | tf_op jit(solution)/shard_map/ppermute | solution.py:366
  107.3 1.6 %collective-permute-done.28 = bf16[8,32,128]{2,1,0:T(8,128)(2,1)S(1)} collective-permute-done((bf16[8,32,128]{2,1,0:T(8,128)(2,1)S(1)}, bf16[8,32,128]{2,1,0:T(8,128)(2,1)S(1)}, u32[]{:S(2)}, u32[]{:S(2)}) %collective-permute-start.28) | collective-permute-done | bytes 65568 | tf_op jit(solution)/shard_map/ppermute | solution.py:366
  109.0 10.9 %collective-permute-start.33 = (bf16[32,32,128]{2,1,0:T(8,128)(2,1)S(1)}, bf16[32,32,128]{2,1,0:T(8,128)(2,1)S(1)}, u32[]{:S(2)}, u32[]{:S(2)}) collective-permute-start(bf16[32,32,128]{2,1,0:T(8,128)(2,1)S(1)} %pad_maximum_fusion.refs_1_), channel_id=1, source_target_pairs={{0,16},{16,0},{1,17},{17,1},{2,18},{18,2},{3,19},{19,3},{4,20},{20... | collective-permute-start | bytes 786440 | tf_op jit(solution)/shard_map/ppermute | solution.py:366
  120.1 1.6 %collective-permute-start.30 = (bf16[32,32,128]{2,1,0:T(8,128)(2,1)S(1)}, bf16[32,32,128]{2,1,0:T(8,128)(2,1)S(1)}, u32[]{:S(2)}, u32[]{:S(2)}) collective-permute-start(bf16[32,32,128]{2,1,0:T(8,128)(2,1)S(1)} %pad_maximum_fusion.refs_1_), channel_id=1, source_target_pairs={{0,4},{16,28},{1,5},{17,29},{2,6},{18,30},{3,7},{19,31},{4,0},{20,... | collective-permute-start | bytes 786440 | tf_op jit(solution)/shard_map/ppermute | solution.py:366
  122.8 2.4 %collective-permute-start.32 = (bf16[32,32,128]{2,1,0:T(8,128)(2,1)S(1)}, bf16[32,32,128]{2,1,0:T(8,128)(2,1)S(1)}, u32[]{:S(2)}, u32[]{:S(2)}) collective-permute-start(bf16[32,32,128]{2,1,0:T(8,128)(2,1)S(1)} %pad_maximum_fusion.refs_1_), channel_id=1, source_target_pairs={{0,5},{16,31},{1,4},{17,30},{2,7},{18,29},{3,6},{19,28},{4,1},{20,... | collective-permute-start | bytes 786440 | tf_op jit(solution)/shard_map/ppermute | solution.py:366
  129.4 1.9 %collective-permute-done.32.refs_4_ = bf16[32,32,128]{2,1,0:T(8,128)(2,1)S(1)} collective-permute-done((bf16[32,32,128]{2,1,0:T(8,128)(2,1)S(1)}, bf16[32,32,128]{2,1,0:T(8,128)(2,1)S(1)}, u32[]{:S(2)}, u32[]{:S(2)}) %collective-permute-start.32) | collective-permute-done | bytes 262176 | tf_op jit(solution)/shard_map/ppermute | solution.py:366
  133.6 7.7 %final_mask.1 = f32[1024,1024]{1,0:T(8,128)} custom-call(s32[653]{0:T(1024)S(1)} %pad_add_fusion.1.refs_0_, bf16[32,32,128]{2,1,0:T(8,128)(2,1)S(1)} %pad_maximum_fusion.refs_1_, bf16[32,32,128]{2,1,0:T(8,128)(2,1)S(1)} %collective-permute-done.30.refs_2_, bf16[32,32,128]{2,1,0:T(8,128)(2,1)S(1)} %collective-permute-done.31.refs_3_, ...), custom_call_target="tpu_custom_call" | custom-call | tf_op jit(solution)/shard_map/final_mask/pallas_call | solution.py:510
  (138 shorter events, 30.3 us)
Async XLA Ops:
  2.0 12.8 %collective-permute-start = (bf16[8,32,128]{2,1,0:T(8,128)(2,1)S(1)}, bf16[8,32,128]{2,1,0:T(8,128)(2,1)S(1)}, u32[]{:S(2)}, u32[]{:S(2)}) collective-permute-start(bf16[8,32,128]{2,1,0:T(8,128)(2,1)S(1)} %pad_maximum_fusion.1), channel_id=1, source_target_pairs={{0,12},{16,20},{1,13},{17,21},{2,14},{18,22},{3,15},{19,23},{4,8},... | collective-permute-start | bytes 196616 | tf_op jit(solution)/shard_map/ppermute | solution.py:366
  4.2 10.6 %collective-permute-start.1 = (bf16[8,32,128]{2,1,0:T(8,128)(2,1)S(1)}, bf16[8,32,128]{2,1,0:T(8,128)(2,1)S(1)}, u32[]{:S(2)}, u32[]{:S(2)}) collective-permute-start(bf16[8,32,128]{2,1,0:T(8,128)(2,1)S(1)} %pad_maximum_fusion.1), channel_id=1, source_target_pairs={{0,3},{16,17},{1,2},{17,16},{2,1},{18,19},{3,0},{19,18},{4,7},{20,... | collective-permute-start | bytes 196616 | tf_op jit(solution)/shard_map/ppermute | solution.py:366
  5.9 9.0 %collective-permute-start.2 = (bf16[8,32,128]{2,1,0:T(8,128)(2,1)S(1)}, bf16[8,32,128]{2,1,0:T(8,128)(2,1)S(1)}, u32[]{:S(2)}, u32[]{:S(2)}) collective-permute-start(bf16[8,32,128]{2,1,0:T(8,128)(2,1)S(1)} %pad_maximum_fusion.1), channel_id=1, source_target_pairs={{0,15},{16,21},{1,14},{17,20},{2,13},{18,23},{3,12},{19,22},{4,11}... | collective-permute-start | bytes 196616 | tf_op jit(solution)/shard_map/ppermute | solution.py:366
  9.3 13.6 %collective-permute-start.5 = (bf16[528,128]{1,0:T(8,128)(2,1)S(1)}, bf16[528,128]{1,0:T(8,128)(2,1)S(1)}, u32[]{:S(2)}, u32[]{:S(2)}) collective-permute-start(bf16[528,128]{1,0:T(8,128)(2,1)S(1)} %fusion.14), channel_id=1, source_target_pairs={{1,0},{2,1},{3,2},{4,3},{5,4},{6,5},{7,6},{8,7},{9,8},{10,9},{11,1... | collective-permute-start | bytes 405512 | tf_op jit(solution)/shard_map/ppermute | solution.py:436
  10.8 12.3 %collective-permute-start.4 = (bf16[528,128]{1,0:T(8,128)(2,1)S(1)}, bf16[528,128]{1,0:T(8,128)(2,1)S(1)}, u32[]{:S(2)}, u32[]{:S(2)}) collective-permute-start(bf16[528,128]{1,0:T(8,128)(2,1)S(1)} %fusion.13), channel_id=1, source_target_pairs={{0,1},{1,2},{2,3},{3,4},{4,5},{5,6},{6,7},{7,8},{8,9},{9,10},{10,1... | collective-permute-start | bytes 405512 | tf_op jit(solution)/shard_map/ppermute | solution.py:435
  14.9 9.4 %collective-permute-start.3 = (bf16[32,32,128]{2,1,0:T(8,128)(2,1)S(1)}, bf16[32,32,128]{2,1,0:T(8,128)(2,1)S(1)}, u32[]{:S(2)}, u32[]{:S(2)}) collective-permute-start(bf16[32,32,128]{2,1,0:T(8,128)(2,1)S(1)} %constant_dynamic-update-slice_fusion.refs_2_), channel_id=1, source_target_pairs={{0,4},{16,28},{1,5},{17,29},{2,6},{18,30},{3,7},{19,31},{4,0},{20,... | collective-permute-start | bytes 786440 | tf_op jit(solution)/shard_map/ppermute | solution.py:366
  19.9 11.4 %collective-permute-start.8 = (bf16[32,32,128]{2,1,0:T(8,128)(2,1)S(1)}, bf16[32,32,128]{2,1,0:T(8,128)(2,1)S(1)}, u32[]{:S(2)}, u32[]{:S(2)}) collective-permute-start(bf16[32,32,128]{2,1,0:T(8,128)(2,1)S(1)} %constant_dynamic-update-slice_fusion.refs_2_), channel_id=1, source_target_pairs={{0,1},{16,19},{1,0},{17,18},{2,3},{18,17},{3,2},{19,16},{4,5},{20,... | collective-permute-start | bytes 786440 | tf_op jit(solution)/shard_map/ppermute | solution.py:366
  20.6 11.2 %collective-permute-start.9 = (bf16[32,32,128]{2,1,0:T(8,128)(2,1)S(1)}, bf16[32,32,128]{2,1,0:T(8,128)(2,1)S(1)}, u32[]{:S(2)}, u32[]{:S(2)}) collective-permute-start(bf16[32,32,128]{2,1,0:T(8,128)(2,1)S(1)} %constant_dynamic-update-slice_fusion.refs_2_), channel_id=1, source_target_pairs={{0,5},{16,31},{1,4},{17,30},{2,7},{18,29},{3,6},{19,28},{4,1},{20,... | collective-permute-start | bytes 786440 | tf_op jit(solution)/shard_map/ppermute | solution.py:366
  24.3 7.6 %collective-permute-start.7 = (bf16[80,1152]{1,0:T(8,128)(2,1)}, bf16[80,1152]{1,0:T(8,128)(2,1)S(1)}, u32[]{:S(2)}, u32[]{:S(2)}) collective-permute-start(bf16[80,1152]{1,0:T(8,128)(2,1)} %get-tuple-element.28), channel_id=1, source_target_pairs={{0,16},{16,0},{1,17},{17,1},{2,18},{18,2},{3,19},{19,3},{4,20},{20... | collective-permute-start | bytes 552968 | tf_op jit(solution)/shard_map/ppermute | solution.py:366
  27.0 6.8 %collective-permute-start.6 = (bf16[80,1152]{1,0:T(8,128)(2,1)S(1)}, bf16[80,1152]{1,0:T(8,128)(2,1)S(1)}, u32[]{:S(2)}, u32[]{:S(2)}) collective-permute-start(bf16[80,1152]{1,0:T(8,128)(2,1)S(1)} %get-tuple-element.27), channel_id=1, source_target_pairs={{32,16},{33,17},{34,18},{35,19},{36,20},{37,21},{38,22},{39,23},{4... | collective-permute-start | bytes 552968 | tf_op jit(solution)/shard_map/ppermute | solution.py:366
  73.5 6.3 %collective-permute-start.17 = (bf16[32,32,128]{2,1,0:T(8,128)(2,1)}, bf16[32,32,128]{2,1,0:T(8,128)(2,1)S(1)}, u32[]{:S(2)}, u32[]{:S(2)}) collective-permute-start(bf16[32,32,128]{2,1,0:T(8,128)(2,1)} %get-tuple-element.35), channel_id=1, source_target_pairs={{0,16},{16,0},{1,17},{17,1},{2,18},{18,2},{3,19},{19,3},{4,20},{20... | collective-permute-start | bytes 786440 | tf_op jit(solution)/shard_map/ppermute | solution.py:366
  73.9 7.5 %collective-permute-start.15 = (bf16[32,32,128]{2,1,0:T(8,128)(2,1)}, bf16[32,32,128]{2,1,0:T(8,128)(2,1)S(1)}, u32[]{:S(2)}, u32[]{:S(2)}) collective-permute-start(bf16[32,32,128]{2,1,0:T(8,128)(2,1)} %get-tuple-element.33), channel_id=1, source_target_pairs={{0,16},{16,0},{1,17},{17,1},{2,18},{18,2},{3,19},{19,3},{4,20},{20... | collective-permute-start | bytes 786440 | tf_op jit(solution)/shard_map/ppermute | solution.py:366
  74.0 8.6 %collective-permute-start.14 = (bf16[32,32,128]{2,1,0:T(8,128)(2,1)S(1)}, bf16[32,32,128]{2,1,0:T(8,128)(2,1)S(1)}, u32[]{:S(2)}, u32[]{:S(2)}) collective-permute-start(bf16[32,32,128]{2,1,0:T(8,128)(2,1)S(1)} %get-tuple-element.31), channel_id=1, source_target_pairs={{0,16},{16,0},{1,17},{17,1},{2,18},{18,2},{3,19},{19,3},{4,20},{20... | collective-permute-start | bytes 786440 | tf_op jit(solution)/shard_map/ppermute | solution.py:366
  75.3 8.2 %collective-permute-start.20 = (bf16[32,32,128]{2,1,0:T(8,128)(2,1)S(1)}, bf16[32,32,128]{2,1,0:T(8,128)(2,1)S(1)}, u32[]{:S(2)}, u32[]{:S(2)}) collective-permute-start(bf16[32,32,128]{2,1,0:T(8,128)(2,1)S(1)} %add_convert_fusion.1), channel_id=1, source_target_pairs={{0,1},{16,19},{1,0},{17,18},{2,3},{18,17},{3,2},{19,16},{4,5},{20,... | collective-permute-start | bytes 786440 | tf_op jit(solution)/shard_map/ppermute | solution.py:366
  79.8 6.7 %collective-permute-start.18 = (bf16[32,32,128]{2,1,0:T(8,128)(2,1)S(1)}, bf16[32,32,128]{2,1,0:T(8,128)(2,1)S(1)}, u32[]{:S(2)}, u32[]{:S(2)}) collective-permute-start(bf16[32,32,128]{2,1,0:T(8,128)(2,1)S(1)} %add_convert_fusion.2), channel_id=1, source_target_pairs={{0,4},{16,28},{1,5},{17,29},{2,6},{18,30},{3,7},{19,31},{4,0},{20,... | collective-permute-start | bytes 786440 | tf_op jit(solution)/shard_map/ppermute | solution.py:366
  81.5 8.6 %collective-permute-start.16 = (bf16[32,32,128]{2,1,0:T(8,128)(2,1)S(1)}, bf16[32,32,128]{2,1,0:T(8,128)(2,1)S(1)}, u32[]{:S(2)}, u32[]{:S(2)}) collective-permute-start(bf16[32,32,128]{2,1,0:T(8,128)(2,1)S(1)} %add_convert_fusion.3), channel_id=1, source_target_pairs={{0,5},{16,31},{1,4},{17,30},{2,7},{18,29},{3,6},{19,28},{4,1},{20,... | collective-permute-start | bytes 786440 | tf_op jit(solution)/shard_map/ppermute | solution.py:366
  90.8 4.9 %collective-permute-start.21 = (bf16[8,32,128]{2,1,0:T(8,128)(2,1)S(1)}, bf16[8,32,128]{2,1,0:T(8,128)(2,1)S(1)}, u32[]{:S(2)}, u32[]{:S(2)}) collective-permute-start(bf16[8,32,128]{2,1,0:T(8,128)(2,1)S(1)} %get-tuple-element.53), channel_id=1, source_target_pairs={{0,15},{16,21},{1,14},{17,20},{2,13},{18,23},{3,12},{19,22},{4,11}... | collective-permute-start | bytes 196616 | tf_op jit(solution)/shard_map/ppermute | solution.py:366
  97.6 5.0 %collective-permute-start.25 = (bf16[8,32,128]{2,1,0:T(8,128)(2,1)S(1)}, bf16[8,32,128]{2,1,0:T(8,128)(2,1)S(1)}, u32[]{:S(2)}, u32[]{:S(2)}) collective-permute-start(bf16[8,32,128]{2,1,0:T(8,128)(2,1)S(1)} %add_convert_fusion.5), channel_id=1, source_target_pairs={{0,32},{16,48},{1,33},{17,49},{2,34},{18,50},{3,35},{19,51},{4,36}... | collective-permute-start | bytes 196616 | tf_op jit(solution)/shard_map/ppermute | solution.py:366
  97.6 5.0 %collective-permute-start.24 = (bf16[8,32,128]{2,1,0:T(8,128)(2,1)S(1)}, bf16[8,32,128]{2,1,0:T(8,128)(2,1)S(1)}, u32[]{:S(2)}, u32[]{:S(2)}) collective-permute-start(bf16[8,32,128]{2,1,0:T(8,128)(2,1)S(1)} %add_convert_fusion.5), channel_id=1, source_target_pairs={{0,64},{16,80},{1,65},{17,81},{2,66},{18,82},{3,67},{19,83},{4,68}... | collective-permute-start | bytes 196616 | tf_op jit(solution)/shard_map/ppermute | solution.py:366
  109.0 16.2 %collective-permute-start.33 = (bf16[32,32,128]{2,1,0:T(8,128)(2,1)S(1)}, bf16[32,32,128]{2,1,0:T(8,128)(2,1)S(1)}, u32[]{:S(2)}, u32[]{:S(2)}) collective-permute-start(bf16[32,32,128]{2,1,0:T(8,128)(2,1)S(1)} %pad_maximum_fusion.refs_1_), channel_id=1, source_target_pairs={{0,16},{16,0},{1,17},{17,1},{2,18},{18,2},{3,19},{19,3},{4,20},{20... | collective-permute-start | bytes 786440 | tf_op jit(solution)/shard_map/ppermute | solution.py:366
  120.1 6.6 %collective-permute-start.30 = (bf16[32,32,128]{2,1,0:T(8,128)(2,1)S(1)}, bf16[32,32,128]{2,1,0:T(8,128)(2,1)S(1)}, u32[]{:S(2)}, u32[]{:S(2)}) collective-permute-start(bf16[32,32,128]{2,1,0:T(8,128)(2,1)S(1)} %pad_maximum_fusion.refs_1_), channel_id=1, source_target_pairs={{0,4},{16,28},{1,5},{17,29},{2,6},{18,30},{3,7},{19,31},{4,0},{20,... | collective-permute-start | bytes 786440 | tf_op jit(solution)/shard_map/ppermute | solution.py:366
  121.7 6.4 %collective-permute-start.31 = (bf16[32,32,128]{2,1,0:T(8,128)(2,1)S(1)}, bf16[32,32,128]{2,1,0:T(8,128)(2,1)S(1)}, u32[]{:S(2)}, u32[]{:S(2)}) collective-permute-start(bf16[32,32,128]{2,1,0:T(8,128)(2,1)S(1)} %pad_maximum_fusion.refs_1_), channel_id=1, source_target_pairs={{0,1},{16,19},{1,0},{17,18},{2,3},{18,17},{3,2},{19,16},{4,5},{20,... | collective-permute-start | bytes 786440 | tf_op jit(solution)/shard_map/ppermute | solution.py:366
  122.8 8.5 %collective-permute-start.32 = (bf16[32,32,128]{2,1,0:T(8,128)(2,1)S(1)}, bf16[32,32,128]{2,1,0:T(8,128)(2,1)S(1)}, u32[]{:S(2)}, u32[]{:S(2)}) collective-permute-start(bf16[32,32,128]{2,1,0:T(8,128)(2,1)S(1)} %pad_maximum_fusion.refs_1_), channel_id=1, source_target_pairs={{0,5},{16,31},{1,4},{17,30},{2,7},{18,29},{3,6},{19,28},{4,1},{20,... | collective-permute-start | bytes 786440 | tf_op jit(solution)/shard_map/ppermute | solution.py:366
  126.7 5.4 %collective-permute-start.34 = (bf16[32,32,128]{2,1,0:T(8,128)(2,1)S(1)}, bf16[32,32,128]{2,1,0:T(8,128)(2,1)S(1)}, u32[]{:S(2)}, u32[]{:S(2)}) collective-permute-start(bf16[32,32,128]{2,1,0:T(8,128)(2,1)S(1)} %collective-permute-done.30.refs_2_), channel_id=1, source_target_pairs={{0,16},{16,0},{1,17},{17,1},{2,18},{18,2},{3,19},{19,3},{4,20},{20... | collective-permute-start | bytes 786440 | tf_op jit(solution)/shard_map/ppermute | solution.py:366
  (28 other events, 258.9 us)
